TPU v7x, 32 devices: a whole 2x2x4 slice. The times are simulated.
32 devices in a mesh: groups: 2 (over y), wide: 16 (over z, x, core).
Axes of the slice: x: 2, y: 2, z: 4, core: 2. Of those that a mesh axis runs over, the one named last changes fastest.
Arguments:
- rows: bfloat16 [16384, 768], P(('groups', 'wide')), parts along dimension 0, may hold values from -6 to 6
- cell: int32 [16384], P(('groups', 'wide')), parts along dimension 0, may hold values from 0 to 511, as said below
- cell_place: int32 [1024], P('groups'), parts along dimension 0, may hold values from 0 to 511, as said below
- coarse: bfloat16 [1024, 768], P(('groups', 'wide')), parts along dimension 0, may hold values from -6 to 6
- fine: bfloat16 [1024, 64, 768], P(('groups', 'wide')), parts along dimension 0, may hold values from -6 to 6
- reseed: int32 [1024, 64], P(('groups', 'wide')), parts along dimension 0, may hold values from 0 to 511
Outputs:
- row_error: float32 [16384], P(('groups', 'wide')), parts along dimension 0
- coarse_new: float32 [1024, 768], P(('groups', 'wide')), parts along dimension 0
- fine_new: float32 [1024, 64, 768], P(('groups', 'wide')), parts along dimension 0
There are 2 independent parts, one for each index of `groups`. A program takes and returns all parts, laid end to end along the dimension named above; each array names one. Nothing has to cross between parts.
Inputs may be any that keep to these rules, and one draw needn't show every extreme that they name: `cell`: the rows of one index of wide name at most 64 rows whose cells are owned by one index of wide, and exactly 64 for some owner in every draw. `cell_place`: each place appears once.
All inputs are finite; a program needn't handle non-finite values.
Results may differ from a plain program's by a relative error of at most 0.0045.
Values may be sent and summed in bfloat16 or wider, within the bound.
No kernel may reach another device: no remote copies, remote signals or barrier semaphores. Data moves between devices by JAX's collectives and lax.ppermute only.
A program may use at most 64 MiB of HBM per device.

v0:
```python
import jax
import jax.numpy as jnp
from jax import lax
from jax.sharding import PartitionSpec as P

TEMP = 16


def membership(ids, cells_dev):
    return (ids[:, None] == jnp.arange(cells_dev, dtype=jnp.int32)[None, :]).astype(jnp.float32)


def score_slots(resid, ids, fine, fine_squared_norm):
    cells_dev, fine_n, width = fine.shape
    count = resid.shape[0]
    member = membership(ids, cells_dev)
    fine_flat = fine.reshape(cells_dev * fine_n, width)
    scores = lax.dot_general(
        resid, fine_flat, (((1,), (1,)), ((), ())), preferred_element_type=jnp.float32
    )
    selected_centres = jnp.sum(
        scores.reshape(count, cells_dev, fine_n) * member[:, :, None], axis=1
    )
    selected_squared_norm = jnp.sum(fine_squared_norm[None, :, :] * member[:, :, None], axis=1)
    residual_gathered = resid.astype(jnp.float32)
    residual_squared_norm = jnp.sum(residual_gathered * residual_gathered, axis=-1)
    squared_distance = (
        residual_squared_norm[:, None] - 2.0 * selected_centres + selected_squared_norm
    )
    logit = -squared_distance / TEMP
    peak = jnp.max(logit, axis=1)
    expo = jnp.exp(logit - peak[:, None])
    total = jnp.sum(expo, axis=1)
    weight = (expo / total[:, None]).astype(jnp.bfloat16)
    error = -TEMP * (peak + jnp.log(total))
    return (weight, error)


def shards(rows, cell, cell_place, coarse, fine, reseed):
    peers = lax.axis_size("wide")
    rows_dev, width = rows.shape
    cells_dev, fine_n = (fine.shape[0], fine.shape[1])
    capacity = max(2, 2 * rows_dev // peers)
    slots_all = peers * capacity
    place = cell_place[cell]
    owner = place // cells_dev
    local = place % cells_dev
    owner_hot = (owner[:, None] == jnp.arange(peers, dtype=jnp.int32)[None, :]).astype(jnp.float32)
    line = jnp.arange(rows_dev, dtype=jnp.int32)
    lower = (line[:, None] >= line[None, :]).astype(jnp.float32)
    running = jnp.dot(lower, owner_hot, precision=lax.Precision.HIGHEST)
    rank = (jnp.sum(running * owner_hot, axis=1) - 1.0).astype(jnp.int32)
    slot = owner * capacity + rank
    table = lax.all_gather(coarse, "wide", axis=0, tiled=True)
    payload = (rows.astype(jnp.float32) - table[place].astype(jnp.float32)).astype(jnp.bfloat16)
    send_rows = (
        jnp.zeros((slots_all, width), jnp.bfloat16)
        .at[slot]
        .set(payload)
        .reshape(peers, capacity, width)
    )
    send_ids = jnp.full((slots_all,), -1, jnp.int32).at[slot].set(local).reshape(peers, capacity)
    fine_wide = fine.astype(jnp.float32)
    fine_squared_norm = jnp.sum(fine_wide * fine_wide, axis=-1)
    got_rows, got_ids = (
        lax.all_to_all(send_rows, "wide", split_axis=0, concat_axis=0, tiled=True),
        lax.all_to_all(send_ids, "wide", split_axis=0, concat_axis=0, tiled=True),
    )
    ids = got_ids.reshape(slots_all)
    resid = got_rows.reshape(slots_all, width)
    weight, error = score_slots(resid, ids, fine, fine_squared_norm)
    returned = lax.all_to_all(
        error.reshape(peers, capacity), "wide", split_axis=0, concat_axis=0, tiled=True
    )
    member = membership(ids, cells_dev)
    spread = (member[:, :, None] * weight.astype(jnp.float32)[:, None, :]).astype(jnp.bfloat16)
    spread = spread.reshape(slots_all, cells_dev * fine_n)
    fsum = lax.dot_general(
        spread, resid, (((0,), (0,)), ((), ())), preferred_element_type=jnp.float32
    )
    fcount = jnp.sum(spread.astype(jnp.float32), axis=0)
    csum = lax.dot_general(
        member.astype(jnp.bfloat16),
        resid,
        (((0,), (0,)), ((), ())),
        preferred_element_type=jnp.float32,
    )
    ccount = jnp.sum(member, axis=0)
    coarse_wide = coarse.astype(jnp.float32)
    seedres = rows[reseed].astype(jnp.float32) - coarse_wide[:, None, :]
    fine_new = (fsum.reshape(cells_dev, fine_n, width) + seedres) / (
        fcount.reshape(cells_dev, fine_n)[:, :, None] + 1.0
    )
    coarse_new = coarse_wide + csum / (ccount[:, None] + 1.0)
    row_error = returned.reshape(slots_all)[slot]
    return (row_error, coarse_new, fine_new)


def solution(mesh):
    in_specs = (
        P(("groups", "wide"), None),
        P(("groups", "wide")),
        P("groups"),
        P(("groups", "wide"), None),
        P(("groups", "wide"), None, None),
        P(("groups", "wide"), None),
    )
    out_specs = (
        P(("groups", "wide")),
        P(("groups", "wide"), None),
        P(("groups", "wide"), None, None),
    )
    return jax.shard_map(shards, mesh=mesh, in_specs=in_specs, out_specs=out_specs, check_vma=False)
```

profile of v0, /device:TPU:0, one launch (start us, length us, event | category | flops | bytes accessed | tf_op | source)
XLA Modules:
  0.0 111.8 jit_solution(14936688326315054960)
XLA Ops:
  0.7 0.8 compare_select_fusion.2
  1.4 3.5 %gather_fusion = s32[512]{0:T(512)S(1)} fusion(s32[512]{0:T(512)S(1)} %copy-done, s32[1024]{0:T(1024)S(1)} %pad_clamp_fusion.2), kind=kCustom, calls=%fused_computation | custom fusion | bytes 6144 | tf_op jit(solution)/shard_map/gather | solution.py:45
  5.3 2.4 %scatter_custom_fusion.1 = s32[1024]{0:T(1024)S(1)} fusion(s32[512]{0:T(512)S(1)} %bitcast.29, s32[512]{0:T(512)S(1)} %get-tuple-element.7, s32[]{:T(128)} %constant.47.clone.1), kind=kCustom, calls=%fused_computation.58 | custom fusion | bytes 4100 | tf_op jit(solution)/shard_map/scatter | solution.py:62
  7.7 0.7 all_to_all.14
  8.4 7.4 %all-to-all-start.1 = ((s32[16,1,64]{2,1,0:T(1,128)}), s32[16,1,64]{2,1,0:T(1,128)S(1)}, u32[]{:S(2)}, u32[]{:S(2)}) async-start(s32[16,1,64]{2,1,0:T(1,128)} %all_to_all.14), calls=%async_computation.1 | async-start | bytes 16384 | tf_op jit(solution)/shard_map/all_to_all | solution.py:67
  15.8 24.3 %all_gather.3 = bf16[512,768]{1,0:T(8,128)(2,1)S(1)} all-gather(bf16[32,768]{1,0:T(8,128)(2,1)} %param.9), channel_id=1, replica_groups=mesh['groups'=2,'wide'=16] {'wide'}, dimensions={0}, use_global_device_ids=true | all-gather | bytes 835584 | tf_op jit(solution)/shard_map/all_gather | solution.py:54
  40.1 6.8 %scatter_custom_fusion = bf16[1024,768]{1,0:T(8,128)(2,1)} fusion(s32[512]{0:T(512)S(1)} %bitcast.30, bf16[512,768]{1,0:T(8,128)(2,1)S(1)} %copy-done.1, bf16[]{:T(256)} %constant.21.clone.1, bf16[512,768]{1,0:T(8,128)(2,1)S(1)} %all_gather.3, s32[1024]{0:T(1024)S(1)} %pad_clamp_fusion.1), kind=kCustom, calls=%fused_computation.25 | custom fusion | flops 1572864 | bytes 3149826 | tf_op jit(solution)/shard_map/scatter | solution.py:59
  46.9 3.9 %all-to-all-start = ((bf16[16,64,768]{2,1,0:T(8,128)(2,1)}), bf16[16,64,768]{2,1,0:T(8,128)(2,1)S(1)}, u32[]{:S(2)}, u32[]{:S(2)}) async-start(bf16[16,64,768]{2,1,0:T(8,128)(2,1)} %bitcast.26), calls=%async_computation | async-start | bytes 3145728 | tf_op jit(solution)/shard_map/all_to_all | solution.py:66
  50.9 9.4 %gather_fusion.2 = bf16[2048,768]{1,0:T(8,128)(2,1)} fusion(bf16[512,768]{1,0:T(8,128)(2,1)S(1)} %copy-done.1, s32[2048]{0:T(1024)S(1)} %broadcast_clamp_fusion), kind=kCustom, calls=%fused_computation.3 | custom fusion | bytes 6299648 | tf_op jit(solution)/shard_map/gather | solution.py:90
  60.3 2.6 %multiply_reduce_fusion.2 = f32[32,64]{1,0:T(8,128)S(1)} fusion(bf16[32,64,768]{2,1,0:T(8,128)(2,1)} %param.10), kind=kLoop, calls=%fused_computation.13 | loop fusion | flops 4716544 | bytes 3153920 | tf_op jit(solution)/shard_map/reduce_sum | solution.py:64
  62.9 0.5 broadcast.247
  63.4 0.7 reduce.8
  64.3 0.6 multiply_reduce_fusion
  64.9 17.6 %all-to-all-done = bf16[16,64,768]{2,1,0:T(8,128)(2,1)S(1)} async-done(((bf16[16,64,768]{2,1,0:T(8,128)(2,1)}), bf16[16,64,768]{2,1,0:T(8,128)(2,1)S(1)}, u32[]{:S(2)}, u32[]{:S(2)}) %all-to-all-start) | async-done | bytes 1572896 | tf_op jit(solution)/shard_map/all_to_all | solution.py:66
  82.5 5.6 %multiply_reduce_fusion.1 = f32[1024,64]{0,1:T(8,128)S(1)} fusion(f32[1024,32]{0,1:T(8,128)S(1)} %fusion.15, bf16[1024,768,1]{1,0,2:T(8,128)(2,1)S(1)} %bitcast.23, bf16[32,64,768]{2,1,0:T(8,128)(2,1)} %param.10), kind=kOutput, calls=%fused_computation.9 | convolution fusion | flops 3225354240 | bytes 5111808 | tf_op jit(solution)/shard_map/dot_general | solution.py:18
  88.2 0.4 multiply_reduce_fusion.3
  88.8 0.7 convert_reduce_fusion
  89.5 0.7 mul.96
  90.2 9.1 %all-to-all-start.2 = ((f32[16,1,64]{2,1,0:T(1,128)}), f32[16,1,64]{2,1,0:T(1,128)S(1)}, u32[]{:S(2)}, u32[]{:S(2)}) async-start(f32[16,1,64]{2,1,0:T(1,128)} %mul.96), calls=%async_computation.2 | async-start | bytes 16384 | tf_op jit(solution)/shard_map/all_to_all | solution.py:72
  99.3 6.8 %fusion.1 = f32[32,64,768]{2,1,0:T(8,128)} fusion(bf16[32,64,768]{2,1,0:T(8,128)(2,1)} %bitcast.27, f32[32,64]{1,0:T(8,128)S(1)} %broadcast_add_fusion, f32[32,768]{1,0:T(8,128)S(1)} %convert_element_type.82, bf16[1024,768,1]{1,0,2:T(8,128)(2,1)S(1)} %bitcast.24, f32[1024,64]{0,1:T(8,128)S(1)} %fusion.14, f32[1024,32]{0,1:T(8,128)S(1)} %fusion.15), kind=kOutput, calls=%fused_computation.12 | convolution fusion | flops 3231711232 | bytes 11509760 | tf_op jit(solution)/shard_map/dot_general | solution.py:78
  106.1 1.0 fusion.9
  107.1 0.5 broadcast.248
  107.6 0.7 reduce.9
  108.4 3.4 %gather_fusion.1 = f32[512]{0:T(512)} fusion(f32[1024]{0:T(1024)S(1)} %reshape.244, s32[1024]{0:T(1024)S(1)} %pad_clamp_fusion), kind=kCustom, calls=%fused_computation.2 | custom fusion | bytes 6144 | tf_op jit(solution)/shard_map/gather | solution.py:95
  (32 shorter events, 1.0 us)
Async XLA Ops:
  0.6 0.8 copy-start
  0.6 39.4 %copy-start.1 = (bf16[512,768]{1,0:T(8,128)(2,1)S(1)}, bf16[512,768]{1,0:T(8,128)(2,1)}, u32[]{:S(2)}) copy-start(bf16[512,768]{1,0:T(8,128)(2,1)} %param.6) | copy-start | bytes 2359300
  8.4 38.5 %all-to-all-start.1 = ((s32[16,1,64]{2,1,0:T(1,128)}), s32[16,1,64]{2,1,0:T(1,128)S(1)}, u32[]{:S(2)}, u32[]{:S(2)}) async-start(s32[16,1,64]{2,1,0:T(1,128)} %all_to_all.14), calls=%async_computation.1 | async-start | bytes 16384 | tf_op jit(solution)/shard_map/all_to_all | solution.py:67
  40.1 10.7 %copy-start.2 = (bf16[32,768]{1,0:T(8,128)(2,1)S(1)}, bf16[32,768]{1,0:T(8,128)(2,1)}, u32[]{:S(2)}) copy-start(bf16[32,768]{1,0:T(8,128)(2,1)} %param.9) | copy-start | bytes 147460
  40.1 10.8 %copy-start.3 = (s32[32,64]{1,0:T(8,128)S(1)}, s32[32,64]{1,0:T(8,128)}, u32[]{:S(2)}) copy-start(s32[32,64]{1,0:T(8,128)} %param.11) | copy-start | bytes 24580
  46.9 35.6 %all-to-all-start = ((bf16[16,64,768]{2,1,0:T(8,128)(2,1)}), bf16[16,64,768]{2,1,0:T(8,128)(2,1)S(1)}, u32[]{:S(2)}, u32[]{:S(2)}) async-start(bf16[16,64,768]{2,1,0:T(8,128)(2,1)} %bitcast.26), calls=%async_computation | async-start | bytes 3145728 | tf_op jit(solution)/shard_map/all_to_all | solution.py:66
  90.2 16.9 %all-to-all-start.2 = ((f32[16,1,64]{2,1,0:T(1,128)}), f32[16,1,64]{2,1,0:T(1,128)S(1)}, u32[]{:S(2)}, u32[]{:S(2)}) async-start(f32[16,1,64]{2,1,0:T(1,128)} %mul.96), calls=%async_computation.2 | async-start | bytes 16384 | tf_op jit(solution)/shard_map/all_to_all | solution.py:72
where the time goes:
time: 112 us
  blocking collectives  24.3 us (22%)
  local copies, waits for them, and re-layouts  21.4 us (19%)
  starting transfers between devices  20.3 us (18%)
  waiting for transfers between devices  17.6 us (16%)
  matrix products  13.7 us (12%)
  other arithmetic  13.6 us (12%)
    all_gather x1, blocking collectives, shards(): table = lax.all_gather(coarse, 'wide', axis=0, tiled=True)  24.3 us
    all_to_all x1, waiting for transfers between devices, shards(): lax.all_to_all(send_rows, 'wide', split_axis=0, concat_axis=0, tiled=True)  17.6 us
    gather x1, local copies, waits for them, and re-layouts, shards(): seedres = rows[reseed].astype(jnp.float32) - coarse_wide[:, None, :]  9.37 us
    all_to_all x1, starting transfers between devices, shards(): lax.all_to_all(error.reshape(peers, capacity), 'wide', split_axis=0, conc...  9.08 us
    all_to_all x1, starting transfers between devices, shards(): lax.all_to_all(send_ids, 'wide', split_axis=0, concat_axis=0, tiled=True)  7.36 us
    scatter x1, other arithmetic, shards(): send_rows = jnp.zeros((slots_all, width), jnp.bfloat16).at[slot].set(payl...  6.82 us
    dot_general x1, matrix products, shards(): lax.dot_general(spread, resid, (((0,), (0,)), ((), ())), preferred_elemen...  6.8 us
    dot_general x1, matrix products, score_slots(): lax.dot_general(resid, fine_flat, (((1,), (1,)), ((), ())), preferred_ele...  5.64 us
  transfers between devices with their start and end apart: 3, of which 1 were waited for; matrix products, arithmetic and copies ran while one was open for 26% of the time, Pallas kernels for 0%

commit v1 on v0

v1 whole, which is shorter than its diff:
```python
import functools

import jax
import jax.numpy as jnp
from jax import lax
from jax.experimental import pallas as pl
from jax.experimental.pallas import tpu as pltpu
from jax.sharding import PartitionSpec as P

TEMP = 16
LANES = 128
META = 16
VMEM_LIMIT = 48 * 1024 * 1024
BF = jnp.bfloat16
F32 = jnp.float32


def iota(shape, dim):
    return lax.broadcasted_iota(jnp.int32, shape, dim)


def hot(index, size, dtype=BF):
    return (iota((size, index.shape[1]), 0) == index).astype(F32).astype(dtype)


def dot(a, b, dims=((1,), (0,))):
    return lax.dot_general(a, b, (dims, ((), ())), preferred_element_type=F32)


def split3(x):
    high = x.astype(BF)
    rest = x - high.astype(F32)
    mid = rest.astype(BF)
    return high, mid, (rest - mid.astype(F32)).astype(BF)


def pack_kernel(peers, capacity, cells_dev, cell_ref, place_ref, rows_ref, send_ref, route_ref):
    rows_dev, width = rows_ref.shape
    cells = place_ref.shape[1]
    chunks = width // LANES
    block = chunks * capacity + META
    cell = cell_ref[...]
    place = place_ref[...]
    table_row = iota((16, cells), 0)
    table = jnp.where(
        table_row == 0, place // cells_dev, jnp.where(table_row == 1, place % cells_dev, 0)
    ).astype(F32).astype(BF)
    found = jnp.zeros((16, rows_dev), F32)
    step = min(cells, 512)
    for first in range(0, cells, step):
        found += dot(table[:, first : first + step], hot(cell - first, step))
    owner = found[0:1].astype(jnp.int32)
    local = found[1:2]
    owner_hot = hot(owner, peers, F32)
    upper = (iota((rows_dev, rows_dev), 0) <= iota((rows_dev, rows_dev), 1)).astype(F32).astype(BF)
    running = dot(owner_hot.astype(BF), upper)
    rank = (jnp.sum(running * owner_hot, axis=0, keepdims=True) - 1.0).astype(jnp.int32)
    route_ref[...] = jnp.where(iota((8, rows_dev), 0) == 0, owner, rank)
    ids = dot((owner_hot * (local + 1.0)).astype(BF), hot(rank, LANES), ((1,), (1,))).astype(BF)
    slot = owner * capacity + rank
    group = max(1, 256 // capacity)
    for first in range(0, peers, group):
        packed = dot(hot(slot - first * capacity, group * capacity), rows_ref[...]).astype(BF)
        for p in range(group):
            start = (first + p) * block
            for j in range(chunks):
                send_ref[start + j * capacity : start + (j + 1) * capacity, :] = packed[
                    p * capacity : (p + 1) * capacity, j * LANES : (j + 1) * LANES
                ]
            send_ref[start + chunks * capacity : start + block, :] = jnp.broadcast_to(
                ids[first + p : first + p + 1], (META, LANES)
            )


def score_kernel(
    peers, capacity, got_ref, coarse_ref, norm_ref, fine_ref,
    error_ref, weight_ref, resid_ref, ids_ref, best_ref, square_ref,
):
    step = pl.program_id(0)
    cells_dev, width = coarse_ref.shape
    fine_n = norm_ref.shape[1]
    slots = peers * capacity
    chunks = width // LANES
    block = chunks * capacity + META
    group = max(1, 256 // capacity)
    span = group * capacity

    @pl.when(step == 0)
    def _():
        for p in range(peers):
            start = p * block + chunks * capacity
            ids_ref[:, p * capacity : (p + 1) * capacity] = (
                got_ref[start : start + META, :].astype(F32)[0:1, :capacity].astype(jnp.int32) - 1
            )
        member = hot(ids_ref[...], cells_dev)
        for first in range(0, peers, group):
            own = dot(
                member[:, first * capacity : first * capacity + span], coarse_ref[...], ((0,), (0,))
            )
            square = jnp.zeros((span, 1), F32)
            for j in range(chunks):
                lanes = slice(j * LANES, (j + 1) * LANES)
                got = jnp.concatenate(
                    [
                        got_ref[p * block + j * capacity : p * block + (j + 1) * capacity, :]
                        for p in range(first, first + group)
                    ],
                    axis=0,
                )
                resid = (got.astype(F32) - own[:, lanes]).astype(BF)
                resid_ref[first * capacity : first * capacity + span, lanes] = resid
                wide = resid.astype(F32)
                square += jnp.sum(wide * wide, axis=1, keepdims=True)
            diagonal = iota((span, span), 0) == iota((span, span), 1)
            square_ref[:, first * capacity : first * capacity + span] = jnp.sum(
                jnp.where(diagonal, square, 0.0), axis=0, keepdims=True
            )
        best_ref[...] = jnp.zeros_like(best_ref)

    cells = fine_ref.shape[0] // fine_n
    ids = ids_ref[...]
    scores = dot(fine_ref[...], resid_ref[...], ((1,), (1,)))
    best = best_ref[...]
    for c in range(cells):
        best = jnp.where(ids == step * cells + c, scores[c * fine_n : (c + 1) * fine_n], best)
    best_ref[...] = best

    @pl.when(step == pl.num_programs(0) - 1)
    def _():
        member = hot(ids, cells_dev)
        norm = sum(dot(part, member, ((0,), (0,))) for part in split3(norm_ref[...]))
        logit = (2.0 * best_ref[...] - norm) * (1.0 / TEMP)
        peak = jnp.max(logit, axis=0, keepdims=True)
        expo = jnp.exp(logit - peak)
        total = jnp.sum(expo, axis=0, keepdims=True)
        weight_ref[...] = (expo / total).astype(BF)
        error = square_ref[...] - TEMP * (peak + jnp.log(total))
        error_ref[...] = jnp.zeros_like(error_ref)
        for p in range(peers):
            error_ref[p, :, :capacity] = error[:, p * capacity : (p + 1) * capacity]


def update_kernel(
    ids_ref, weight_ref, resid_ref, coarse_ref, seed_ref, coarse_out_ref, fine_out_ref
):
    step = pl.program_id(0)
    cells_dev, width = coarse_ref.shape
    cells, fine_n, _ = fine_out_ref.shape
    ids = ids_ref[...]
    weight = weight_ref[...].astype(F32)

    @pl.when(step == 0)
    def _():
        member = hot(ids, cells_dev, F32)
        count = jnp.sum(member, axis=1, keepdims=True)
        coarse_out_ref[...] = coarse_ref[...].astype(F32) + dot(
            member.astype(BF), resid_ref[...]
        ) / (count + 1.0)

    spread = [jnp.where(ids == step * cells + c, weight, 0.0) for c in range(cells)]
    total = dot(jnp.concatenate([s.astype(BF) for s in spread], axis=0), resid_ref[...])
    own = coarse_ref[pl.ds(step * cells, cells), :].astype(F32) if cells % 8 == 0 else None
    for c in range(cells):
        count = jnp.sum(spread[c], axis=1, keepdims=True)
        if own is None:
            hit = iota((cells_dev, 1), 0) == step * cells + c
            centre = jnp.sum(
                jnp.where(hit, coarse_ref[...].astype(F32), 0.0), axis=0, keepdims=True
            )
        else:
            centre = own[c : c + 1]
        rows = slice(c * fine_n, (c + 1) * fine_n)
        seed = seed_ref[rows, :].astype(F32) - centre
        fine_out_ref[c] = (total[rows] + seed) / (count + 1.0)


def collect_kernel(peers, route_ref, error_ref, out_ref):
    owner_hot = hot(route_ref[0:1, :], peers, F32)
    rank_hot = hot(route_ref[1:2, :], LANES)
    error = error_ref[...].reshape(peers, LANES)
    picked = sum(dot(part, rank_hot) for part in split3(error))
    out_ref[...] = jnp.sum(picked * owner_hot, axis=0, keepdims=True)


def whole(shape):
    return pl.BlockSpec(shape, lambda *_: (0,) * len(shape))


def call(kernel, grid, in_specs, out_specs, out_shape, scratch=(), flops=0, moved=0):
    return pl.pallas_call(
        kernel,
        grid=grid,
        in_specs=in_specs,
        out_specs=out_specs,
        out_shape=out_shape,
        scratch_shapes=scratch,
        compiler_params=pltpu.CompilerParams(vmem_limit_bytes=VMEM_LIMIT),
        cost_estimate=pl.CostEstimate(flops=flops, bytes_accessed=moved, transcendentals=0),
    )


def shards(rows, cell, cell_place, coarse, fine, reseed):
    peers = lax.axis_size("wide")
    rows_dev, width = rows.shape
    cells_dev, fine_n, _ = fine.shape
    cells = cell_place.shape[0]
    capacity = max(16, 2 * rows_dev // peers)
    slots = peers * capacity
    block = (width // LANES) * capacity + META
    fine_all = cells_dev * fine_n

    send, route = call(
        functools.partial(pack_kernel, peers, capacity, cells_dev),
        (1,),
        [whole((1, rows_dev)), whole((1, cells)), whole((rows_dev, width))],
        [whole((peers * block, LANES)), whole((8, rows_dev))],
        [
            jax.ShapeDtypeStruct((peers * block, LANES), BF),
            jax.ShapeDtypeStruct((8, rows_dev), jnp.int32),
        ],
        flops=2 * slots * rows_dev * width,
        moved=2 * (slots + rows_dev) * width,
    )(cell.reshape(1, rows_dev), cell_place.reshape(1, cells), rows)

    got = lax.all_to_all(
        send.reshape(peers, block, LANES), "wide", split_axis=0, concat_axis=0, tiled=False
    ).reshape(peers * block, LANES)

    fine_wide = fine.astype(F32)
    norm = jnp.sum(fine_wide * fine_wide, axis=-1)
    seed = rows[reseed.reshape(fine_all)]

    cells_step = max(1, 256 // fine_n)
    steps = cells_dev // cells_step
    tile = cells_step * fine_n
    error, weight, resid, ids = call(
        functools.partial(score_kernel, peers, capacity),
        (steps,),
        [
            whole((peers * block, LANES)),
            whole((cells_dev, width)),
            whole((cells_dev, fine_n)),
            pl.BlockSpec((tile, width), lambda i: (i, 0)),
        ],
        [
            whole((peers, 1, LANES)),
            whole((fine_n, slots)),
            whole((slots, width)),
            whole((1, slots)),
        ],
        [
            jax.ShapeDtypeStruct((peers, 1, LANES), F32),
            jax.ShapeDtypeStruct((fine_n, slots), BF),
            jax.ShapeDtypeStruct((slots, width), BF),
            jax.ShapeDtypeStruct((1, slots), jnp.int32),
        ],
        scratch=[pltpu.VMEM((fine_n, slots), F32), pltpu.VMEM((1, slots), F32)],
        flops=2 * slots * fine_all * width,
        moved=2 * (2 * slots + fine_all) * width,
    )(got, coarse, norm, fine.reshape(fine_all, width))

    returned = lax.all_to_all(error, "wide", split_axis=0, concat_axis=0, tiled=False)

    coarse_new, fine_new = call(
        update_kernel,
        (steps,),
        [
            whole((1, slots)),
            whole((fine_n, slots)),
            whole((slots, width)),
            whole((cells_dev, width)),
            pl.BlockSpec((tile, width), lambda i: (i, 0)),
        ],
        [
            whole((cells_dev, width)),
            pl.BlockSpec((cells_step, fine_n, width), lambda i: (i, 0, 0)),
        ],
        [
            jax.ShapeDtypeStruct((cells_dev, width), F32),
            jax.ShapeDtypeStruct((cells_dev, fine_n, width), F32),
        ],
        flops=2 * slots * fine_all * width,
        moved=2 * slots * width + 6 * fine_all * width,
    )(ids, weight, resid, coarse, seed)

    row_error = call(
        functools.partial(collect_kernel, peers),
        (1,),
        [whole((8, rows_dev)), whole((peers, 1, LANES))],
        whole((1, rows_dev)),
        jax.ShapeDtypeStruct((1, rows_dev), F32),
        moved=4 * (8 * rows_dev + peers * LANES),
    )(route, returned).reshape(rows_dev)
    return row_error, coarse_new, fine_new


def solution(mesh):
    in_specs = (
        P(("groups", "wide"), None),
        P(("groups", "wide")),
        P("groups"),
        P(("groups", "wide"), None),
        P(("groups", "wide"), None, None),
        P(("groups", "wide"), None),
    )
    out_specs = (
        P(("groups", "wide")),
        P(("groups", "wide"), None),
        P(("groups", "wide"), None, None),
    )
    return jax.shard_map(shards, mesh=mesh, in_specs=in_specs, out_specs=out_specs, check_vma=False)
```

time: 112 us -> 78.7 us (0.70)
  blocking collectives: 24.3 us -> 0 us
  Pallas kernels: 0 us -> 18.8 us
  matrix products: 13.7 us -> 0 us
  other arithmetic: 13.6 us -> 2.58 us
  starting transfers between devices: 20.3 us -> 16.7 us
  waiting for transfers between devices: 17.6 us -> 21 us
  local copies, waits for them, and re-layouts: 21.4 us -> 18.4 us
    all_gather x1 -> x0, blocking collectives: 24.3 us -> none  [shards(): table = lax.all_gather(coarse, 'wide', axis=0, tiled=True)]
    pallas_call x0 -> x4, Pallas kernels: none -> 18.8 us  [the longest x1 9.68 us: shards(): call(functools.partial(score_kernel, peers, capacity), (steps,), [whole((...]
    dot_general x4 -> x0, matrix products: 13.7 us -> none  [the longest x1 6.8 us: shards(): lax.dot_general(spread, resid, (((0,), (0,)), ((), ())), preferred_elemen...]
    unnamed x8 -> x24, local copies, waits for them, and re-layouts: 0.03 us -> 8.89 us
    gather x3 -> x1, local copies, waits for them, and re-layouts: 16.3 us -> 9.4 us  [shards(): seed = rows[reseed.reshape(fine_all)]]
    scatter x1 -> x0, other arithmetic: 6.82 us -> none  [shards(): send_rows = jnp.zeros((slots_all, width), jnp.bfloat16).at[slot].set(payl...]
    all_to_all x3 -> x2, starting transfers between devices: 20.3 us -> 16.7 us  [the longest x1 9.38 us: shards(): lax.all_to_all(error, 'wide', split_axis=0, concat_axis=0, tiled=False)]
    all_to_all x3 -> x2, waiting for transfers between devices: 17.6 us -> 21 us  [the longest x1 21 us: shards(): lax.all_to_all(send.reshape(peers, block, LANES), 'wide', split_axis=0, c...]
  transfers between devices with their start and end apart: 3 -> 2, of which waited for: 1 -> 1; matrix products, arithmetic and copies ran while one was open for 26% -> 15% of each run, Pallas kernels for 0% -> 9%
where the time goes in v1:
time: 78.7 us; the launch traced here: 78.2 us
  waiting for transfers between devices  21 us (27%)
  Pallas kernels  18.8 us (24%)
  local copies, waits for them, and re-layouts  18.4 us (23%)
  starting transfers between devices  16.7 us (21%)
  other arithmetic  2.58 us (3%)
    all_to_all x1, waiting for transfers between devices, shards(): lax.all_to_all(send.reshape(peers, block, LANES), 'wide', split_axis=0, c...  21 us
    pallas_call x1, Pallas kernels, shards(): call(functools.partial(score_kernel, peers, capacity), (steps,), [whole((...  9.68 us
    gather x1, local copies, waits for them, and re-layouts, shards(): seed = rows[reseed.reshape(fine_all)]  9.4 us
    all_to_all x1, starting transfers between devices, shards(): lax.all_to_all(error, 'wide', split_axis=0, concat_axis=0, tiled=False)  9.38 us
    unnamed x24, local copies, waits for them, and re-layouts  8.89 us
    all_to_all x1, starting transfers between devices, shards(): lax.all_to_all(send.reshape(peers, block, LANES), 'wide', split_axis=0, c...  7.36 us
    pallas_call x1, Pallas kernels, shards(): call(update_kernel, (steps,), [whole((1, slots)), whole((fine_n, slots)),...  6.98 us
    reduce_sum x1, other arithmetic, shards(): norm = jnp.sum(fine_wide * fine_wide, axis=-1)  2.57 us
  transfers between devices with their start and end apart: 2, of which 1 were waited for; matrix products, arithmetic and copies ran while one was open for 15% of the time, Pallas kernels for 9%

profile of v1, /device:TPU:0, one launch (start us, length us, event | category | flops | bytes accessed | tf_op | source)
XLA Modules:
  0.0 78.2 jit_solution(5429334934661985944)
XLA Ops:
  0.6 0.0 copy-start
  0.6 1.1 %copy-done = bf16[512,768]{1,0:T(8,128)(2,1)S(1)} copy-done((bf16[512,768]{1,0:T(8,128)(2,1)S(1)}, bf16[512,768]{1,0:T(8,128)(2,1)}, u32[]{:S(2)}) %copy-start) | copy-done | bytes 786456
  1.8 0.7 copy-done.7
  2.4 0.7 copy-done.8
  3.1 1.3 %shard_map.85 = (bf16[6400,128]{1,0:T(8,128)(2,1)S(1)}, s32[8,512]{1,0:T(8,128)S(1)}) custom-call(s32[1,512]{1,0:T(1,128)S(1)} %bitcast.9, s32[1,512]{1,0:T(1,128)S(1)} %bitcast.10, bf16[512,768]{1,0:T(8,128)(2,1)S(1)} %copy-done), custom_call_target="tpu_custom_call" | custom-call | flops 805306368 | bytes 2359296 | tf_op jit(solution)/shard_map/pallas_call | solution.py:212
  4.5 0.0 copy-start.5
  4.5 1.2 %copy-done.5 = bf16[6400,128]{1,0:T(8,128)(2,1)} copy-done((bf16[6400,128]{1,0:T(8,128)(2,1)}, bf16[6400,128]{1,0:T(8,128)(2,1)S(1)}, u32[]{:S(2)}) %copy-start.5) | copy-done | bytes 1638424
  5.7 7.4 %all-to-all-start = ((bf16[16,400,128]{2,1,0:T(8,128)(2,1)}), bf16[16,400,128]{2,1,0:T(8,128)(2,1)S(1)}, u32[]{:S(2)}, u32[]{:S(2)}) async-start(bf16[16,400,128]{2,1,0:T(8,128)(2,1)} %bitcast.8), calls=%async_computation | async-start | bytes 3276800 | tf_op jit(solution)/shard_map/all_to_all | solution.py:225
  13.0 0.0 copy-done.11
  13.1 0.1 reshape.61
  13.2 9.4 %gather_fusion = bf16[2048,768]{1,0:T(8,128)(2,1)} fusion(bf16[512,768]{1,0:T(8,128)(2,1)S(1)} %copy-done.1, s32[2048]{0:T(1024)S(1)} %broadcast_clamp_fusion), kind=kCustom, calls=%fused_computation | custom fusion | bytes 6299648 | tf_op jit(solution)/shard_map/gather | solution.py:231
  22.6 2.6 %multiply_reduce_fusion.norm_ref = f32[32,64]{1,0:T(8,128)S(1)} fusion(bf16[32,64,768]{2,1,0:T(8,128)(2,1)} %param.10), kind=kLoop, calls=%fused_computation.1 | loop fusion | flops 4716544 | bytes 3153920 | tf_op jit(solution)/shard_map/reduce_sum | solution.py:230
  25.1 21.0 %all-to-all-done = bf16[16,400,128]{2,1,0:T(8,128)(2,1)S(1)} async-done(((bf16[16,400,128]{2,1,0:T(8,128)(2,1)}), bf16[16,400,128]{2,1,0:T(8,128)(2,1)S(1)}, u32[]{:S(2)}, u32[]{:S(2)}) %all-to-all-start) | async-done | bytes 1638432 | tf_op jit(solution)/shard_map/all_to_all | solution.py:225
  46.2 1.2 %copy-done.3 = bf16[16,400,128]{2,1,0:T(8,128)(2,1)} copy-done((bf16[16,400,128]{2,1,0:T(8,128)(2,1)}, bf16[16,400,128]{2,1,0:T(8,128)(2,1)S(1)}, u32[]{:S(2)}) %copy-start.3) | copy-done | bytes 1638424
  47.4 1.4 %copy-done.4 = bf16[16,400,128]{2,1,0:T(8,128)(2,1)S(1)} copy-done((bf16[16,400,128]{2,1,0:T(8,128)(2,1)S(1)}, bf16[16,400,128]{2,1,0:T(8,128)(2,1)}, u32[]{:S(2)}) %copy-start.4) | copy-done | bytes 1638424
  48.8 9.7 %shard_map.86 = (f32[16,1,128]{2,1,0:T(1,128)}, bf16[64,1024]{1,0:T(8,128)(2,1)S(1)}, bf16[1024,768]{1,0:T(8,128)(2,1)S(1)}, s32[1,1024]{1,0:T(1,128)S(1)}) custom-call(bf16[6400,128]{1,0:T(8,128)(2,1)S(1)} %bitcast.7, bf16[32,768]{1,0:T(8,128)(2,1)S(1)} %copy-done.6, f32[32,64]{1,0:T(8,128)S(1)} %multiply_reduce_fusion.norm_ref, bf16[2048,768]{1,0:T(8,128)(2,1)} %bitcast.11), custom_call_target="tpu_custom_call" | custom-call | flops 3221225472 | bytes 6291456 | tf_op jit(solution)/shard_map/pallas_call | solution.py:236
  58.5 1.2 %copy-done.9 = bf16[1024,768]{1,0:T(8,128)(2,1)} copy-done((bf16[1024,768]{1,0:T(8,128)(2,1)}, bf16[1024,768]{1,0:T(8,128)(2,1)S(1)}, u32[]{:S(2)}) %copy-start.9) | copy-done | bytes 1572888
  59.6 9.4 %all-to-all-start.1 = ((f32[16,1,128]{2,1,0:T(1,128)}), f32[16,1,128]{2,1,0:T(1,128)S(1)}, u32[]{:S(2)}, u32[]{:S(2)}) async-start(f32[16,1,128]{2,1,0:T(1,128)} %get-tuple-element.13), calls=%async_computation.1 | async-start | bytes 16384 | tf_op jit(solution)/shard_map/all_to_all | solution.py:262
  69.0 0.0 copy-done.2
  69.0 0.0 copy-start.10
  69.1 1.4 %copy-done.10 = bf16[1024,768]{1,0:T(8,128)(2,1)S(1)} copy-done((bf16[1024,768]{1,0:T(8,128)(2,1)S(1)}, bf16[1024,768]{1,0:T(8,128)(2,1)}, u32[]{:S(2)}) %copy-start.10) | copy-done | bytes 1572888
  70.5 7.0 %shard_map.88 = (f32[32,768]{1,0:T(8,128)}, f32[32,64,768]{2,1,0:T(8,128)}) custom-call(s32[1,1024]{1,0:T(1,128)S(1)} %get-tuple-element.14.ids_ref, bf16[64,1024]{1,0:T(8,128)(2,1)S(1)} %get-tuple-element.15.weight_ref, bf16[1024,768]{1,0:T(8,128)(2,1)S(1)} %copy-done.10, bf16[32,768]{1,0:T(8,128)(2,1)S(1)} %copy-done.6, bf16[2048,768]{1,0:T(8,128)(2,1)S(1)} %copy-done.2), custom_call_target="tpu_custom_call" | custom-call | flops 3221225472 | bytes 11010048 | tf_op jit(solution)/shard_map/pallas_call | solution.py:264
  77.4 0.0 all-to-all-done.1.error_ref
  77.4 0.8 %shard_map.87 = f32[1,512]{1,0:T(1,128)} custom-call(s32[8,512]{1,0:T(8,128)S(1)} %get-tuple-element.11.route_ref, f32[16,1,128]{2,1,0:T(1,128)S(1)} %all-to-all-done.1.error_ref), custom_call_target="tpu_custom_call" | custom-call | bytes 24576 | tf_op jit(solution)/shard_map/pallas_call | solution.py:286
  (13 shorter events, 0.0 us)
Async XLA Ops:
  0.6 1.1 %copy-start = (bf16[512,768]{1,0:T(8,128)(2,1)S(1)}, bf16[512,768]{1,0:T(8,128)(2,1)}, u32[]{:S(2)}) copy-start(bf16[512,768]{1,0:T(8,128)(2,1)} %rows_ref.1) | copy-start | bytes 2359300
  1.8 0.7 copy-start.7
  2.4 0.7 copy-start.8
  3.1 9.9 %copy-start.11 = (s32[32,64]{1,0:T(8,128)S(1)}, s32[32,64]{1,0:T(8,128)}, u32[]{:S(2)}) copy-start(s32[32,64]{1,0:T(8,128)} %param.11) | copy-start | bytes 24580
  3.1 10.0 %copy-start.1 = (bf16[512,768]{1,0:T(8,128)(2,1)S(1)}, bf16[512,768]{1,0:T(8,128)(2,1)}, u32[]{:S(2)}) copy-start(bf16[512,768]{1,0:T(8,128)(2,1)} %rows_ref.1) | copy-start | bytes 2359300
  4.5 1.2 %copy-start.5 = (bf16[6400,128]{1,0:T(8,128)(2,1)}, bf16[6400,128]{1,0:T(8,128)(2,1)S(1)}, u32[]{:S(2)}) copy-start(bf16[6400,128]{1,0:T(8,128)(2,1)S(1)} %get-tuple-element.12) | copy-start | bytes 4915204
  5.7 40.5 %all-to-all-start = ((bf16[16,400,128]{2,1,0:T(8,128)(2,1)}), bf16[16,400,128]{2,1,0:T(8,128)(2,1)S(1)}, u32[]{:S(2)}, u32[]{:S(2)}) async-start(bf16[16,400,128]{2,1,0:T(8,128)(2,1)} %bitcast.8), calls=%async_computation | async-start | bytes 3276800 | tf_op jit(solution)/shard_map/all_to_all | solution.py:225
  22.6 24.8 %copy-start.6 = (bf16[32,768]{1,0:T(8,128)(2,1)S(1)}, bf16[32,768]{1,0:T(8,128)(2,1)}, u32[]{:S(2)}) copy-start(bf16[32,768]{1,0:T(8,128)(2,1)} %coarse_ref.3) | copy-start | bytes 147460
  46.2 1.2 %copy-start.3 = (bf16[16,400,128]{2,1,0:T(8,128)(2,1)}, bf16[16,400,128]{2,1,0:T(8,128)(2,1)S(1)}, u32[]{:S(2)}) copy-start(bf16[16,400,128]{2,1,0:T(8,128)(2,1)S(1)} %all-to-all-done) | copy-start | bytes 4915204
  47.4 1.4 %copy-start.4 = (bf16[16,400,128]{2,1,0:T(8,128)(2,1)S(1)}, bf16[16,400,128]{2,1,0:T(8,128)(2,1)}, u32[]{:S(2)}) copy-start(bf16[16,400,128]{2,1,0:T(8,128)(2,1)} %copy-done.3) | copy-start | bytes 4915204
  48.8 20.2 %copy-start.2 = (bf16[2048,768]{1,0:T(8,128)(2,1)S(1)}, bf16[2048,768]{1,0:T(8,128)(2,1)}, u32[]{:S(2)}) copy-start(bf16[2048,768]{1,0:T(8,128)(2,1)} %gather_fusion) | copy-start | bytes 9437188
  58.5 1.2 %copy-start.9 = (bf16[1024,768]{1,0:T(8,128)(2,1)}, bf16[1024,768]{1,0:T(8,128)(2,1)S(1)}, u32[]{:S(2)}) copy-start(bf16[1024,768]{1,0:T(8,128)(2,1)S(1)} %get-tuple-element.16.resid_ref) | copy-start | bytes 4718596
  59.6 17.8 %all-to-all-start.1 = ((f32[16,1,128]{2,1,0:T(1,128)}), f32[16,1,128]{2,1,0:T(1,128)S(1)}, u32[]{:S(2)}, u32[]{:S(2)}) async-start(f32[16,1,128]{2,1,0:T(1,128)} %get-tuple-element.13), calls=%async_computation.1 | async-start | bytes 16384 | tf_op jit(solution)/shard_map/all_to_all | solution.py:262
  69.0 1.4 %copy-start.10 = (bf16[1024,768]{1,0:T(8,128)(2,1)S(1)}, bf16[1024,768]{1,0:T(8,128)(2,1)}, u32[]{:S(2)}) copy-start(bf16[1024,768]{1,0:T(8,128)(2,1)} %copy-done.9) | copy-start | bytes 4718596

commit v2 on v0

v2 whole, which is shorter than its diff:
```python
import functools

import jax
import jax.numpy as jnp
from jax import lax
from jax.experimental import pallas as pl
from jax.experimental.pallas import tpu as pltpu
from jax.sharding import PartitionSpec as P

TEMP = 16
LANES = 128
META = 16
VMEM_LIMIT = 24 * 1024 * 1024
BF = jnp.bfloat16
F32 = jnp.float32


def iota(shape, dim):
    return lax.broadcasted_iota(jnp.int32, shape, dim)


def hot(index, size, dtype=BF):
    return (iota((size, index.shape[1]), 0) == index).astype(F32).astype(dtype)


def dot(a, b, dims=((1,), (0,))):
    return lax.dot_general(a, b, (dims, ((), ())), preferred_element_type=F32)


def split3(x):
    high = x.astype(BF)
    rest = x - high.astype(F32)
    mid = rest.astype(BF)
    return high, mid, (rest - mid.astype(F32)).astype(BF)


def put_block(ref, base, rows, meta):
    count, width = rows.shape
    chunks = width // LANES
    whole_rows = count // 16 * 16
    for j in range(chunks):
        ref[base + j * whole_rows : base + (j + 1) * whole_rows, :] = rows[
            :whole_rows, j * LANES : (j + 1) * LANES
        ].astype(BF)
    base += chunks * whole_rows
    if count > whole_rows:
        for j in range(0, chunks, 2):
            pair = [
                rows[whole_rows:, i * LANES : (i + 1) * LANES] for i in (j, j + 1)
            ]
            ref[base : base + 16, :] = jnp.concatenate(pair, axis=0).astype(BF)
            base += 16
    ref[base : base + META, :] = meta


def get_block(ref, base, count, chunks):
    whole_rows = count // 16 * 16
    parts = [
        ref[base + j * whole_rows : base + (j + 1) * whole_rows, :].astype(F32)
        for j in range(chunks)
    ]
    if count > whole_rows:
        base += chunks * whole_rows
        for j in range(0, chunks, 2):
            pair = ref[base + j * 8 : base + j * 8 + 16, :].astype(F32)
            parts[j] = jnp.concatenate([parts[j], pair[:8]], axis=0)
            parts[j + 1] = jnp.concatenate([parts[j + 1], pair[8:]], axis=0)
    return parts


def get_meta(ref, base, count, chunks):
    first = base + chunks * count
    return ref[first : first + META, :].astype(F32)


def find_route(cells_dev, peers, cell_ref, place_ref, upper):
    rows_dev = cell_ref.shape[1]
    cells = place_ref.shape[1]
    cell = cell_ref[...]
    place = place_ref[...]
    table_row = iota((16, cells), 0)
    table = jnp.where(
        table_row == 0, place // cells_dev, jnp.where(table_row == 1, place % cells_dev, 0)
    ).astype(F32).astype(BF)
    found = jnp.zeros((16, rows_dev), F32)
    step = min(cells, 512)
    for first in range(0, cells, step):
        found += dot(table[:, first : first + step], hot(cell - first, step))
    owner = found[0:1].astype(jnp.int32)
    owner_hot = hot(owner, peers, F32)
    running = dot(owner_hot.astype(BF), upper)
    rank = (jnp.sum(running * owner_hot, axis=0, keepdims=True) - 1.0).astype(jnp.int32)
    return owner, found[1:2], rank, owner_hot


def prefix(rows_dev):
    return (iota((rows_dev, rows_dev), 0) <= iota((rows_dev, rows_dev), 1)).astype(F32).astype(BF)


def fetch(sources, targets, sems):
    copies = [
        pltpu.make_async_copy(source, target, sems.at[i])
        for i, (source, target) in enumerate(zip(sources, targets, strict=True))
    ]
    for copy in copies:
        copy.start()
    return copies


def pack_kernel(
    peers, capacity, cells_dev, cell_hbm, place_hbm, rows_hbm,
    send_hbm, route_ref, cell_ref, place_ref, rows_ref, send_ref, in_sems, out_sems,
):
    arrivals = fetch(
        (cell_hbm, place_hbm, rows_hbm), (cell_ref, place_ref, rows_ref), in_sems
    )
    rows_dev, width = rows_ref.shape
    block = (width // LANES) * capacity + META
    upper = prefix(rows_dev)
    arrivals[0].wait()
    arrivals[1].wait()
    owner, local, rank, owner_hot = find_route(cells_dev, peers, cell_ref, place_ref, upper)
    route_ref[...] = jnp.where(iota((8, rows_dev), 0) == 0, owner, rank)
    ids = dot((owner_hot * (local + 1.0)).astype(BF), hot(rank, LANES), ((1,), (1,))).astype(BF)
    slot = owner * capacity + rank
    group = max(1, 256 // capacity)
    arrivals[2].wait()
    departures = []
    for first in range(0, peers, group):
        packed = dot(hot(slot - first * capacity, group * capacity), rows_ref[...])
        for p in range(group):
            put_block(
                send_ref,
                (first + p) * block,
                packed[p * capacity : (p + 1) * capacity],
                jnp.broadcast_to(ids[first + p : first + p + 1], (META, LANES)),
            )
        part = pl.ds(first * block, group * block)
        departures.append(
            pltpu.make_async_copy(
                send_ref.at[part], send_hbm.at[part], out_sems.at[first // group]
            )
        )
        departures[-1].start()
    for copy in departures:
        copy.wait()


def pack_split_kernel(
    peers, capacity, cells_dev, distances, cell_hbm, place_hbm, rows_hbm, *refs
):
    far_hbms = refs[: len(distances)]
    (
        near_hbm, route_ref, cell_ref, place_ref, rows_ref, send_ref, in_sems, out_sems
    ) = refs[len(distances) :]
    arrivals = fetch(
        (cell_hbm, place_hbm, rows_hbm), (cell_ref, place_ref, rows_ref), in_sems
    )
    rows_dev, width = rows_ref.shape
    half = peers // 2
    block = (width // LANES) * capacity + META
    upper = prefix(rows_dev)
    me = lax.axis_index("wide")
    arrivals[0].wait()
    arrivals[1].wait()
    owner, local, rank, _ = find_route(cells_dev, peers, cell_ref, place_ref, upper)
    route_ref[...] = jnp.where(iota((8, rows_dev), 0) == 0, owner, rank)
    apart = owner ^ me
    order = owner & (half - 1)
    for i, r in enumerate(distances):
        order = jnp.where(apart == r, half + i, order)
    slot = order * capacity + rank
    ids = dot(
        (hot(order, peers, F32) * (local + 1.0)).astype(BF), hot(rank, LANES), ((1,), (1,))
    ).astype(BF)
    group = max(1, 256 // capacity)
    arrivals[2].wait()
    departures = []
    for first in range(0, peers, group):
        packed = dot(hot(slot - first * capacity, group * capacity), rows_ref[...])
        for p in range(group):
            i = first + p
            put_block(
                send_ref,
                i * block,
                packed[p * capacity : (p + 1) * capacity],
                jnp.broadcast_to(ids[i : i + 1], (META, LANES)),
            )
            target = near_hbm.at[pl.ds(i * block, block)] if i < half else far_hbms[i - half]
            departures.append(
                pltpu.make_async_copy(
                    send_ref.at[pl.ds(i * block, block)], target, out_sems.at[i]
                )
            )
            departures[-1].start()
    for copy in departures:
        copy.wait()


def seed_kernel(reseed_ref, rows_ref, seed_hbm, seed_ref, sems):
    rows_dev = rows_ref.shape[0]
    part = seed_ref.shape[0] // sems.shape[0]
    copies = []
    for i in range(sems.shape[0]):
        here = slice(i * part, (i + 1) * part)
        picked = hot(reseed_ref[:, here], rows_dev)
        seed_ref[here, :] = dot(picked, rows_ref[...], ((0,), (0,))).astype(BF)
        copies.append(
            pltpu.make_async_copy(seed_ref.at[here], seed_hbm.at[here], sems.at[i])
        )
        copies[-1].start()
    for copy in copies:
        copy.wait()


def score_kernel(blocks, capacity, far_of, known, coarse_ref, norm_ref, fine_ref, *refs):
    got_refs = refs[: len(blocks)]
    known_refs = refs[len(blocks) : len(blocks) + len(known)]
    error_ref, weight_ref, ids_ref, resid_hbm, resid_ref, sems = refs[len(blocks) + len(known) :]
    cells_dev, width = coarse_ref.shape
    fine_n = norm_ref.shape[1]
    chunks = width // LANES
    size = chunks * capacity + META
    group = max(1, 256 // capacity)
    tile = max(1, 512 // fine_n) * fine_n
    places = [(ref, b * size) for ref, count in zip(got_refs, blocks) for b in range(count)]
    error_ref[...] = jnp.zeros_like(error_ref)
    rows_of = list(range(len(places)))
    if far_of is not None:
        me = lax.axis_index("wide")
        rows_of = [me ^ r for r in far_of]
        half = error_ref.shape[0] // 2
        for ref, distances in zip(known_refs, known):
            for i in range(ref.shape[0]):
                row = (me & half) + i if distances is None else me ^ distances[i]
                error_ref[row] = ref[i]
    for p, (ref, base) in enumerate(places):
        ids_ref[:, p * capacity : (p + 1) * capacity] = (
            get_meta(ref, base, capacity, chunks)[0:1, :capacity].astype(jnp.int32) - 1
        )
    norms = split3(norm_ref[...])
    copies = []
    for first in range(0, len(places), group):
        some = places[first : first + group]
        span = len(some) * capacity
        here = slice(first * capacity, first * capacity + span)
        ids = ids_ref[:, here]
        member = hot(ids, cells_dev)
        own = dot(member, coarse_ref[...], ((0,), (0,)))
        square = jnp.zeros((span, LANES), F32)
        got = [get_block(ref, base, capacity, chunks) for ref, base in some]
        for j in range(chunks):
            lanes = slice(j * LANES, (j + 1) * LANES)
            part = (jnp.concatenate([g[j] for g in got], axis=0) - own[:, lanes]).astype(BF)
            resid_ref[here, lanes] = part
            wide = part.astype(F32)
            square += wide * wide
        resid = resid_ref[here, :]
        copies.append(
            pltpu.make_async_copy(resid_ref.at[here], resid_hbm.at[here], sems.at[first // group])
        )
        copies[-1].start()
        column = jnp.sum(square, axis=1, keepdims=True)
        diagonal = iota((span, span), 0) == iota((span, span), 1)
        square_row = jnp.sum(jnp.where(diagonal, column, 0.0), axis=0, keepdims=True)
        best = jnp.zeros((fine_n, span), F32)
        for start in range(0, cells_dev * fine_n, tile):
            scores = dot(fine_ref[start : start + tile, :], resid, ((1,), (1,)))
            for c in range(tile // fine_n):
                best = jnp.where(
                    ids == start // fine_n + c, scores[c * fine_n : (c + 1) * fine_n], best
                )
        norm = sum(dot(part, member, ((0,), (0,))) for part in norms)
        logit = (2.0 * best - norm) * (1.0 / TEMP)
        peak = jnp.max(logit, axis=0, keepdims=True)
        expo = jnp.exp(logit - peak)
        total = jnp.sum(expo, axis=0, keepdims=True)
        weight_ref[:, here] = (expo / total).astype(BF)
        error = square_row - TEMP * (peak + jnp.log(total))
        for p in range(len(some)):
            error_ref[rows_of[first + p], :, :capacity] = error[
                :, p * capacity : (p + 1) * capacity
            ]
    for copy in copies:
        copy.wait()


def update_kernel(sets, coarse_ref, *refs):
    ids_refs, weight_refs, resid_hbms = (refs[i * sets : (i + 1) * sets] for i in range(3))
    (
        seed_hbm, coarse_out_ref, fine_hbm, resid_ref, seed_ref, out_ref, spread_ref, share_ref,
        in_sems, seed_sems, out_sems,
    ) = refs[3 * sets :]
    cells_dev, width = coarse_ref.shape
    fine_n = weight_refs[0].shape[0]
    steps = out_sems.shape[0]
    cells = cells_dev // steps
    rows = cells * fine_n
    starts = [sum(r.shape[0] for r in resid_hbms[:i]) for i in range(sets)]
    arrivals = fetch(
        resid_hbms,
        [resid_ref.at[pl.ds(s, r.shape[0])] for s, r in zip(starts, resid_hbms)],
        in_sems,
    )
    half = seed_ref.shape[0] // 2
    parts = [pl.ds(0, half), pl.ds(half, half)]
    seeds = fetch([seed_hbm.at[p] for p in parts], [seed_ref.at[p] for p in parts], seed_sems)
    ids = jnp.concatenate([ref[...] for ref in ids_refs], axis=1)
    weight = jnp.concatenate([ref[...] for ref in weight_refs], axis=1).astype(F32)
    centre = coarse_ref[...].astype(F32)

    def spread(step):
        for c in range(cells):
            part = jnp.where(ids == step * cells + c, weight, 0.0)
            spread_ref[step % 2, c * fine_n : (c + 1) * fine_n, :] = part.astype(BF)
            first = step * rows + c * fine_n
            share_ref[first : first + fine_n, :] = jnp.broadcast_to(
                1.0 / (jnp.sum(part, axis=1, keepdims=True) + 1.0), (fine_n, LANES)
            )

    def finish(step):
        for c in range(cells):
            here = slice(step * rows + c * fine_n, step * rows + (c + 1) * fine_n)
            own = centre[step * cells + c : step * cells + c + 1]
            share = share_ref[here, :]
            for j in range(0, width, LANES):
                lanes = slice(j, j + LANES)
                seed = seed_ref[here, lanes].astype(F32) - own[:, lanes]
                out_ref[here, lanes] = (out_ref[here, lanes] + seed) * share
        part = pl.ds(step * rows, rows)
        copy = pltpu.make_async_copy(out_ref.at[part], fine_hbm.at[part], out_sems.at[step])
        copy.start()
        return copy

    spread(0)
    for copy in arrivals:
        copy.wait()
    departures = []
    for step in range(steps + 1):
        if step == 1:
            seeds[0].wait()
        if step == steps // 2 + 1:
            seeds[1].wait()
        if step < steps:
            out_ref[step * rows : (step + 1) * rows, :] = dot(spread_ref[step % 2], resid_ref[...])
        if step + 1 < steps:
            spread(step + 1)
        if step > 0:
            departures.append(finish(step - 1))
    member = hot(ids, cells_dev, F32)
    count = jnp.sum(member, axis=1, keepdims=True)
    coarse_out_ref[...] = centre + dot(member.astype(BF), resid_ref[...]) / (count + 1.0)
    for copy in departures:
        copy.wait()


def collect_kernel(peers, route_ref, error_ref, out_ref):
    owner_hot = hot(route_ref[0:1, :], peers, F32)
    rank_hot = hot(route_ref[1:2, :], LANES)
    error = error_ref[...].reshape(peers, LANES)
    picked = sum(dot(part, rank_hot) for part in split3(error))
    out_ref[...] = jnp.sum(picked * owner_hot, axis=0, keepdims=True)


def far(x):
    return pltpu.with_memory_space_constraint(x, pltpu.HBM)


def whole(shape):
    return pl.BlockSpec(shape, lambda *_: (0,) * len(shape))


HBM = pl.BlockSpec(memory_space=pltpu.HBM)
VMEM = pl.BlockSpec(memory_space=pltpu.VMEM)


def call(kernel, grid, in_specs, out_specs, out_shape, scratch=(), flops=0, moved=0):
    return pl.pallas_call(
        kernel,
        grid=grid,
        in_specs=in_specs,
        out_specs=out_specs,
        out_shape=out_shape,
        scratch_shapes=scratch,
        compiler_params=pltpu.CompilerParams(vmem_limit_bytes=VMEM_LIMIT),
        cost_estimate=pl.CostEstimate(flops=flops, bytes_accessed=moved, transcendentals=0),
    )


def shape_of(shape, dtype):
    return jax.ShapeDtypeStruct(shape, dtype)


def score(got, blocks, capacity, coarse, norm, fine, far_of=None, known=(), errors=(), peers=0):
    width = coarse.shape[1]
    fine_n = norm.shape[1]
    count = sum(blocks)
    slots = count * capacity
    return call(
        functools.partial(score_kernel, blocks, capacity, far_of, known),
        (),
        [VMEM] * (3 + len(got) + len(errors)),
        [VMEM, VMEM, VMEM, HBM],
        [
            shape_of((peers or count, 1, LANES), F32),
            shape_of((fine_n, slots), BF),
            shape_of((1, slots), jnp.int32),
            pltpu.HBM((slots, width), BF),
        ],
        scratch=[
            pltpu.VMEM((slots, width), BF),
            pltpu.SemaphoreType.DMA((count,)),
        ],
        flops=2 * slots * fine.shape[0] * width,
        moved=2 * (2 * slots + fine.shape[0]) * width,
    )(coarse, norm, fine, *got, *errors)


def update(scored, coarse, seed, cells_dev, fine_n):
    width = coarse.shape[1]
    fine_all = cells_dev * fine_n
    sets = len(scored)
    _, weights, ids, resids = zip(*scored)
    slots = sum(r.shape[0] for r in resids)
    steps = max(2, cells_dev // 4)
    coarse_new, fine_new = call(
        functools.partial(update_kernel, sets),
        (),
        [VMEM] * (1 + 2 * sets) + [HBM] * (sets + 1),
        [VMEM, HBM],
        [shape_of((cells_dev, width), F32), pltpu.HBM((fine_all, width), F32)],
        scratch=[
            pltpu.VMEM((slots, width), BF),
            pltpu.VMEM((fine_all, width), BF),
            pltpu.VMEM((fine_all, width), F32),
            pltpu.VMEM((2, fine_all // steps, slots), BF),
            pltpu.VMEM((fine_all, LANES), F32),
            pltpu.SemaphoreType.DMA((sets,)),
            pltpu.SemaphoreType.DMA((2,)),
            pltpu.SemaphoreType.DMA((steps,)),
        ],
        flops=2 * slots * fine_all * width,
        moved=2 * slots * width + 6 * fine_all * width,
    )(coarse, *ids, *weights, *[far(r) for r in resids], far(seed))
    return coarse_new, fine_new.reshape(cells_dev, fine_n, width)


def shards(rows, cell, cell_place, coarse, fine, reseed):
    peers = lax.axis_size("wide")
    rows_dev, width = rows.shape
    cells_dev, fine_n, _ = fine.shape
    cells = cell_place.shape[0]
    capacity = max(16, 2 * rows_dev // peers)
    slots = peers * capacity
    block = (width // LANES) * capacity + META
    fine_all = cells_dev * fine_n

    fine_wide = fine.astype(F32)
    norm = jnp.sum(fine_wide * fine_wide, axis=-1)
    fine_flat = fine.reshape(fine_all, width)
    seed = call(
        seed_kernel,
        (),
        [VMEM, VMEM],
        HBM,
        pltpu.HBM((fine_all, width), BF),
        scratch=[pltpu.VMEM((fine_all, width), BF), pltpu.SemaphoreType.DMA((4,))],
        flops=2 * fine_all * rows_dev * width,
        moved=2 * (fine_all + rows_dev) * width,
    )(reseed.reshape(1, fine_all), rows)
    cell = far(cell.reshape(1, rows_dev))
    cell_place = far(cell_place.reshape(1, cells))
    if capacity == 64 and peers == 16:
        half = peers // 2
        distances = [8, 12, 9, 13, 10, 14, 11, 15]
        *sends, near_send, route = call(
            functools.partial(pack_split_kernel, peers, capacity, cells_dev, distances),
            (),
            [HBM] * 3,
            [HBM] * (half + 1) + [VMEM],
            [
                *[pltpu.HBM((block, LANES), BF)] * half,
                pltpu.HBM((half * block, LANES), BF),
                shape_of((8, rows_dev), jnp.int32),
            ],
            scratch=[
                pltpu.VMEM((1, rows_dev), jnp.int32),
                pltpu.VMEM((1, cells), jnp.int32),
                pltpu.VMEM((rows_dev, width), BF),
                pltpu.VMEM((peers * block, LANES), BF),
                pltpu.SemaphoreType.DMA((3,)),
                pltpu.SemaphoreType.DMA((peers,)),
            ],
            flops=2 * slots * rows_dev * width,
            moved=2 * (slots + 2 * rows_dev) * width,
        )(cell, cell_place, far(rows))
        got = []
        window = 5
        for i, r in enumerate(distances):
            block_out = sends[i]
            if i >= window:
                block_out, got[i - window] = lax.optimization_barrier((block_out, got[i - window]))
            got.append(lax.ppermute(block_out, "wide", [(p, p ^ r) for p in range(peers)]))
        halves = [list(range(half)), list(range(half, peers))]
        got_near = lax.all_to_all(
            near_send.reshape(half, block, LANES), "wide", split_axis=0, concat_axis=0,
            tiled=False, axis_index_groups=halves,
        ).reshape(half * block, LANES)
        tables = (coarse, norm, fine_flat)
        scored = [score([got_near], [half], capacity, *tables)]
        scored.append(score(got[:4], [1] * 4, capacity, *tables))
        known = (None, distances[:4])
        errors = [x[0] for x in scored]
        scored.append(
            score(got[4:], [1] * 4, capacity, *tables, distances[4:], known, errors, peers)
        )
    else:
        send, route = call(
            functools.partial(pack_kernel, peers, capacity, cells_dev),
            (),
            [HBM] * 3,
            [HBM, VMEM],
            [pltpu.HBM((peers * block, LANES), BF), shape_of((8, rows_dev), jnp.int32)],
            scratch=[
                pltpu.VMEM((1, rows_dev), jnp.int32),
                pltpu.VMEM((1, cells), jnp.int32),
                pltpu.VMEM((rows_dev, width), BF),
                pltpu.VMEM((peers * block, LANES), BF),
                pltpu.SemaphoreType.DMA((3,)),
                pltpu.SemaphoreType.DMA((peers,)),
            ],
            flops=2 * slots * rows_dev * width,
            moved=2 * (slots + rows_dev) * width,
        )(cell, cell_place, far(rows))
        got = lax.all_to_all(
            send.reshape(peers, block, LANES), "wide", split_axis=0, concat_axis=0, tiled=False
        ).reshape(peers * block, LANES)
        scored = [score([got], [peers], capacity, coarse, norm, fine_flat)]

    returned = lax.all_to_all(scored[-1][0], "wide", split_axis=0, concat_axis=0, tiled=False)
    coarse_new, fine_new = update(scored, coarse, seed, cells_dev, fine_n)
    row_error = call(
        functools.partial(collect_kernel, peers),
        (),
        [VMEM, VMEM],
        VMEM,
        shape_of((1, rows_dev), F32),
        moved=4 * (8 * rows_dev + peers * LANES),
    )(route, returned).reshape(rows_dev)
    return row_error, coarse_new, fine_new


def solution(mesh):
    in_specs = (
        P(("groups", "wide"), None),
        P(("groups", "wide")),
        P("groups"),
        P(("groups", "wide"), None),
        P(("groups", "wide"), None, None),
        P(("groups", "wide"), None),
    )
    out_specs = (
        P(("groups", "wide")),
        P(("groups", "wide"), None),
        P(("groups", "wide"), None, None),
    )
    return jax.shard_map(shards, mesh=mesh, in_specs=in_specs, out_specs=out_specs, check_vma=False)
```

time: 112 us -> 67.9 us (0.61)
  Pallas kernels: 0 us -> 25 us
  blocking collectives: 24.3 us -> 0 us
  local copies, waits for them, and re-layouts: 21.4 us -> 2.54 us
  matrix products: 13.7 us -> 0 us
  other arithmetic: 13.6 us -> 0.68 us
  starting transfers between devices: 20.3 us -> 30.8 us
  waiting for transfers between devices: 17.6 us -> 7.6 us
    pallas_call x0 -> x7, Pallas kernels: none -> 25 us  [the longest x3 9.5 us: score(): call(functools.partial(score_kernel, blocks, capacity, far_of, known), ()...]
    all_gather x1 -> x0, blocking collectives: 24.3 us -> none  [shards(): table = lax.all_gather(coarse, 'wide', axis=0, tiled=True)]
    ppermute x0 -> x8, starting transfers between devices: none -> 18.9 us  [shards(): lax.ppermute(block_out, 'wide', [(p, p ^ r) for p in range(peers)])]
    all_to_all x3 -> x2, waiting for transfers between devices: 17.6 us -> 0.01 us  [the longest x1 0.01 us: shards(): lax.all_to_all(near_send.reshape(half, block, LANES), 'wide', split_axis=...]
    gather x3 -> x0, local copies, waits for them, and re-layouts: 16.3 us -> none  [the longest x1 9.37 us: shards(): seedres = rows[reseed].astype(jnp.float32) - coarse_wide[:, None, :]]
    dot_general x4 -> x0, matrix products: 13.7 us -> none  [the longest x1 6.8 us: shards(): lax.dot_general(spread, resid, (((0,), (0,)), ((), ())), preferred_elemen...]
    all_to_all x3 -> x2, starting transfers between devices: 20.3 us -> 12 us  [the longest x1 6.73 us: shards(): lax.all_to_all(scored[-1][0], 'wide', split_axis=0, concat_axis=0, tiled=...]
    ppermute x0 -> x8, waiting for transfers between devices: none -> 7.59 us  [shards(): lax.ppermute(block_out, 'wide', [(p, p ^ r) for p in range(peers)])]
  transfers between devices with their start and end apart: 3 -> 10, of which waited for: 1 -> 3; matrix products, arithmetic and copies ran while one was open for 26% -> 2% of each run, Pallas kernels for 0% -> 26%
where the time goes in v2:
time: 67.9 us; the launch traced here: 67.5 us
  starting transfers between devices  30.8 us (45%)
  Pallas kernels  25 us (37%)
  waiting for transfers between devices  7.6 us (11%)
  local copies, waits for them, and re-layouts  2.54 us (4%)
  between operations  0.77 us (1%)
  other arithmetic  0.68 us (1%)
    ppermute x8, starting transfers between devices, shards(): lax.ppermute(block_out, 'wide', [(p, p ^ r) for p in range(peers)])  18.9 us
    pallas_call x3, Pallas kernels, score(): call(functools.partial(score_kernel, blocks, capacity, far_of, known), ()...  9.5 us
    pallas_call x1, Pallas kernels, update(): call(functools.partial(update_kernel, sets), (), [VMEM] * (1 + 2 * sets)...  8.69 us
    ppermute x8, waiting for transfers between devices, shards(): lax.ppermute(block_out, 'wide', [(p, p ^ r) for p in range(peers)])  7.59 us
    all_to_all x1, starting transfers between devices, shards(): lax.all_to_all(scored[-1][0], 'wide', split_axis=0, concat_axis=0, tiled=...  6.73 us
    all_to_all x1, starting transfers between devices, shards(): lax.all_to_all(near_send.reshape(half, block, LANES), 'wide', split_axis=...  5.24 us
    pallas_call x1, Pallas kernels, shards(): call(functools.partial(pack_split_kernel, peers, capacity, cells_dev, dis...  3.26 us
    pallas_call x1, Pallas kernels, shards(): call(seed_kernel, (), [VMEM, VMEM], HBM, pltpu.HBM((fine_all, width), BF)...  2.8 us
  transfers between devices with their start and end apart: 10, of which 3 were waited for; matrix products, arithmetic and copies ran while one was open for 2% of the time, Pallas kernels for 26%

profile of v2, /device:TPU:0, one launch (start us, length us, event | category | flops | bytes accessed | tf_op | source)
XLA Modules:
  0.0 67.5 jit_solution(7630494276608925421)
XLA Ops:
  0.7 3.3 %shard_map.85 = (bf16[400,128]{1,0:T(8,128)(2,1)}, bf16[400,128]{1,0:T(8,128)(2,1)}, bf16[400,128]{1,0:T(8,128)(2,1)}, bf16[400,128]{1,0:T(8,128)(2,1)}, bf16[40...) custom-call(s32[1,512]{1,0:T(1,128)} %bitcast.12, ...), custom_call_target="tpu_custom_call" | custom-call | flops 805306368 | bytes 3145728 | tf_op jit(solution)/shard_map/pallas_call | solution.py:476
  3.9 5.2 %all-to-all-start = ((bf16[8,400,128]{2,1,0:T(8,128)(2,1)}), bf16[8,400,128]{2,1,0:T(8,128)(2,1)}, u32[]{:S(2)}, u32[]{:S(2)}) async-start(bf16[8,400,128]{2,1,0:T(8,128)(2,1)} %bitcast.10), calls=%async_computation | async-start | bytes 1638400 | tf_op jit(solution)/shard_map/all_to_all | solution.py:505
  9.2 4.4 %collective-permute-start = (bf16[400,128]{1,0:T(8,128)(2,1)}, bf16[400,128]{1,0:T(8,128)(2,1)}, u32[]{:S(2)}, u32[]{:S(2)}) collective-permute-start(bf16[400,128]{1,0:T(8,128)(2,1)} %get-tuple-element.34), channel_id=1, source_target_pairs={{0,10},{1,11},{2,8},{3,9},{4,14},{5,15},{6,12},{7,13},{8,2},{9,3},... | collective-permute-start | bytes 307208 | tf_op jit(solution)/shard_map/ppermute | solution.py:503
  13.5 0.0 collective-permute-start.1
  13.5 3.8 %collective-permute-start.3 = (bf16[400,128]{1,0:T(8,128)(2,1)}, bf16[400,128]{1,0:T(8,128)(2,1)S(1)}, u32[]{:S(2)}, u32[]{:S(2)}) collective-permute-start(bf16[400,128]{1,0:T(8,128)(2,1)} %get-tuple-element.39), channel_id=1, source_target_pairs={{0,12},{1,13},{2,14},{3,15},{4,8},{5,9},{6,10},{7,11},{8,4},{9,5},... | collective-permute-start | bytes 307208 | tf_op jit(solution)/shard_map/ppermute | solution.py:503
  17.4 1.7 %collective-permute-start.7 = (bf16[400,128]{1,0:T(8,128)(2,1)}, bf16[400,128]{1,0:T(8,128)(2,1)}, u32[]{:S(2)}, u32[]{:S(2)}) collective-permute-start(bf16[400,128]{1,0:T(8,128)(2,1)} %get-tuple-element.49), channel_id=1, source_target_pairs={{0,13},{1,12},{2,15},{3,14},{4,9},{5,8},{6,11},{7,10},{8,5},{9,4},... | collective-permute-start | bytes 307208 | tf_op jit(solution)/shard_map/ppermute | solution.py:503
  19.1 0.8 %reshape.36.reseed_ref = s32[1,2048]{1,0:T(1,128)S(1)} reshape(s32[32,64]{1,0:T(8,128)} %param.11) | data formatting | bytes 16384 | tf_op jit(solution)/shard_map/reshape | solution.py:470
  19.9 0.7 %multiply_reduce_fusion.norm_ref = f32[32,64]{1,0:T(8,128)S(1)} fusion(bf16[32,64,768]{2,1,0:T(8,128)(2,1)S(1)} %copy-done), kind=kLoop, calls=%fused_computation | loop fusion | flops 4716544 | bytes 3153920 | tf_op jit(solution)/shard_map/reduce_sum | solution.py:459
  20.6 0.0 copy-start.2
  20.6 1.1 %copy-done.2 = bf16[512,768]{1,0:T(8,128)(2,1)S(1)} copy-done((bf16[512,768]{1,0:T(8,128)(2,1)S(1)}, bf16[512,768]{1,0:T(8,128)(2,1)}, u32[]{:S(2)}) %copy-start.2) | copy-done | bytes 786456
  21.7 2.8 %shard_map.90.refs_9_ = bf16[2048,768]{1,0:T(8,128)(2,1)} custom-call(s32[1,2048]{1,0:T(1,128)S(1)} %reshape.36.reseed_ref, bf16[512,768]{1,0:T(8,128)(2,1)S(1)} %copy-done.2), custom_call_target="tpu_custom_call" | custom-call | flops 1610612736 | bytes 3932160 | tf_op jit(solution)/shard_map/pallas_call | solution.py:461
  24.5 4.5 %collective-permute-start.2 = (bf16[400,128]{1,0:T(8,128)(2,1)}, bf16[400,128]{1,0:T(8,128)(2,1)}, u32[]{:S(2)}, u32[]{:S(2)}) collective-permute-start(bf16[400,128]{1,0:T(8,128)(2,1)} %get-tuple-element.37), channel_id=1, source_target_pairs={{0,14},{1,15},{2,12},{3,13},{4,10},{5,11},{6,8},{7,9},{8,6},{9,7},... | collective-permute-start | bytes 307208 | tf_op jit(solution)/shard_map/ppermute | solution.py:503
  29.0 1.7 %collective-permute-done.3.refs_1_ = bf16[400,128]{1,0:T(8,128)(2,1)S(1)} collective-permute-done((bf16[400,128]{1,0:T(8,128)(2,1)}, bf16[400,128]{1,0:T(8,128)(2,1)S(1)}, u32[]{:S(2)}, u32[]{:S(2)}) %collective-permute-start.3) | collective-permute-done | bytes 102432 | tf_op jit(solution)/shard_map/ppermute | solution.py:503
  30.7 5.2 %collective-permute-done.5.refs_2_ = bf16[400,128]{1,0:T(8,128)(2,1)S(1)} collective-permute-done((bf16[400,128]{1,0:T(8,128)(2,1)}, bf16[400,128]{1,0:T(8,128)(2,1)S(1)}, u32[]{:S(2)}, u32[]{:S(2)}) %collective-permute-start.5) | collective-permute-done | bytes 102432 | tf_op jit(solution)/shard_map/ppermute | solution.py:503
  35.9 4.4 %collective-permute-start.6 = (bf16[400,128]{1,0:T(8,128)(2,1)}, bf16[400,128]{1,0:T(8,128)(2,1)}, u32[]{:S(2)}, u32[]{:S(2)}) collective-permute-start(bf16[400,128]{1,0:T(8,128)(2,1)} %get-tuple-element.43), channel_id=1, source_target_pairs={{0,15},{1,14},{2,13},{3,12},{4,11},{5,10},{6,9},{7,8},{8,7},{9,6},... | collective-permute-start | bytes 307208 | tf_op jit(solution)/shard_map/ppermute | solution.py:503
  40.3 2.4 %shard_map.87 = (f32[4,1,128]{2,1,0:T(1,128)S(1)}, bf16[64,256]{1,0:T(8,128)(2,1)S(1)}, s32[1,256]{1,0:T(1,128)S(1)}, bf16[256,768]{1,0:T(8,128)(2,1)}) custom-call(bf16[32,768]{1,0:T(8,128)(2,1)S(1)} %copy-done.1, f32[32,64]{1,0:T(8,128)S(1)} %multiply_reduce_fusion.norm_ref, bf16[2048,768]{1,0:T(8,128)(2,1)S(1)} %bitcast.7, ...), custom_call_target="tpu_custom_call" | custom-call | flops 805306368 | bytes 3932160 | tf_op jit(solution)/shard_map/pallas_call | solution.py:399
  42.7 0.0 copy-start.3
  42.8 0.6 copy-done.3
  43.4 3.9 %shard_map.86 = (f32[8,1,128]{2,1,0:T(1,128)S(1)}, bf16[64,512]{1,0:T(8,128)(2,1)S(1)}, s32[1,512]{1,0:T(1,128)S(1)}, bf16[512,768]{1,0:T(8,128)(2,1)}) custom-call(bf16[32,768]{1,0:T(8,128)(2,1)S(1)} %copy-done.1, f32[32,64]{1,0:T(8,128)S(1)} %multiply_reduce_fusion.norm_ref, bf16[2048,768]{1,0:T(8,128)(2,1)S(1)} %bitcast.8, bf16[3200,128]{1,0:T(8,128)(2,1)} %bitcast.4.refs_0_), custom_call_target="tpu_custom_call" | custom-call | flops 1610612736 | bytes 4718592 | tf_op jit(solution)/shard_map/pallas_call | solution.py:399
  47.3 0.7 %collective-permute-done.4.refs_2_ = bf16[400,128]{1,0:T(8,128)(2,1)} collective-permute-done((bf16[400,128]{1,0:T(8,128)(2,1)}, bf16[400,128]{1,0:T(8,128)(2,1)}, u32[]{:S(2)}, u32[]{:S(2)}) %collective-permute-start.4) | collective-permute-done | bytes 102432 | tf_op jit(solution)/shard_map/ppermute | solution.py:503
  48.0 3.2 %shard_map.88 = (f32[16,1,128]{2,1,0:T(1,128)}, bf16[64,256]{1,0:T(8,128)(2,1)S(1)}, s32[1,256]{1,0:T(1,128)S(1)}, bf16[256,768]{1,0:T(8,128)(2,1)}) custom-call(bf16[32,768]{1,0:T(8,128)(2,1)S(1)} %copy-done.1, f32[32,64]{1,0:T(8,128)S(1)} %multiply_reduce_fusion.norm_ref, bf16[2048,768]{1,0:T(8,128)(2,1)S(1)} %bitcast.9, ...), custom_call_target="tpu_custom_call" | custom-call | flops 805306368 | bytes 3932160 | tf_op jit(solution)/shard_map/pallas_call | solution.py:399
  51.2 6.7 %all-to-all-start.1 = ((f32[16,1,128]{2,1,0:T(1,128)}), f32[16,1,128]{2,1,0:T(1,128)S(1)}, u32[]{:S(2)}, u32[]{:S(2)}) async-start(f32[16,1,128]{2,1,0:T(1,128)} %get-tuple-element.51), calls=%async_computation.1 | async-start | bytes 16384 | tf_op jit(solution)/shard_map/all_to_all | solution.py:540
  58.0 8.7 %shard_map.91 = (f32[32,768]{1,0:T(8,128)}, f32[2048,768]{1,0:T(8,128)}) custom-call(bf16[32,768]{1,0:T(8,128)(2,1)S(1)} %copy-done.1, s32[1,512]{1,0:T(1,128)S(1)} %get-tuple-element.52.refs_0_, s32[1,256]{1,0:T(1,128)S(1)} %get-tuple-element.53.refs_1_, s32[1,256]{1,0:T(1,128)S(1)} %get-tuple-element.54.refs_2_, ...), custom_call_target="tpu_custom_call" | custom-call | flops 3221225472 | bytes 11010048 | tf_op jit(solution)/shard_map/pallas_call | solution.py:426
  66.7 0.8 %shard_map.89 = f32[1,512]{1,0:T(1,128)} custom-call(s32[8,512]{1,0:T(8,128)S(1)} %get-tuple-element.33.route_ref, f32[16,1,128]{2,1,0:T(1,128)S(1)} %all-to-all-done.1.error_ref), custom_call_target="tpu_custom_call" | custom-call | bytes 24576 | tf_op jit(solution)/shard_map/pallas_call | solution.py:542
  (15 shorter events, 0.0 us)
Async XLA Ops:
  0.6 19.3 %copy-start = (bf16[32,64,768]{2,1,0:T(8,128)(2,1)S(1)}, bf16[32,64,768]{2,1,0:T(8,128)(2,1)}, u32[]{:S(2)}) copy-start(bf16[32,64,768]{2,1,0:T(8,128)(2,1)} %param.10) | copy-start | bytes 9437188
  0.6 39.7 %copy-start.1 = (bf16[32,768]{1,0:T(8,128)(2,1)S(1)}, bf16[32,768]{1,0:T(8,128)(2,1)}, u32[]{:S(2)}) copy-start(bf16[32,768]{1,0:T(8,128)(2,1)} %coarse_ref.7) | copy-start | bytes 147460
  3.9 39.4 %all-to-all-start = ((bf16[8,400,128]{2,1,0:T(8,128)(2,1)}), bf16[8,400,128]{2,1,0:T(8,128)(2,1)}, u32[]{:S(2)}, u32[]{:S(2)}) async-start(bf16[8,400,128]{2,1,0:T(8,128)(2,1)} %bitcast.10), calls=%async_computation | async-start | bytes 1638400 | tf_op jit(solution)/shard_map/all_to_all | solution.py:505
  9.2 38.1 %collective-permute-start = (bf16[400,128]{1,0:T(8,128)(2,1)}, bf16[400,128]{1,0:T(8,128)(2,1)}, u32[]{:S(2)}, u32[]{:S(2)}) collective-permute-start(bf16[400,128]{1,0:T(8,128)(2,1)} %get-tuple-element.34), channel_id=1, source_target_pairs={{0,10},{1,11},{2,8},{3,9},{4,14},{5,15},{6,12},{7,13},{8,2},{9,3},... | collective-permute-start | bytes 307208 | tf_op jit(solution)/shard_map/ppermute | solution.py:503
  13.5 11.0 %collective-permute-start.1 = (bf16[400,128]{1,0:T(8,128)(2,1)}, bf16[400,128]{1,0:T(8,128)(2,1)S(1)}, u32[]{:S(2)}, u32[]{:S(2)}) collective-permute-start(bf16[400,128]{1,0:T(8,128)(2,1)} %get-tuple-element.36), channel_id=1, source_target_pairs={{0,8},{1,9},{2,10},{3,11},{4,12},{5,13},{6,14},{7,15},{8,0},{9,1},... | collective-permute-start | bytes 307208 | tf_op jit(solution)/shard_map/ppermute | solution.py:503
  13.5 17.1 %collective-permute-start.3 = (bf16[400,128]{1,0:T(8,128)(2,1)}, bf16[400,128]{1,0:T(8,128)(2,1)S(1)}, u32[]{:S(2)}, u32[]{:S(2)}) collective-permute-start(bf16[400,128]{1,0:T(8,128)(2,1)} %get-tuple-element.39), channel_id=1, source_target_pairs={{0,12},{1,13},{2,14},{3,15},{4,8},{5,9},{6,10},{7,11},{8,4},{9,5},... | collective-permute-start | bytes 307208 | tf_op jit(solution)/shard_map/ppermute | solution.py:503
  17.4 18.5 %collective-permute-start.5 = (bf16[400,128]{1,0:T(8,128)(2,1)}, bf16[400,128]{1,0:T(8,128)(2,1)S(1)}, u32[]{:S(2)}, u32[]{:S(2)}) collective-permute-start(bf16[400,128]{1,0:T(8,128)(2,1)} %get-tuple-element.42), channel_id=1, source_target_pairs={{0,9},{1,8},{2,11},{3,10},{4,13},{5,12},{6,15},{7,14},{8,1},{9,0},... | collective-permute-start | bytes 307208 | tf_op jit(solution)/shard_map/ppermute | solution.py:503
  17.4 22.9 %collective-permute-start.7 = (bf16[400,128]{1,0:T(8,128)(2,1)}, bf16[400,128]{1,0:T(8,128)(2,1)}, u32[]{:S(2)}, u32[]{:S(2)}) collective-permute-start(bf16[400,128]{1,0:T(8,128)(2,1)} %get-tuple-element.49), channel_id=1, source_target_pairs={{0,13},{1,12},{2,15},{3,14},{4,9},{5,8},{6,11},{7,10},{8,5},{9,4},... | collective-permute-start | bytes 307208 | tf_op jit(solution)/shard_map/ppermute | solution.py:503
  20.6 1.1 %copy-start.2 = (bf16[512,768]{1,0:T(8,128)(2,1)S(1)}, bf16[512,768]{1,0:T(8,128)(2,1)}, u32[]{:S(2)}) copy-start(bf16[512,768]{1,0:T(8,128)(2,1)} %rows_ref.1) | copy-start | bytes 2359300
  24.5 22.8 %collective-permute-start.2 = (bf16[400,128]{1,0:T(8,128)(2,1)}, bf16[400,128]{1,0:T(8,128)(2,1)}, u32[]{:S(2)}, u32[]{:S(2)}) collective-permute-start(bf16[400,128]{1,0:T(8,128)(2,1)} %get-tuple-element.37), channel_id=1, source_target_pairs={{0,14},{1,15},{2,12},{3,13},{4,10},{5,11},{6,8},{7,9},{8,6},{9,7},... | collective-permute-start | bytes 307208 | tf_op jit(solution)/shard_map/ppermute | solution.py:503
  30.7 17.3 %collective-permute-start.4 = (bf16[400,128]{1,0:T(8,128)(2,1)}, bf16[400,128]{1,0:T(8,128)(2,1)}, u32[]{:S(2)}, u32[]{:S(2)}) collective-permute-start(bf16[400,128]{1,0:T(8,128)(2,1)} %get-tuple-element.40), channel_id=1, source_target_pairs={{0,11},{1,10},{2,9},{3,8},{4,15},{5,14},{6,13},{7,12},{8,3},{9,2},... | collective-permute-start | bytes 307208 | tf_op jit(solution)/shard_map/ppermute | solution.py:503
  35.9 12.2 %collective-permute-start.6 = (bf16[400,128]{1,0:T(8,128)(2,1)}, bf16[400,128]{1,0:T(8,128)(2,1)}, u32[]{:S(2)}, u32[]{:S(2)}) collective-permute-start(bf16[400,128]{1,0:T(8,128)(2,1)} %get-tuple-element.43), channel_id=1, source_target_pairs={{0,15},{1,14},{2,13},{3,12},{4,11},{5,10},{6,9},{7,8},{8,7},{9,6},... | collective-permute-start | bytes 307208 | tf_op jit(solution)/shard_map/ppermute | solution.py:503
  42.7 0.6 copy-start.3
  43.4 14.6 %copy-start.4 = (bf16[64,256]{1,0:T(8,128)(2,1)S(1)}, bf16[64,256]{1,0:T(8,128)(2,1)}, u32[]{:S(2)}) copy-start(bf16[64,256]{1,0:T(8,128)(2,1)} %copy-done.3) | copy-start | bytes 98308
  51.2 15.5 %all-to-all-start.1 = ((f32[16,1,128]{2,1,0:T(1,128)}), f32[16,1,128]{2,1,0:T(1,128)S(1)}, u32[]{:S(2)}, u32[]{:S(2)}) async-start(f32[16,1,128]{2,1,0:T(1,128)} %get-tuple-element.51), calls=%async_computation.1 | async-start | bytes 16384 | tf_op jit(solution)/shard_map/all_to_all | solution.py:540

commit v3 on v2

--- a/solution.py
+++ b/solution.py
@@ -10,6 +10,8 @@
 TEMP = 16
 LANES = 128
 META = 16
+DISTANCES = [8, 1, 12, 2, 9, 3, 13, 4, 10, 5, 14, 6, 11, 7, 15, 0]
+WINDOW = 6
 VMEM_LIMIT = 24 * 1024 * 1024
 BF = jnp.bfloat16
 F32 = jnp.float32
@@ -149,15 +151,12 @@
 def pack_split_kernel(
     peers, capacity, cells_dev, distances, cell_hbm, place_hbm, rows_hbm, *refs
 ):
-    far_hbms = refs[: len(distances)]
-    (
-        near_hbm, route_ref, cell_ref, place_ref, rows_ref, send_ref, in_sems, out_sems
-    ) = refs[len(distances) :]
+    send_hbms = refs[:peers]
+    route_ref, cell_ref, place_ref, rows_ref, send_ref, in_sems, out_sems = refs[peers:]
     arrivals = fetch(
         (cell_hbm, place_hbm, rows_hbm), (cell_ref, place_ref, rows_ref), in_sems
     )
     rows_dev, width = rows_ref.shape
-    half = peers // 2
     block = (width // LANES) * capacity + META
     upper = prefix(rows_dev)
     me = lax.axis_index("wide")
@@ -166,9 +165,9 @@
     owner, local, rank, _ = find_route(cells_dev, peers, cell_ref, place_ref, upper)
     route_ref[...] = jnp.where(iota((8, rows_dev), 0) == 0, owner, rank)
     apart = owner ^ me
-    order = owner & (half - 1)
+    order = jnp.zeros_like(owner)
     for i, r in enumerate(distances):
-        order = jnp.where(apart == r, half + i, order)
+        order = jnp.where(apart == r, i, order)
     slot = order * capacity + rank
     ids = dot(
         (hot(order, peers, F32) * (local + 1.0)).astype(BF), hot(rank, LANES), ((1,), (1,))
@@ -186,10 +185,9 @@
                 packed[p * capacity : (p + 1) * capacity],
                 jnp.broadcast_to(ids[i : i + 1], (META, LANES)),
             )
-            target = near_hbm.at[pl.ds(i * block, block)] if i < half else far_hbms[i - half]
             departures.append(
                 pltpu.make_async_copy(
-                    send_ref.at[pl.ds(i * block, block)], target, out_sems.at[i]
+                    send_ref.at[pl.ds(i * block, block)], send_hbms[i], out_sems.at[i]
                 )
             )
             departures[-1].start()
@@ -471,18 +469,13 @@
     cell = far(cell.reshape(1, rows_dev))
     cell_place = far(cell_place.reshape(1, cells))
     if capacity == 64 and peers == 16:
-        half = peers // 2
-        distances = [8, 12, 9, 13, 10, 14, 11, 15]
-        *sends, near_send, route = call(
+        distances = DISTANCES
+        *sends, route = call(
             functools.partial(pack_split_kernel, peers, capacity, cells_dev, distances),
             (),
             [HBM] * 3,
-            [HBM] * (half + 1) + [VMEM],
-            [
-                *[pltpu.HBM((block, LANES), BF)] * half,
-                pltpu.HBM((half * block, LANES), BF),
-                shape_of((8, rows_dev), jnp.int32),
-            ],
+            [HBM] * peers + [VMEM],
+            [pltpu.HBM((block, LANES), BF)] * peers + [shape_of((8, rows_dev), jnp.int32)],
             scratch=[
                 pltpu.VMEM((1, rows_dev), jnp.int32),
                 pltpu.VMEM((1, cells), jnp.int32),
@@ -495,25 +488,25 @@
             moved=2 * (slots + 2 * rows_dev) * width,
         )(cell, cell_place, far(rows))
         got = []
-        window = 5
         for i, r in enumerate(distances):
             block_out = sends[i]
-            if i >= window:
-                block_out, got[i - window] = lax.optimization_barrier((block_out, got[i - window]))
-            got.append(lax.ppermute(block_out, "wide", [(p, p ^ r) for p in range(peers)]))
-        halves = [list(range(half)), list(range(half, peers))]
-        got_near = lax.all_to_all(
-            near_send.reshape(half, block, LANES), "wide", split_axis=0, concat_axis=0,
-            tiled=False, axis_index_groups=halves,
-        ).reshape(half * block, LANES)
+            if i >= WINDOW:
+                block_out, got[i - WINDOW] = lax.optimization_barrier((block_out, got[i - WINDOW]))
+            if r:
+                block_out = lax.ppermute(block_out, "wide", [(p, p ^ r) for p in range(peers)])
+            got.append(block_out)
         tables = (coarse, norm, fine_flat)
-        scored = [score([got_near], [half], capacity, *tables)]
-        scored.append(score(got[:4], [1] * 4, capacity, *tables))
-        known = (None, distances[:4])
-        errors = [x[0] for x in scored]
-        scored.append(
-            score(got[4:], [1] * 4, capacity, *tables, distances[4:], known, errors, peers)
-        )
+        scored = []
+        for first in range(0, peers, 4):
+            some = got[first : first + 4]
+            if first + 4 < peers:
+                scored.append(score(some, [1] * 4, capacity, *tables))
+            else:
+                known = tuple(distances[i : i + 4] for i in range(0, first, 4))
+                errors = [x[0] for x in scored]
+                scored.append(
+                    score(some, [1] * 4, capacity, *tables, distances[first:], known, errors, peers)
+                )
     else:
         send, route = call(
             functools.partial(pack_kernel, peers, capacity, cells_dev),

time: 67.9 us -> 64.8 us (0.954)
  starting transfers between devices: 30.8 us -> 28 us
  other arithmetic: 0.68 us -> 2.56 us
  Pallas kernels: 25 us -> 23.7 us
  waiting for transfers between devices: 7.6 us -> 6.86 us
    all_to_all x1 -> x0, starting transfers between devices: 5.24 us -> none  [shards(): lax.all_to_all(near_send.reshape(half, block, LANES), 'wide', split_axis=...]
    ppermute x8 -> x15, starting transfers between devices: 18.9 us -> 23.8 us  [shards(): lax.ppermute(block_out, 'wide', [(p, p ^ r) for p in range(peers)])]
    all_to_all x1, starting transfers between devices: 6.73 us -> 4.24 us  [shards(): lax.all_to_all(scored[-1][0], 'wide', split_axis=0, concat_axis=0, tiled=...]
    reduce_sum x1, other arithmetic: 0.68 us -> 2.56 us  [shards(): norm = jnp.sum(fine_wide * fine_wide, axis=-1)]
    pallas_call x3 -> x4, Pallas kernels: 9.5 us -> 7.68 us  [score(): call(functools.partial(score_kernel, blocks, capacity, far_of, known), ()...]
    ppermute x8 -> x15, waiting for transfers between devices: 7.59 us -> 6.85 us  [shards(): lax.ppermute(block_out, 'wide', [(p, p ^ r) for p in range(peers)])]
    unnamed x10 -> x18, local copies, waits for them, and re-layouts: 1.75 us -> 1.77 us
  transfers between devices with their start and end apart: 10 -> 16, of which waited for: 3 -> 2; matrix products, arithmetic and copies ran while one was open for 2% -> 5% of each run, Pallas kernels for 26% -> 27%
where the time goes in v3:
time: 64.8 us; the launch traced here: 64.5 us
  starting transfers between devices  28 us (43%)
  Pallas kernels  23.7 us (37%)
  waiting for transfers between devices  6.86 us (11%)
  local copies, waits for them, and re-layouts  2.57 us (4%)
  other arithmetic  2.56 us (4%)
  between operations  0.81 us (1%)
    ppermute x15, starting transfers between devices, shards(): lax.ppermute(block_out, 'wide', [(p, p ^ r) for p in range(peers)])  23.8 us
    pallas_call x1, Pallas kernels, update(): call(functools.partial(update_kernel, sets), (), [VMEM] * (1 + 2 * sets)...  9.15 us
    pallas_call x4, Pallas kernels, score(): call(functools.partial(score_kernel, blocks, capacity, far_of, known), ()...  7.68 us
    ppermute x15, waiting for transfers between devices, shards(): lax.ppermute(block_out, 'wide', [(p, p ^ r) for p in range(peers)])  6.85 us
    all_to_all x1, starting transfers between devices, shards(): lax.all_to_all(scored[-1][0], 'wide', split_axis=0, concat_axis=0, tiled=...  4.24 us
    pallas_call x1, Pallas kernels, shards(): call(functools.partial(pack_split_kernel, peers, capacity, cells_dev, dis...  3.25 us
    pallas_call x1, Pallas kernels, shards(): call(seed_kernel, (), [VMEM, VMEM], HBM, pltpu.HBM((fine_all, width), BF)...  2.8 us
    reduce_sum x1, other arithmetic, shards(): norm = jnp.sum(fine_wide * fine_wide, axis=-1)  2.56 us
  transfers between devices with their start and end apart: 16, of which 2 were waited for; matrix products, arithmetic and copies ran while one was open for 5% of the time, Pallas kernels for 27%

profile of v3, /device:TPU:0, one launch (start us, length us, event | category | flops | bytes accessed | tf_op | source)
XLA Modules:
  0.0 64.5 jit_solution(7145598673326531812)
XLA Ops:
  0.7 3.2 %shard_map.85 = (bf16[400,128]{1,0:T(8,128)(2,1)}, bf16[400,128]{1,0:T(8,128)(2,1)}, bf16[400,128]{1,0:T(8,128)(2,1)}, bf16[400,128]{1,0:T(8,128)(2,1)}, bf16[40...) custom-call(s32[1,512]{1,0:T(1,128)} %bitcast.10, ...), custom_call_target="tpu_custom_call" | custom-call | flops 805306368 | bytes 3145728 | tf_op jit(solution)/shard_map/pallas_call | solution.py:473
  3.9 4.1 %collective-permute-start = (bf16[400,128]{1,0:T(8,128)(2,1)}, bf16[400,128]{1,0:T(8,128)(2,1)S(1)}, u32[]{:S(2)}, u32[]{:S(2)}) collective-permute-start(bf16[400,128]{1,0:T(8,128)(2,1)} %get-tuple-element.61), channel_id=1, source_target_pairs={{0,8},{1,9},{2,10},{3,11},{4,12},{5,13},{6,14},{7,15},{8,0},{9,1},... | collective-permute-start | bytes 307208 | tf_op jit(solution)/shard_map/ppermute | solution.py:496
  8.0 1.3 %collective-permute-start.6 = (bf16[400,128]{1,0:T(8,128)(2,1)}, bf16[400,128]{1,0:T(8,128)(2,1)}, u32[]{:S(2)}, u32[]{:S(2)}) collective-permute-start(bf16[400,128]{1,0:T(8,128)(2,1)} %get-tuple-element.71), channel_id=1, source_target_pairs={{0,12},{1,13},{2,14},{3,15},{4,8},{5,9},{6,10},{7,11},{8,4},{9,5},... | collective-permute-start | bytes 307208 | tf_op jit(solution)/shard_map/ppermute | solution.py:496
  9.4 1.5 %collective-permute-start.9 = (bf16[400,128]{1,0:T(8,128)(2,1)}, bf16[400,128]{1,0:T(8,128)(2,1)}, u32[]{:S(2)}, u32[]{:S(2)}) collective-permute-start(bf16[400,128]{1,0:T(8,128)(2,1)} %get-tuple-element.76), channel_id=1, source_target_pairs={{0,2},{1,3},{2,0},{3,1},{4,6},{5,7},{6,4},{7,5},{8,10},{9,11},{10,... | collective-permute-start | bytes 307208 | tf_op jit(solution)/shard_map/ppermute | solution.py:496
  10.9 1.2 %collective-permute-start.11 = (bf16[400,128]{1,0:T(8,128)(2,1)}, bf16[400,128]{1,0:T(8,128)(2,1)S(1)}, u32[]{:S(2)}, u32[]{:S(2)}) collective-permute-start(bf16[400,128]{1,0:T(8,128)(2,1)} %get-tuple-element.85), channel_id=1, source_target_pairs={{0,9},{1,8},{2,11},{3,10},{4,13},{5,12},{6,15},{7,14},{8,1},{9,0},... | collective-permute-start | bytes 307208 | tf_op jit(solution)/shard_map/ppermute | solution.py:496
  12.1 2.6 %multiply_reduce_fusion.norm_ref = f32[32,64]{1,0:T(8,128)S(1)} fusion(bf16[32,64,768]{2,1,0:T(8,128)(2,1)} %param.10), kind=kLoop, calls=%fused_computation | loop fusion | flops 4716544 | bytes 3153920 | tf_op jit(solution)/shard_map/reduce_sum | solution.py:457
  14.7 0.8 %reshape.28.reseed_ref = s32[1,2048]{1,0:T(1,128)S(1)} reshape(s32[32,64]{1,0:T(8,128)} %param.11) | data formatting | bytes 16384 | tf_op jit(solution)/shard_map/reshape | solution.py:468
  15.5 3.1 %collective-permute-done.refs_0_ = bf16[400,128]{1,0:T(8,128)(2,1)S(1)} collective-permute-done((bf16[400,128]{1,0:T(8,128)(2,1)}, bf16[400,128]{1,0:T(8,128)(2,1)S(1)}, u32[]{:S(2)}, u32[]{:S(2)}) %collective-permute-start) | collective-permute-done | bytes 102432 | tf_op jit(solution)/shard_map/ppermute | solution.py:496
  18.5 4.0 %collective-permute-start.1 = (bf16[400,128]{1,0:T(8,128)(2,1)}, bf16[400,128]{1,0:T(8,128)(2,1)S(1)}, u32[]{:S(2)}, u32[]{:S(2)}) collective-permute-start(bf16[400,128]{1,0:T(8,128)(2,1)} %get-tuple-element.62), channel_id=1, source_target_pairs={{0,13},{1,12},{2,15},{3,14},{4,9},{5,8},{6,11},{7,10},{8,5},{9,4},... | collective-permute-start | bytes 307208 | tf_op jit(solution)/shard_map/ppermute | solution.py:496
  22.5 1.6 %collective-permute-start.7 = (bf16[400,128]{1,0:T(8,128)(2,1)}, bf16[400,128]{1,0:T(8,128)(2,1)S(1)}, u32[]{:S(2)}, u32[]{:S(2)}) collective-permute-start(bf16[400,128]{1,0:T(8,128)(2,1)} %get-tuple-element.72), channel_id=1, source_target_pairs={{0,10},{1,11},{2,8},{3,9},{4,14},{5,15},{6,12},{7,13},{8,2},{9,3},... | collective-permute-start | bytes 307208 | tf_op jit(solution)/shard_map/ppermute | solution.py:496
  24.7 1.1 %copy-done.3 = bf16[512,768]{1,0:T(8,128)(2,1)S(1)} copy-done((bf16[512,768]{1,0:T(8,128)(2,1)S(1)}, bf16[512,768]{1,0:T(8,128)(2,1)}, u32[]{:S(2)}) %copy-start.3) | copy-done | bytes 786456
  25.8 2.8 %shard_map.91.refs_12_ = bf16[2048,768]{1,0:T(8,128)(2,1)} custom-call(s32[1,2048]{1,0:T(1,128)S(1)} %reshape.28.reseed_ref, bf16[512,768]{1,0:T(8,128)(2,1)S(1)} %copy-done.3), custom_call_target="tpu_custom_call" | custom-call | flops 1610612736 | bytes 3932160 | tf_op jit(solution)/shard_map/pallas_call | solution.py:459
  28.6 3.2 %collective-permute-start.13 = (bf16[400,128]{1,0:T(8,128)(2,1)}, bf16[400,128]{1,0:T(8,128)(2,1)S(1)}, u32[]{:S(2)}, u32[]{:S(2)}) collective-permute-start(bf16[400,128]{1,0:T(8,128)(2,1)} %get-tuple-element.95), channel_id=1, source_target_pairs={{0,14},{1,15},{2,12},{3,13},{4,10},{5,11},{6,8},{7,9},{8,6},{9,7},... | collective-permute-start | bytes 307208 | tf_op jit(solution)/shard_map/ppermute | solution.py:496
  31.9 2.5 %shard_map.86 = (f32[4,1,128]{2,1,0:T(1,128)S(1)}, bf16[64,256]{1,0:T(8,128)(2,1)S(1)}, s32[1,256]{1,0:T(1,128)S(1)}, bf16[256,768]{1,0:T(8,128)(2,1)}) custom-call(bf16[32,768]{1,0:T(8,128)(2,1)S(1)} %copy-done.1, f32[32,64]{1,0:T(8,128)S(1)} %multiply_reduce_fusion.norm_ref, bf16[2048,768]{1,0:T(8,128)(2,1)S(1)} %bitcast.5, ...), custom_call_target="tpu_custom_call" | custom-call | flops 805306368 | bytes 3932160 | tf_op jit(solution)/shard_map/pallas_call | solution.py:397
  34.4 0.6 copy-done.4
  35.0 2.3 %collective-permute-start.2 = (bf16[400,128]{1,0:T(8,128)(2,1)S(1)}, bf16[400,128]{1,0:T(8,128)(2,1)S(1)}, u32[]{:S(2)}, u32[]{:S(2)}) collective-permute-start(bf16[400,128]{1,0:T(8,128)(2,1)S(1)} %copy-done.8), channel_id=1, source_target_pairs={{0,11},{1,10},{2,9},{3,8},{4,15},{5,14},{6,13},{7,12},{8,3},{9,2},... | collective-permute-start | bytes 307208 | tf_op jit(solution)/shard_map/ppermute | solution.py:496
  37.9 3.3 %collective-permute-start.8 = (bf16[400,128]{1,0:T(8,128)(2,1)S(1)}, bf16[400,128]{1,0:T(8,128)(2,1)S(1)}, u32[]{:S(2)}, u32[]{:S(2)}) collective-permute-start(bf16[400,128]{1,0:T(8,128)(2,1)S(1)} %copy-done.6), channel_id=1, source_target_pairs={{0,15},{1,14},{2,13},{3,12},{4,11},{5,10},{6,9},{7,8},{8,7},{9,6},... | collective-permute-start | bytes 307208 | tf_op jit(solution)/shard_map/ppermute | solution.py:496
  41.2 1.5 %shard_map.87 = (f32[4,1,128]{2,1,0:T(1,128)S(1)}, bf16[64,256]{1,0:T(8,128)(2,1)S(1)}, s32[1,256]{1,0:T(1,128)S(1)}, bf16[256,768]{1,0:T(8,128)(2,1)}) custom-call(bf16[32,768]{1,0:T(8,128)(2,1)S(1)} %copy-done.1, f32[32,64]{1,0:T(8,128)S(1)} %multiply_reduce_fusion.norm_ref, bf16[2048,768]{1,0:T(8,128)(2,1)S(1)} %bitcast.6, ...), custom_call_target="tpu_custom_call" | custom-call | flops 805306368 | bytes 3932160 | tf_op jit(solution)/shard_map/pallas_call | solution.py:397
  42.8 1.5 %shard_map.88 = (f32[4,1,128]{2,1,0:T(1,128)S(1)}, bf16[64,256]{1,0:T(8,128)(2,1)S(1)}, s32[1,256]{1,0:T(1,128)S(1)}, bf16[256,768]{1,0:T(8,128)(2,1)}) custom-call(bf16[32,768]{1,0:T(8,128)(2,1)S(1)} %copy-done.1, f32[32,64]{1,0:T(8,128)S(1)} %multiply_reduce_fusion.norm_ref, bf16[2048,768]{1,0:T(8,128)(2,1)S(1)} %bitcast.7, ...), custom_call_target="tpu_custom_call" | custom-call | flops 805306368 | bytes 3932160 | tf_op jit(solution)/shard_map/pallas_call | solution.py:397
  44.4 3.8 %collective-permute-done.8.refs_2_ = bf16[400,128]{1,0:T(8,128)(2,1)S(1)} collective-permute-done((bf16[400,128]{1,0:T(8,128)(2,1)S(1)}, bf16[400,128]{1,0:T(8,128)(2,1)S(1)}, u32[]{:S(2)}, u32[]{:S(2)}) %collective-permute-start.8) | collective-permute-done | bytes 102432 | tf_op jit(solution)/shard_map/ppermute | solution.py:496
  48.1 2.1 %shard_map.89 = (f32[16,1,128]{2,1,0:T(1,128)}, bf16[64,256]{1,0:T(8,128)(2,1)S(1)}, s32[1,256]{1,0:T(1,128)S(1)}, bf16[256,768]{1,0:T(8,128)(2,1)}) custom-call(bf16[32,768]{1,0:T(8,128)(2,1)S(1)} %copy-done.1, f32[32,64]{1,0:T(8,128)S(1)} %multiply_reduce_fusion.norm_ref, bf16[2048,768]{1,0:T(8,128)(2,1)S(1)} %bitcast.8, ...), custom_call_target="tpu_custom_call" | custom-call | flops 805306368 | bytes 3932160 | tf_op jit(solution)/shard_map/pallas_call | solution.py:397
  50.3 4.2 %all-to-all-start = ((f32[16,1,128]{2,1,0:T(1,128)}), f32[16,1,128]{2,1,0:T(1,128)S(1)}, u32[]{:S(2)}, u32[]{:S(2)}) async-start(f32[16,1,128]{2,1,0:T(1,128)} %get-tuple-element.98), calls=%async_computation | async-start | bytes 16384 | tf_op jit(solution)/shard_map/all_to_all | solution.py:533
  54.5 9.1 %shard_map.92 = (f32[32,768]{1,0:T(8,128)}, f32[2048,768]{1,0:T(8,128)}) custom-call(bf16[32,768]{1,0:T(8,128)(2,1)S(1)} %copy-done.1, s32[1,256]{1,0:T(1,128)S(1)} %get-tuple-element.99.refs_0_, s32[1,256]{1,0:T(1,128)S(1)} %get-tuple-element.100.refs_1_, s32[1,256]{1,0:T(1,128)S(1)} %get-tuple-element.101.refs_2_, ...), custom_call_target="tpu_custom_call" | custom-call | flops 3221225472 | bytes 11010048 | tf_op jit(solution)/shard_map/pallas_call | solution.py:424
  63.7 0.8 %shard_map.90 = f32[1,512]{1,0:T(1,128)} custom-call(s32[8,512]{1,0:T(8,128)S(1)} %get-tuple-element.58.route_ref, f32[16,1,128]{2,1,0:T(1,128)S(1)} %all-to-all-done.error_ref), custom_call_target="tpu_custom_call" | custom-call | bytes 24576 | tf_op jit(solution)/shard_map/pallas_call | solution.py:535
  (36 shorter events, 1.3 us)
Async XLA Ops:
  0.6 31.3 %copy-start = (bf16[32,64,768]{2,1,0:T(8,128)(2,1)S(1)}, bf16[32,64,768]{2,1,0:T(8,128)(2,1)}, u32[]{:S(2)}) copy-start(bf16[32,64,768]{2,1,0:T(8,128)(2,1)} %param.10) | copy-start | bytes 9437188
  0.6 31.3 %copy-start.1 = (bf16[32,768]{1,0:T(8,128)(2,1)S(1)}, bf16[32,768]{1,0:T(8,128)(2,1)}, u32[]{:S(2)}) copy-start(bf16[32,768]{1,0:T(8,128)(2,1)} %coarse_ref.9) | copy-start | bytes 147460
  3.9 14.6 %collective-permute-start = (bf16[400,128]{1,0:T(8,128)(2,1)}, bf16[400,128]{1,0:T(8,128)(2,1)S(1)}, u32[]{:S(2)}, u32[]{:S(2)}) collective-permute-start(bf16[400,128]{1,0:T(8,128)(2,1)} %get-tuple-element.61), channel_id=1, source_target_pairs={{0,8},{1,9},{2,10},{3,11},{4,12},{5,13},{6,14},{7,15},{8,0},{9,1},... | collective-permute-start | bytes 307208 | tf_op jit(solution)/shard_map/ppermute | solution.py:496
  8.0 10.5 %collective-permute-start.3 = (bf16[400,128]{1,0:T(8,128)(2,1)}, bf16[400,128]{1,0:T(8,128)(2,1)S(1)}, u32[]{:S(2)}, u32[]{:S(2)}) collective-permute-start(bf16[400,128]{1,0:T(8,128)(2,1)} %get-tuple-element.66), channel_id=1, source_target_pairs={{0,1},{1,0},{2,3},{3,2},{4,5},{5,4},{6,7},{7,6},{8,9},{9,8},{10,11... | collective-permute-start | bytes 307208 | tf_op jit(solution)/shard_map/ppermute | solution.py:496
  8.0 14.5 %collective-permute-start.6 = (bf16[400,128]{1,0:T(8,128)(2,1)}, bf16[400,128]{1,0:T(8,128)(2,1)}, u32[]{:S(2)}, u32[]{:S(2)}) collective-permute-start(bf16[400,128]{1,0:T(8,128)(2,1)} %get-tuple-element.71), channel_id=1, source_target_pairs={{0,12},{1,13},{2,14},{3,15},{4,8},{5,9},{6,10},{7,11},{8,4},{9,5},... | collective-permute-start | bytes 307208 | tf_op jit(solution)/shard_map/ppermute | solution.py:496
  9.4 13.2 %collective-permute-start.9 = (bf16[400,128]{1,0:T(8,128)(2,1)}, bf16[400,128]{1,0:T(8,128)(2,1)}, u32[]{:S(2)}, u32[]{:S(2)}) collective-permute-start(bf16[400,128]{1,0:T(8,128)(2,1)} %get-tuple-element.76), channel_id=1, source_target_pairs={{0,2},{1,3},{2,0},{3,1},{4,6},{5,7},{6,4},{7,5},{8,10},{9,11},{10,... | collective-permute-start | bytes 307208 | tf_op jit(solution)/shard_map/ppermute | solution.py:496
  10.9 13.3 %collective-permute-start.11 = (bf16[400,128]{1,0:T(8,128)(2,1)}, bf16[400,128]{1,0:T(8,128)(2,1)S(1)}, u32[]{:S(2)}, u32[]{:S(2)}) collective-permute-start(bf16[400,128]{1,0:T(8,128)(2,1)} %get-tuple-element.85), channel_id=1, source_target_pairs={{0,9},{1,8},{2,11},{3,10},{4,13},{5,12},{6,15},{7,14},{8,1},{9,0},... | collective-permute-start | bytes 307208 | tf_op jit(solution)/shard_map/ppermute | solution.py:496
  18.5 10.1 %collective-permute-start.12 = (bf16[400,128]{1,0:T(8,128)(2,1)}, bf16[400,128]{1,0:T(8,128)(2,1)S(1)}, u32[]{:S(2)}, u32[]{:S(2)}) collective-permute-start(bf16[400,128]{1,0:T(8,128)(2,1)} %get-tuple-element.88), channel_id=1, source_target_pairs={{0,3},{1,2},{2,1},{3,0},{4,7},{5,6},{6,5},{7,4},{8,11},{9,10},{10,... | collective-permute-start | bytes 307208 | tf_op jit(solution)/shard_map/ppermute | solution.py:496
  18.5 13.3 %collective-permute-start.1 = (bf16[400,128]{1,0:T(8,128)(2,1)}, bf16[400,128]{1,0:T(8,128)(2,1)S(1)}, u32[]{:S(2)}, u32[]{:S(2)}) collective-permute-start(bf16[400,128]{1,0:T(8,128)(2,1)} %get-tuple-element.62), channel_id=1, source_target_pairs={{0,13},{1,12},{2,15},{3,14},{4,9},{5,8},{6,11},{7,10},{8,5},{9,4},... | collective-permute-start | bytes 307208 | tf_op jit(solution)/shard_map/ppermute | solution.py:496
  22.5 12.5 %collective-permute-start.4 = (bf16[400,128]{1,0:T(8,128)(2,1)}, bf16[400,128]{1,0:T(8,128)(2,1)S(1)}, u32[]{:S(2)}, u32[]{:S(2)}) collective-permute-start(bf16[400,128]{1,0:T(8,128)(2,1)} %get-tuple-element.67), channel_id=1, source_target_pairs={{0,4},{1,5},{2,6},{3,7},{4,0},{5,1},{6,2},{7,3},{8,12},{9,13},{10,... | collective-permute-start | bytes 307208 | tf_op jit(solution)/shard_map/ppermute | solution.py:496
  22.5 14.8 %collective-permute-start.7 = (bf16[400,128]{1,0:T(8,128)(2,1)}, bf16[400,128]{1,0:T(8,128)(2,1)S(1)}, u32[]{:S(2)}, u32[]{:S(2)}) collective-permute-start(bf16[400,128]{1,0:T(8,128)(2,1)} %get-tuple-element.72), channel_id=1, source_target_pairs={{0,10},{1,11},{2,8},{3,9},{4,14},{5,15},{6,12},{7,13},{8,2},{9,3},... | collective-permute-start | bytes 307208 | tf_op jit(solution)/shard_map/ppermute | solution.py:496
  24.1 13.8 %collective-permute-start.10 = (bf16[400,128]{1,0:T(8,128)(2,1)}, bf16[400,128]{1,0:T(8,128)(2,1)S(1)}, u32[]{:S(2)}, u32[]{:S(2)}) collective-permute-start(bf16[400,128]{1,0:T(8,128)(2,1)} %get-tuple-element.77), channel_id=1, source_target_pairs={{0,5},{1,4},{2,7},{3,6},{4,1},{5,0},{6,3},{7,2},{8,13},{9,12},{10,... | collective-permute-start | bytes 307208 | tf_op jit(solution)/shard_map/ppermute | solution.py:496
  24.7 1.1 %copy-start.3 = (bf16[512,768]{1,0:T(8,128)(2,1)S(1)}, bf16[512,768]{1,0:T(8,128)(2,1)}, u32[]{:S(2)}) copy-start(bf16[512,768]{1,0:T(8,128)(2,1)} %rows_ref.1) | copy-start | bytes 2359300
  25.8 9.3 %copy-start.8 = (bf16[400,128]{1,0:T(8,128)(2,1)S(1)}, bf16[400,128]{1,0:T(8,128)(2,1)}, u32[]{:S(2)}) copy-start(bf16[400,128]{1,0:T(8,128)(2,1)} %get-tuple-element.63) | copy-start | bytes 307204
  25.8 11.5 %copy-start.7 = (bf16[400,128]{1,0:T(8,128)(2,1)S(1)}, bf16[400,128]{1,0:T(8,128)(2,1)}, u32[]{:S(2)}) copy-start(bf16[400,128]{1,0:T(8,128)(2,1)} %get-tuple-element.68) | copy-start | bytes 307204
  25.8 12.1 %copy-start.6 = (bf16[400,128]{1,0:T(8,128)(2,1)S(1)}, bf16[400,128]{1,0:T(8,128)(2,1)}, u32[]{:S(2)}) copy-start(bf16[400,128]{1,0:T(8,128)(2,1)} %get-tuple-element.73) | copy-start | bytes 307204
  28.6 19.5 %copy-start.2 = (bf16[400,128]{1,0:T(8,128)(2,1)S(1)}, bf16[400,128]{1,0:T(8,128)(2,1)}, u32[]{:S(2)}) copy-start(bf16[400,128]{1,0:T(8,128)(2,1)} %get-tuple-element.78.refs_3_) | copy-start | bytes 307204
  28.6 14.2 %collective-permute-start.13 = (bf16[400,128]{1,0:T(8,128)(2,1)}, bf16[400,128]{1,0:T(8,128)(2,1)S(1)}, u32[]{:S(2)}, u32[]{:S(2)}) collective-permute-start(bf16[400,128]{1,0:T(8,128)(2,1)} %get-tuple-element.95), channel_id=1, source_target_pairs={{0,14},{1,15},{2,12},{3,13},{4,10},{5,11},{6,8},{7,9},{8,6},{9,7},... | collective-permute-start | bytes 307208 | tf_op jit(solution)/shard_map/ppermute | solution.py:496
  31.9 10.9 %collective-permute-start.14 = (bf16[400,128]{1,0:T(8,128)(2,1)}, bf16[400,128]{1,0:T(8,128)(2,1)S(1)}, u32[]{:S(2)}, u32[]{:S(2)}) collective-permute-start(bf16[400,128]{1,0:T(8,128)(2,1)} %get-tuple-element.96), channel_id=1, source_target_pairs={{0,6},{1,7},{2,4},{3,5},{4,2},{5,3},{6,0},{7,1},{8,14},{9,15},{10,... | collective-permute-start | bytes 307208 | tf_op jit(solution)/shard_map/ppermute | solution.py:496
  35.0 19.5 %copy-start.5 = (bf16[64,256]{1,0:T(8,128)(2,1)S(1)}, bf16[64,256]{1,0:T(8,128)(2,1)}, u32[]{:S(2)}) copy-start(bf16[64,256]{1,0:T(8,128)(2,1)} %copy-done.4) | copy-start | bytes 98308
  35.0 9.3 %collective-permute-start.2 = (bf16[400,128]{1,0:T(8,128)(2,1)S(1)}, bf16[400,128]{1,0:T(8,128)(2,1)S(1)}, u32[]{:S(2)}, u32[]{:S(2)}) collective-permute-start(bf16[400,128]{1,0:T(8,128)(2,1)S(1)} %copy-done.8), channel_id=1, source_target_pairs={{0,11},{1,10},{2,9},{3,8},{4,15},{5,14},{6,13},{7,12},{8,3},{9,2},... | collective-permute-start | bytes 307208 | tf_op jit(solution)/shard_map/ppermute | solution.py:496
  37.3 7.1 %collective-permute-start.5 = (bf16[400,128]{1,0:T(8,128)(2,1)S(1)}, bf16[400,128]{1,0:T(8,128)(2,1)S(1)}, u32[]{:S(2)}, u32[]{:S(2)}) collective-permute-start(bf16[400,128]{1,0:T(8,128)(2,1)S(1)} %copy-done.7), channel_id=1, source_target_pairs={{0,7},{1,6},{2,5},{3,4},{4,3},{5,2},{6,1},{7,0},{8,15},{9,14},{10,... | collective-permute-start | bytes 307208 | tf_op jit(solution)/shard_map/ppermute | solution.py:496
  37.9 10.2 %collective-permute-start.8 = (bf16[400,128]{1,0:T(8,128)(2,1)S(1)}, bf16[400,128]{1,0:T(8,128)(2,1)S(1)}, u32[]{:S(2)}, u32[]{:S(2)}) collective-permute-start(bf16[400,128]{1,0:T(8,128)(2,1)S(1)} %copy-done.6), channel_id=1, source_target_pairs={{0,15},{1,14},{2,13},{3,12},{4,11},{5,10},{6,9},{7,8},{8,7},{9,6},... | collective-permute-start | bytes 307208 | tf_op jit(solution)/shard_map/ppermute | solution.py:496
  50.3 13.4 %all-to-all-start = ((f32[16,1,128]{2,1,0:T(1,128)}), f32[16,1,128]{2,1,0:T(1,128)S(1)}, u32[]{:S(2)}, u32[]{:S(2)}) async-start(f32[16,1,128]{2,1,0:T(1,128)} %get-tuple-element.98), calls=%async_computation | async-start | bytes 16384 | tf_op jit(solution)/shard_map/all_to_all | solution.py:533
  (1 other events, 0.6 us)

commit v4 on v3

--- a/solution.py
+++ b/solution.py
@@ -10,8 +10,9 @@
 TEMP = 16
 LANES = 128
 META = 16
-DISTANCES = [8, 1, 12, 2, 9, 3, 13, 4, 10, 5, 14, 6, 11, 7, 15, 0]
+DISTANCES = [8, 7, 12, 6, 10, 5, 14, 4, 9, 3, 13, 2, 11, 1, 15, 0]
 WINDOW = 6
+SIZES = (4, 4, 6, 2)
 VMEM_LIMIT = 24 * 1024 * 1024
 BF = jnp.bfloat16
 F32 = jnp.float32
@@ -497,15 +498,19 @@
             got.append(block_out)
         tables = (coarse, norm, fine_flat)
         scored = []
-        for first in range(0, peers, 4):
-            some = got[first : first + 4]
-            if first + 4 < peers:
-                scored.append(score(some, [1] * 4, capacity, *tables))
+        for size in SIZES:
+            first = sum(SIZES[: len(scored)])
+            some = got[first : first + size]
+            if first + size < peers:
+                scored.append(score(some, [1] * size, capacity, *tables))
             else:
-                known = tuple(distances[i : i + 4] for i in range(0, first, 4))
+                ends = [sum(SIZES[: i + 1]) for i in range(len(scored))]
+                known = tuple(distances[e - n : e] for e, n in zip(ends, SIZES))
                 errors = [x[0] for x in scored]
                 scored.append(
-                    score(some, [1] * 4, capacity, *tables, distances[first:], known, errors, peers)
+                    score(
+                        some, [1] * size, capacity, *tables, distances[first:], known, errors, peers
+                    )
                 )
     else:
         send, route = call(

time: 64.8 us -> 61.7 us (0.952)
  waiting for transfers between devices: 6.86 us -> 3.64 us
  Pallas kernels: 23.7 us -> 24.6 us
  starting transfers between devices: 28 us -> 27.3 us
    ppermute x15, waiting for transfers between devices: 6.85 us -> 3.64 us  [shards(): lax.ppermute(block_out, 'wide', [(p, p ^ r) for p in range(peers)])]
    pallas_call x4, Pallas kernels: 7.68 us -> 8.61 us  [score(): call(functools.partial(score_kernel, blocks, capacity, far_of, known), ()...]
    unnamed x18 -> x14, local copies, waits for them, and re-layouts: 1.77 us -> 1.76 us
  transfers between devices with their start and end apart: 16 -> 16, of which waited for: 2 -> 4; matrix products, arithmetic and copies ran while one was open for 5% -> 5% of each run, Pallas kernels for 27% -> 30%
where the time goes in v4:
time: 61.7 us; the launch traced here: 61.4 us
  starting transfers between devices  27.3 us (44%)
  Pallas kernels  24.6 us (40%)
  waiting for transfers between devices  3.64 us (6%)
  local copies, waits for them, and re-layouts  2.56 us (4%)
  other arithmetic  2.56 us (4%)
  between operations  0.79 us (1%)
    ppermute x15, starting transfers between devices, shards(): lax.ppermute(block_out, 'wide', [(p, p ^ r) for p in range(peers)])  23.6 us
    pallas_call x1, Pallas kernels, update(): call(functools.partial(update_kernel, sets), (), [VMEM] * (1 + 2 * sets)...  9.13 us
    pallas_call x4, Pallas kernels, score(): call(functools.partial(score_kernel, blocks, capacity, far_of, known), ()...  8.61 us
    ppermute x15, waiting for transfers between devices, shards(): lax.ppermute(block_out, 'wide', [(p, p ^ r) for p in range(peers)])  3.64 us
    all_to_all x1, starting transfers between devices, shards(): lax.all_to_all(scored[-1][0], 'wide', split_axis=0, concat_axis=0, tiled=...  3.63 us
    pallas_call x1, Pallas kernels, shards(): call(functools.partial(pack_split_kernel, peers, capacity, cells_dev, dis...  3.26 us
    pallas_call x1, Pallas kernels, shards(): call(seed_kernel, (), [VMEM, VMEM], HBM, pltpu.HBM((fine_all, width), BF)...  2.83 us
    reduce_sum x1, other arithmetic, shards(): norm = jnp.sum(fine_wide * fine_wide, axis=-1)  2.56 us
  transfers between devices with their start and end apart: 16, of which 4 were waited for; matrix products, arithmetic and copies ran while one was open for 5% of the time, Pallas kernels for 30%

profile of v4, /device:TPU:0, one launch (start us, length us, event | category | flops | bytes accessed | tf_op | source)
XLA Modules:
  0.0 61.4 jit_solution(5721777935646408446)
XLA Ops:
  0.7 3.3 %shard_map.85 = (bf16[400,128]{1,0:T(8,128)(2,1)}, bf16[400,128]{1,0:T(8,128)(2,1)}, bf16[400,128]{1,0:T(8,128)(2,1)}, bf16[400,128]{1,0:T(8,128)(2,1)}, bf16[40...) custom-call(s32[1,512]{1,0:T(1,128)} %bitcast.10, ...), custom_call_target="tpu_custom_call" | custom-call | flops 805306368 | bytes 3145728 | tf_op jit(solution)/shard_map/pallas_call | solution.py:474
  3.9 5.1 %collective-permute-start = (bf16[400,128]{1,0:T(8,128)(2,1)}, bf16[400,128]{1,0:T(8,128)(2,1)S(1)}, u32[]{:S(2)}, u32[]{:S(2)}) collective-permute-start(bf16[400,128]{1,0:T(8,128)(2,1)} %get-tuple-element.61), channel_id=1, source_target_pairs={{0,12},{1,13},{2,14},{3,15},{4,8},{5,9},{6,10},{7,11},{8,4},{9,5},... | collective-permute-start | bytes 307208 | tf_op jit(solution)/shard_map/ppermute | solution.py:497
  9.5 1.2 %collective-permute-start.5 = (bf16[400,128]{1,0:T(8,128)(2,1)}, bf16[400,128]{1,0:T(8,128)(2,1)}, u32[]{:S(2)}, u32[]{:S(2)}) collective-permute-start(bf16[400,128]{1,0:T(8,128)(2,1)} %get-tuple-element.70), channel_id=1, source_target_pairs={{0,8},{1,9},{2,10},{3,11},{4,12},{5,13},{6,14},{7,15},{8,0},{9,1},... | collective-permute-start | bytes 307208 | tf_op jit(solution)/shard_map/ppermute | solution.py:497
  10.8 3.6 %collective-permute-start.7 = (bf16[400,128]{1,0:T(8,128)(2,1)}, bf16[400,128]{1,0:T(8,128)(2,1)S(1)}, u32[]{:S(2)}, u32[]{:S(2)}) collective-permute-start(bf16[400,128]{1,0:T(8,128)(2,1)} %get-tuple-element.79), channel_id=1, source_target_pairs={{0,10},{1,11},{2,8},{3,9},{4,14},{5,15},{6,12},{7,13},{8,2},{9,3},... | collective-permute-start | bytes 307208 | tf_op jit(solution)/shard_map/ppermute | solution.py:497
  14.4 2.6 %multiply_reduce_fusion.norm_ref = f32[32,64]{1,0:T(8,128)S(1)} fusion(bf16[32,64,768]{2,1,0:T(8,128)(2,1)} %param.10), kind=kLoop, calls=%fused_computation | loop fusion | flops 4716544 | bytes 3153920 | tf_op jit(solution)/shard_map/reduce_sum | solution.py:458
  17.0 0.8 %reshape.28.reseed_ref = s32[1,2048]{1,0:T(1,128)S(1)} reshape(s32[32,64]{1,0:T(8,128)} %param.11) | data formatting | bytes 16384 | tf_op jit(solution)/shard_map/reshape | solution.py:469
  19.6 4.7 %collective-permute-start.9 = (bf16[400,128]{1,0:T(8,128)(2,1)}, bf16[400,128]{1,0:T(8,128)(2,1)S(1)}, u32[]{:S(2)}, u32[]{:S(2)}) collective-permute-start(bf16[400,128]{1,0:T(8,128)(2,1)} %get-tuple-element.85), channel_id=1, source_target_pairs={{0,14},{1,15},{2,12},{3,13},{4,10},{5,11},{6,8},{7,9},{8,6},{9,7},... | collective-permute-start | bytes 307208 | tf_op jit(solution)/shard_map/ppermute | solution.py:497
  24.3 1.1 %copy-done.3 = bf16[512,768]{1,0:T(8,128)(2,1)S(1)} copy-done((bf16[512,768]{1,0:T(8,128)(2,1)S(1)}, bf16[512,768]{1,0:T(8,128)(2,1)}, u32[]{:S(2)}) %copy-start.3) | copy-done | bytes 786456
  25.4 2.8 %shard_map.91.refs_12_ = bf16[2048,768]{1,0:T(8,128)(2,1)} custom-call(s32[1,2048]{1,0:T(1,128)S(1)} %reshape.28.reseed_ref, bf16[512,768]{1,0:T(8,128)(2,1)S(1)} %copy-done.3), custom_call_target="tpu_custom_call" | custom-call | flops 1610612736 | bytes 3932160 | tf_op jit(solution)/shard_map/pallas_call | solution.py:460
  28.3 0.7 %collective-permute-start.11 = (bf16[400,128]{1,0:T(8,128)(2,1)}, bf16[400,128]{1,0:T(8,128)(2,1)S(1)}, u32[]{:S(2)}, u32[]{:S(2)}) collective-permute-start(bf16[400,128]{1,0:T(8,128)(2,1)} %get-tuple-element.93), channel_id=1, source_target_pairs={{0,13},{1,12},{2,15},{3,14},{4,9},{5,8},{6,11},{7,10},{8,5},{9,4},... | collective-permute-start | bytes 307208 | tf_op jit(solution)/shard_map/ppermute | solution.py:497
  28.9 1.3 %collective-permute-start.12 = (bf16[400,128]{1,0:T(8,128)(2,1)}, bf16[400,128]{1,0:T(8,128)(2,1)S(1)}, u32[]{:S(2)}, u32[]{:S(2)}) collective-permute-start(bf16[400,128]{1,0:T(8,128)(2,1)} %get-tuple-element.94), channel_id=1, source_target_pairs={{0,2},{1,3},{2,0},{3,1},{4,6},{5,7},{6,4},{7,5},{8,10},{9,11},{10,... | collective-permute-start | bytes 307208 | tf_op jit(solution)/shard_map/ppermute | solution.py:497
  30.2 0.9 %collective-permute-done.10.refs_3_ = bf16[400,128]{1,0:T(8,128)(2,1)S(1)} collective-permute-done((bf16[400,128]{1,0:T(8,128)(2,1)}, bf16[400,128]{1,0:T(8,128)(2,1)S(1)}, u32[]{:S(2)}, u32[]{:S(2)}) %collective-permute-start.10) | collective-permute-done | bytes 102432 | tf_op jit(solution)/shard_map/ppermute | solution.py:497
  31.1 3.1 %collective-permute-start.13 = (bf16[400,128]{1,0:T(8,128)(2,1)}, bf16[400,128]{1,0:T(8,128)(2,1)S(1)}, u32[]{:S(2)}, u32[]{:S(2)}) collective-permute-start(bf16[400,128]{1,0:T(8,128)(2,1)} %get-tuple-element.95), channel_id=1, source_target_pairs={{0,11},{1,10},{2,9},{3,8},{4,15},{5,14},{6,13},{7,12},{8,3},{9,2},... | collective-permute-start | bytes 307208 | tf_op jit(solution)/shard_map/ppermute | solution.py:497
  34.2 0.7 %collective-permute-start.14 = (bf16[400,128]{1,0:T(8,128)(2,1)}, bf16[400,128]{1,0:T(8,128)(2,1)S(1)}, u32[]{:S(2)}, u32[]{:S(2)}) collective-permute-start(bf16[400,128]{1,0:T(8,128)(2,1)} %get-tuple-element.96), channel_id=1, source_target_pairs={{0,1},{1,0},{2,3},{3,2},{4,5},{5,4},{6,7},{7,6},{8,9},{9,8},{10,11... | collective-permute-start | bytes 307208 | tf_op jit(solution)/shard_map/ppermute | solution.py:497
  34.9 2.5 %shard_map.86 = (f32[4,1,128]{2,1,0:T(1,128)S(1)}, bf16[64,256]{1,0:T(8,128)(2,1)S(1)}, s32[1,256]{1,0:T(1,128)S(1)}, bf16[256,768]{1,0:T(8,128)(2,1)}) custom-call(bf16[32,768]{1,0:T(8,128)(2,1)S(1)} %copy-done.1, f32[32,64]{1,0:T(8,128)S(1)} %multiply_reduce_fusion.norm_ref, bf16[2048,768]{1,0:T(8,128)(2,1)S(1)} %bitcast.5, ...), custom_call_target="tpu_custom_call" | custom-call | flops 805306368 | bytes 3932160 | tf_op jit(solution)/shard_map/pallas_call | solution.py:398
  37.4 0.6 copy-done.4
  38.0 1.3 %collective-permute-start.2 = (bf16[400,128]{1,0:T(8,128)(2,1)S(1)}, bf16[400,128]{1,0:T(8,128)(2,1)S(1)}, u32[]{:S(2)}, u32[]{:S(2)}) collective-permute-start(bf16[400,128]{1,0:T(8,128)(2,1)S(1)} %copy-done.6), channel_id=1, source_target_pairs={{0,15},{1,14},{2,13},{3,12},{4,11},{5,10},{6,9},{7,8},{8,7},{9,6},... | collective-permute-start | bytes 307208 | tf_op jit(solution)/shard_map/ppermute | solution.py:497
  39.3 1.5 %shard_map.87 = (f32[4,1,128]{2,1,0:T(1,128)S(1)}, bf16[64,256]{1,0:T(8,128)(2,1)S(1)}, s32[1,256]{1,0:T(1,128)S(1)}, bf16[256,768]{1,0:T(8,128)(2,1)}) custom-call(bf16[32,768]{1,0:T(8,128)(2,1)S(1)} %copy-done.1, f32[32,64]{1,0:T(8,128)S(1)} %multiply_reduce_fusion.norm_ref, bf16[2048,768]{1,0:T(8,128)(2,1)S(1)} %bitcast.6, ...), custom_call_target="tpu_custom_call" | custom-call | flops 805306368 | bytes 3932160 | tf_op jit(solution)/shard_map/pallas_call | solution.py:398
  41.3 2.6 %shard_map.88 = (f32[6,1,128]{2,1,0:T(1,128)S(1)}, bf16[64,384]{1,0:T(8,128)(2,1)S(1)}, s32[1,384]{1,0:T(1,128)S(1)}, bf16[384,768]{1,0:T(8,128)(2,1)}) custom-call(bf16[32,768]{1,0:T(8,128)(2,1)S(1)} %copy-done.1, f32[32,64]{1,0:T(8,128)S(1)} %multiply_reduce_fusion.norm_ref, bf16[2048,768]{1,0:T(8,128)(2,1)S(1)} %bitcast.7, ...), custom_call_target="tpu_custom_call" | custom-call | flops 1207959552 | bytes 4325376 | tf_op jit(solution)/shard_map/pallas_call | solution.py:398
  43.9 1.9 %collective-permute-done.2.refs_0_ = bf16[400,128]{1,0:T(8,128)(2,1)S(1)} collective-permute-done((bf16[400,128]{1,0:T(8,128)(2,1)S(1)}, bf16[400,128]{1,0:T(8,128)(2,1)S(1)}, u32[]{:S(2)}, u32[]{:S(2)}) %collective-permute-start.2) | collective-permute-done | bytes 102432 | tf_op jit(solution)/shard_map/ppermute | solution.py:497
  45.8 2.0 %shard_map.89 = (f32[16,1,128]{2,1,0:T(1,128)}, bf16[64,128]{1,0:T(8,128)(2,1)S(1)}, s32[1,128]{1,0:T(1,128)S(1)}, bf16[128,768]{1,0:T(8,128)(2,1)}) custom-call(bf16[32,768]{1,0:T(8,128)(2,1)S(1)} %copy-done.1, f32[32,64]{1,0:T(8,128)S(1)} %multiply_reduce_fusion.norm_ref, bf16[2048,768]{1,0:T(8,128)(2,1)S(1)} %bitcast.8, ...), custom_call_target="tpu_custom_call" | custom-call | flops 402653184 | bytes 3538944 | tf_op jit(solution)/shard_map/pallas_call | solution.py:398
  47.8 3.6 %all-to-all-start = ((f32[16,1,128]{2,1,0:T(1,128)}), f32[16,1,128]{2,1,0:T(1,128)S(1)}, u32[]{:S(2)}, u32[]{:S(2)}) async-start(f32[16,1,128]{2,1,0:T(1,128)} %get-tuple-element.98), calls=%async_computation | async-start | bytes 16384 | tf_op jit(solution)/shard_map/all_to_all | solution.py:538
  51.5 9.1 %shard_map.92 = (f32[32,768]{1,0:T(8,128)}, f32[2048,768]{1,0:T(8,128)}) custom-call(bf16[32,768]{1,0:T(8,128)(2,1)S(1)} %copy-done.1, s32[1,256]{1,0:T(1,128)S(1)} %get-tuple-element.99.refs_0_, s32[1,256]{1,0:T(1,128)S(1)} %get-tuple-element.100.refs_1_, s32[1,384]{1,0:T(1,128)S(1)} %get-tuple-element.101.refs_2_, ...), custom_call_target="tpu_custom_call" | custom-call | flops 3221225472 | bytes 11010048 | tf_op jit(solution)/shard_map/pallas_call | solution.py:425
  60.6 0.8 %shard_map.90 = f32[1,512]{1,0:T(1,128)} custom-call(s32[8,512]{1,0:T(8,128)S(1)} %get-tuple-element.58.route_ref, f32[16,1,128]{2,1,0:T(1,128)S(1)} %all-to-all-done.error_ref), custom_call_target="tpu_custom_call" | custom-call | bytes 24576 | tf_op jit(solution)/shard_map/pallas_call | solution.py:540
  (32 shorter events, 2.8 us)
Async XLA Ops:
  0.6 34.2 %copy-start = (bf16[32,64,768]{2,1,0:T(8,128)(2,1)S(1)}, bf16[32,64,768]{2,1,0:T(8,128)(2,1)}, u32[]{:S(2)}) copy-start(bf16[32,64,768]{2,1,0:T(8,128)(2,1)} %param.10) | copy-start | bytes 9437188
  0.6 34.2 %copy-start.1 = (bf16[32,768]{1,0:T(8,128)(2,1)S(1)}, bf16[32,768]{1,0:T(8,128)(2,1)}, u32[]{:S(2)}) copy-start(bf16[32,768]{1,0:T(8,128)(2,1)} %coarse_ref.9) | copy-start | bytes 147460
  3.9 13.9 %collective-permute-start = (bf16[400,128]{1,0:T(8,128)(2,1)}, bf16[400,128]{1,0:T(8,128)(2,1)S(1)}, u32[]{:S(2)}, u32[]{:S(2)}) collective-permute-start(bf16[400,128]{1,0:T(8,128)(2,1)} %get-tuple-element.61), channel_id=1, source_target_pairs={{0,12},{1,13},{2,14},{3,15},{4,8},{5,9},{6,10},{7,11},{8,4},{9,5},... | collective-permute-start | bytes 307208 | tf_op jit(solution)/shard_map/ppermute | solution.py:497
  9.0 9.2 %collective-permute-start.3 = (bf16[400,128]{1,0:T(8,128)(2,1)}, bf16[400,128]{1,0:T(8,128)(2,1)S(1)}, u32[]{:S(2)}, u32[]{:S(2)}) collective-permute-start(bf16[400,128]{1,0:T(8,128)(2,1)} %get-tuple-element.66), channel_id=1, source_target_pairs={{0,6},{1,7},{2,4},{3,5},{4,2},{5,3},{6,0},{7,1},{8,14},{9,15},{10,... | collective-permute-start | bytes 307208 | tf_op jit(solution)/shard_map/ppermute | solution.py:497
  9.5 9.7 %collective-permute-start.5 = (bf16[400,128]{1,0:T(8,128)(2,1)}, bf16[400,128]{1,0:T(8,128)(2,1)}, u32[]{:S(2)}, u32[]{:S(2)}) collective-permute-start(bf16[400,128]{1,0:T(8,128)(2,1)} %get-tuple-element.70), channel_id=1, source_target_pairs={{0,8},{1,9},{2,10},{3,11},{4,12},{5,13},{6,14},{7,15},{8,0},{9,1},... | collective-permute-start | bytes 307208 | tf_op jit(solution)/shard_map/ppermute | solution.py:497
  10.7 8.9 %collective-permute-start.6 = (bf16[400,128]{1,0:T(8,128)(2,1)}, bf16[400,128]{1,0:T(8,128)(2,1)}, u32[]{:S(2)}, u32[]{:S(2)}) collective-permute-start(bf16[400,128]{1,0:T(8,128)(2,1)} %get-tuple-element.73), channel_id=1, source_target_pairs={{0,7},{1,6},{2,5},{3,4},{4,3},{5,2},{6,1},{7,0},{8,15},{9,14},{10,... | collective-permute-start | bytes 307208 | tf_op jit(solution)/shard_map/ppermute | solution.py:497
  10.8 13.4 %collective-permute-start.7 = (bf16[400,128]{1,0:T(8,128)(2,1)}, bf16[400,128]{1,0:T(8,128)(2,1)S(1)}, u32[]{:S(2)}, u32[]{:S(2)}) collective-permute-start(bf16[400,128]{1,0:T(8,128)(2,1)} %get-tuple-element.79), channel_id=1, source_target_pairs={{0,10},{1,11},{2,8},{3,9},{4,14},{5,15},{6,12},{7,13},{8,2},{9,3},... | collective-permute-start | bytes 307208 | tf_op jit(solution)/shard_map/ppermute | solution.py:497
  17.8 10.5 %collective-permute-start.8 = (bf16[400,128]{1,0:T(8,128)(2,1)}, bf16[400,128]{1,0:T(8,128)(2,1)S(1)}, u32[]{:S(2)}, u32[]{:S(2)}) collective-permute-start(bf16[400,128]{1,0:T(8,128)(2,1)} %get-tuple-element.82), channel_id=1, source_target_pairs={{0,5},{1,4},{2,7},{3,6},{4,1},{5,0},{6,3},{7,2},{8,13},{9,12},{10,... | collective-permute-start | bytes 307208 | tf_op jit(solution)/shard_map/ppermute | solution.py:497
  18.2 16.0 %collective-permute-start.1 = (bf16[400,128]{1,0:T(8,128)(2,1)}, bf16[400,128]{1,0:T(8,128)(2,1)S(1)}, u32[]{:S(2)}, u32[]{:S(2)}) collective-permute-start(bf16[400,128]{1,0:T(8,128)(2,1)} %get-tuple-element.62), channel_id=1, source_target_pairs={{0,9},{1,8},{2,11},{3,10},{4,13},{5,12},{6,15},{7,14},{8,1},{9,0},... | collective-permute-start | bytes 307208 | tf_op jit(solution)/shard_map/ppermute | solution.py:497
  19.2 18.8 %collective-permute-start.4 = (bf16[400,128]{1,0:T(8,128)(2,1)}, bf16[400,128]{1,0:T(8,128)(2,1)S(1)}, u32[]{:S(2)}, u32[]{:S(2)}) collective-permute-start(bf16[400,128]{1,0:T(8,128)(2,1)} %get-tuple-element.67), channel_id=1, source_target_pairs={{0,3},{1,2},{2,1},{3,0},{4,7},{5,6},{6,5},{7,4},{8,11},{9,10},{10,... | collective-permute-start | bytes 307208 | tf_op jit(solution)/shard_map/ppermute | solution.py:497
  19.6 9.3 %collective-permute-start.9 = (bf16[400,128]{1,0:T(8,128)(2,1)}, bf16[400,128]{1,0:T(8,128)(2,1)S(1)}, u32[]{:S(2)}, u32[]{:S(2)}) collective-permute-start(bf16[400,128]{1,0:T(8,128)(2,1)} %get-tuple-element.85), channel_id=1, source_target_pairs={{0,14},{1,15},{2,12},{3,13},{4,10},{5,11},{6,8},{7,9},{8,6},{9,7},... | collective-permute-start | bytes 307208 | tf_op jit(solution)/shard_map/ppermute | solution.py:497
  24.3 6.9 %collective-permute-start.10 = (bf16[400,128]{1,0:T(8,128)(2,1)}, bf16[400,128]{1,0:T(8,128)(2,1)S(1)}, u32[]{:S(2)}, u32[]{:S(2)}) collective-permute-start(bf16[400,128]{1,0:T(8,128)(2,1)} %get-tuple-element.88), channel_id=1, source_target_pairs={{0,4},{1,5},{2,6},{3,7},{4,0},{5,1},{6,2},{7,3},{8,12},{9,13},{10,... | collective-permute-start | bytes 307208 | tf_op jit(solution)/shard_map/ppermute | solution.py:497
  24.3 1.1 %copy-start.3 = (bf16[512,768]{1,0:T(8,128)(2,1)S(1)}, bf16[512,768]{1,0:T(8,128)(2,1)}, u32[]{:S(2)}) copy-start(bf16[512,768]{1,0:T(8,128)(2,1)} %rows_ref.1) | copy-start | bytes 2359300
  25.4 12.6 %copy-start.6 = (bf16[400,128]{1,0:T(8,128)(2,1)S(1)}, bf16[400,128]{1,0:T(8,128)(2,1)}, u32[]{:S(2)}) copy-start(bf16[400,128]{1,0:T(8,128)(2,1)} %get-tuple-element.63) | copy-start | bytes 307204
  28.2 17.6 %copy-start.2 = (bf16[400,128]{1,0:T(8,128)(2,1)S(1)}, bf16[400,128]{1,0:T(8,128)(2,1)}, u32[]{:S(2)}) copy-start(bf16[400,128]{1,0:T(8,128)(2,1)} %get-tuple-element.68.refs_1_) | copy-start | bytes 307204
  28.3 12.6 %collective-permute-start.11 = (bf16[400,128]{1,0:T(8,128)(2,1)}, bf16[400,128]{1,0:T(8,128)(2,1)S(1)}, u32[]{:S(2)}, u32[]{:S(2)}) collective-permute-start(bf16[400,128]{1,0:T(8,128)(2,1)} %get-tuple-element.93), channel_id=1, source_target_pairs={{0,13},{1,12},{2,15},{3,14},{4,9},{5,8},{6,11},{7,10},{8,5},{9,4},... | collective-permute-start | bytes 307208 | tf_op jit(solution)/shard_map/ppermute | solution.py:497
  28.9 12.0 %collective-permute-start.12 = (bf16[400,128]{1,0:T(8,128)(2,1)}, bf16[400,128]{1,0:T(8,128)(2,1)S(1)}, u32[]{:S(2)}, u32[]{:S(2)}) collective-permute-start(bf16[400,128]{1,0:T(8,128)(2,1)} %get-tuple-element.94), channel_id=1, source_target_pairs={{0,2},{1,3},{2,0},{3,1},{4,6},{5,7},{6,4},{7,5},{8,10},{9,11},{10,... | collective-permute-start | bytes 307208 | tf_op jit(solution)/shard_map/ppermute | solution.py:497
  31.1 10.2 %collective-permute-start.13 = (bf16[400,128]{1,0:T(8,128)(2,1)}, bf16[400,128]{1,0:T(8,128)(2,1)S(1)}, u32[]{:S(2)}, u32[]{:S(2)}) collective-permute-start(bf16[400,128]{1,0:T(8,128)(2,1)} %get-tuple-element.95), channel_id=1, source_target_pairs={{0,11},{1,10},{2,9},{3,8},{4,15},{5,14},{6,13},{7,12},{8,3},{9,2},... | collective-permute-start | bytes 307208 | tf_op jit(solution)/shard_map/ppermute | solution.py:497
  34.2 7.1 %collective-permute-start.14 = (bf16[400,128]{1,0:T(8,128)(2,1)}, bf16[400,128]{1,0:T(8,128)(2,1)S(1)}, u32[]{:S(2)}, u32[]{:S(2)}) collective-permute-start(bf16[400,128]{1,0:T(8,128)(2,1)} %get-tuple-element.96), channel_id=1, source_target_pairs={{0,1},{1,0},{2,3},{3,2},{4,5},{5,4},{6,7},{7,6},{8,9},{9,8},{10,11... | collective-permute-start | bytes 307208 | tf_op jit(solution)/shard_map/ppermute | solution.py:497
  37.4 0.6 %copy-start.4 = (bf16[64,256]{1,0:T(8,128)(2,1)}, bf16[64,256]{1,0:T(8,128)(2,1)S(1)}, u32[]{:S(2)}) copy-start(bf16[64,256]{1,0:T(8,128)(2,1)S(1)} %get-tuple-element.103.refs_4_) | copy-start | bytes 98308
  38.0 13.5 %copy-start.5 = (bf16[64,256]{1,0:T(8,128)(2,1)S(1)}, bf16[64,256]{1,0:T(8,128)(2,1)}, u32[]{:S(2)}) copy-start(bf16[64,256]{1,0:T(8,128)(2,1)} %copy-done.4) | copy-start | bytes 98308
  38.0 7.8 %collective-permute-start.2 = (bf16[400,128]{1,0:T(8,128)(2,1)S(1)}, bf16[400,128]{1,0:T(8,128)(2,1)S(1)}, u32[]{:S(2)}, u32[]{:S(2)}) collective-permute-start(bf16[400,128]{1,0:T(8,128)(2,1)S(1)} %copy-done.6), channel_id=1, source_target_pairs={{0,15},{1,14},{2,13},{3,12},{4,11},{5,10},{6,9},{7,8},{8,7},{9,6},... | collective-permute-start | bytes 307208 | tf_op jit(solution)/shard_map/ppermute | solution.py:497
  47.8 12.8 %all-to-all-start = ((f32[16,1,128]{2,1,0:T(1,128)}), f32[16,1,128]{2,1,0:T(1,128)S(1)}, u32[]{:S(2)}, u32[]{:S(2)}) async-start(f32[16,1,128]{2,1,0:T(1,128)} %get-tuple-element.98), calls=%async_computation | async-start | bytes 16384 | tf_op jit(solution)/shard_map/all_to_all | solution.py:538

commit v5 on v4

--- a/solution.py
+++ b/solution.py
@@ -10,7 +10,7 @@
 TEMP = 16
 LANES = 128
 META = 16
-DISTANCES = [8, 7, 12, 6, 10, 5, 14, 4, 9, 3, 13, 2, 11, 1, 15, 0]
+DISTANCES = [10, 7, 14, 6, 8, 5, 12, 4, 11, 3, 15, 2, 9, 1, 13, 0]
 WINDOW = 6
 SIZES = (4, 4, 6, 2)
 VMEM_LIMIT = 24 * 1024 * 1024

time: 61.7 us -> 60.9 us (0.987)
  waiting for transfers between devices: 3.64 us -> 2.43 us
    ppermute x15, waiting for transfers between devices: 3.64 us -> 2.43 us  [shards(): lax.ppermute(block_out, 'wide', [(p, p ^ r) for p in range(peers)])]
  transfers between devices with their start and end apart: 16 -> 16, of which waited for: 4 -> 3; matrix products, arithmetic and copies ran while one was open for 5% -> 6% of each run, Pallas kernels for 30% -> 31%
where the time goes in v5:
time: 60.9 us; the launch traced here: 60.5 us
  starting transfers between devices  27.6 us (45%)
  Pallas kernels  24.6 us (40%)
  local copies, waits for them, and re-layouts  2.56 us (4%)
  other arithmetic  2.56 us (4%)
  waiting for transfers between devices  2.43 us (4%)
  between operations  0.81 us (1%)
    ppermute x15, starting transfers between devices, shards(): lax.ppermute(block_out, 'wide', [(p, p ^ r) for p in range(peers)])  23.6 us
    pallas_call x1, Pallas kernels, update(): call(functools.partial(update_kernel, sets), (), [VMEM] * (1 + 2 * sets)...  9.13 us
    pallas_call x4, Pallas kernels, score(): call(functools.partial(score_kernel, blocks, capacity, far_of, known), ()...  8.61 us
    all_to_all x1, starting transfers between devices, shards(): lax.all_to_all(scored[-1][0], 'wide', split_axis=0, concat_axis=0, tiled=...  3.92 us
    pallas_call x1, Pallas kernels, shards(): call(functools.partial(pack_split_kernel, peers, capacity, cells_dev, dis...  3.26 us
    pallas_call x1, Pallas kernels, shards(): call(seed_kernel, (), [VMEM, VMEM], HBM, pltpu.HBM((fine_all, width), BF)...  2.82 us
    reduce_sum x1, other arithmetic, shards(): norm = jnp.sum(fine_wide * fine_wide, axis=-1)  2.56 us
    ppermute x15, waiting for transfers between devices, shards(): lax.ppermute(block_out, 'wide', [(p, p ^ r) for p in range(peers)])  2.43 us
  transfers between devices with their start and end apart: 16, of which 3 were waited for; matrix products, arithmetic and copies ran while one was open for 6% of the time, Pallas kernels for 31%

profile of v5, /device:TPU:0, one launch (start us, length us, event | category | flops | bytes accessed | tf_op | source)
XLA Modules:
  0.0 60.5 jit_solution(691126214554558173)
XLA Ops:
  0.7 3.3 %shard_map.85 = (bf16[400,128]{1,0:T(8,128)(2,1)}, bf16[400,128]{1,0:T(8,128)(2,1)}, bf16[400,128]{1,0:T(8,128)(2,1)}, bf16[400,128]{1,0:T(8,128)(2,1)}, bf16[40...) custom-call(s32[1,512]{1,0:T(1,128)} %bitcast.10, ...), custom_call_target="tpu_custom_call" | custom-call | flops 805306368 | bytes 3145728 | tf_op jit(solution)/shard_map/pallas_call | solution.py:474
  3.9 6.0 %collective-permute-start = (bf16[400,128]{1,0:T(8,128)(2,1)}, bf16[400,128]{1,0:T(8,128)(2,1)S(1)}, u32[]{:S(2)}, u32[]{:S(2)}) collective-permute-start(bf16[400,128]{1,0:T(8,128)(2,1)} %get-tuple-element.61), channel_id=1, source_target_pairs={{0,14},{1,15},{2,12},{3,13},{4,10},{5,11},{6,8},{7,9},{8,6},{9,7},... | collective-permute-start | bytes 307208 | tf_op jit(solution)/shard_map/ppermute | solution.py:497
  10.0 1.7 %collective-permute-start.5 = (bf16[400,128]{1,0:T(8,128)(2,1)}, bf16[400,128]{1,0:T(8,128)(2,1)}, u32[]{:S(2)}, u32[]{:S(2)}) collective-permute-start(bf16[400,128]{1,0:T(8,128)(2,1)} %get-tuple-element.70), channel_id=1, source_target_pairs={{0,10},{1,11},{2,8},{3,9},{4,14},{5,15},{6,12},{7,13},{8,2},{9,3},... | collective-permute-start | bytes 307208 | tf_op jit(solution)/shard_map/ppermute | solution.py:497
  11.8 2.6 %collective-permute-start.7 = (bf16[400,128]{1,0:T(8,128)(2,1)}, bf16[400,128]{1,0:T(8,128)(2,1)S(1)}, u32[]{:S(2)}, u32[]{:S(2)}) collective-permute-start(bf16[400,128]{1,0:T(8,128)(2,1)} %get-tuple-element.79), channel_id=1, source_target_pairs={{0,8},{1,9},{2,10},{3,11},{4,12},{5,13},{6,14},{7,15},{8,0},{9,1},... | collective-permute-start | bytes 307208 | tf_op jit(solution)/shard_map/ppermute | solution.py:497
  14.4 2.6 %multiply_reduce_fusion.norm_ref = f32[32,64]{1,0:T(8,128)S(1)} fusion(bf16[32,64,768]{2,1,0:T(8,128)(2,1)} %param.10), kind=kLoop, calls=%fused_computation | loop fusion | flops 4716544 | bytes 3153920 | tf_op jit(solution)/shard_map/reduce_sum | solution.py:458
  16.9 0.8 %reshape.28.reseed_ref = s32[1,2048]{1,0:T(1,128)S(1)} reshape(s32[32,64]{1,0:T(8,128)} %param.11) | data formatting | bytes 16384 | tf_op jit(solution)/shard_map/reshape | solution.py:469
  17.8 0.9 %collective-permute-start.8 = (bf16[400,128]{1,0:T(8,128)(2,1)}, bf16[400,128]{1,0:T(8,128)(2,1)S(1)}, u32[]{:S(2)}, u32[]{:S(2)}) collective-permute-start(bf16[400,128]{1,0:T(8,128)(2,1)} %get-tuple-element.82), channel_id=1, source_target_pairs={{0,5},{1,4},{2,7},{3,6},{4,1},{5,0},{6,3},{7,2},{8,13},{9,12},{10,... | collective-permute-start | bytes 307208 | tf_op jit(solution)/shard_map/ppermute | solution.py:497
  20.5 3.7 %collective-permute-start.9 = (bf16[400,128]{1,0:T(8,128)(2,1)}, bf16[400,128]{1,0:T(8,128)(2,1)S(1)}, u32[]{:S(2)}, u32[]{:S(2)}) collective-permute-start(bf16[400,128]{1,0:T(8,128)(2,1)} %get-tuple-element.85), channel_id=1, source_target_pairs={{0,12},{1,13},{2,14},{3,15},{4,8},{5,9},{6,10},{7,11},{8,4},{9,5},... | collective-permute-start | bytes 307208 | tf_op jit(solution)/shard_map/ppermute | solution.py:497
  24.2 1.1 %copy-done.3 = bf16[512,768]{1,0:T(8,128)(2,1)S(1)} copy-done((bf16[512,768]{1,0:T(8,128)(2,1)S(1)}, bf16[512,768]{1,0:T(8,128)(2,1)}, u32[]{:S(2)}) %copy-start.3) | copy-done | bytes 786456
  25.4 2.8 %shard_map.91.refs_12_ = bf16[2048,768]{1,0:T(8,128)(2,1)} custom-call(s32[1,2048]{1,0:T(1,128)S(1)} %reshape.28.reseed_ref, bf16[512,768]{1,0:T(8,128)(2,1)S(1)} %copy-done.3), custom_call_target="tpu_custom_call" | custom-call | flops 1610612736 | bytes 3932160 | tf_op jit(solution)/shard_map/pallas_call | solution.py:460
  28.2 1.3 %collective-permute-start.11 = (bf16[400,128]{1,0:T(8,128)(2,1)}, bf16[400,128]{1,0:T(8,128)(2,1)S(1)}, u32[]{:S(2)}, u32[]{:S(2)}) collective-permute-start(bf16[400,128]{1,0:T(8,128)(2,1)} %get-tuple-element.93), channel_id=1, source_target_pairs={{0,15},{1,14},{2,13},{3,12},{4,11},{5,10},{6,9},{7,8},{8,7},{9,6},... | collective-permute-start | bytes 307208 | tf_op jit(solution)/shard_map/ppermute | solution.py:497
  29.6 1.3 %collective-permute-start.12 = (bf16[400,128]{1,0:T(8,128)(2,1)}, bf16[400,128]{1,0:T(8,128)(2,1)S(1)}, u32[]{:S(2)}, u32[]{:S(2)}) collective-permute-start(bf16[400,128]{1,0:T(8,128)(2,1)} %get-tuple-element.94), channel_id=1, source_target_pairs={{0,2},{1,3},{2,0},{3,1},{4,6},{5,7},{6,4},{7,5},{8,10},{9,11},{10,... | collective-permute-start | bytes 307208 | tf_op jit(solution)/shard_map/ppermute | solution.py:497
  30.9 0.9 %collective-permute-done.10.refs_3_ = bf16[400,128]{1,0:T(8,128)(2,1)S(1)} collective-permute-done((bf16[400,128]{1,0:T(8,128)(2,1)}, bf16[400,128]{1,0:T(8,128)(2,1)S(1)}, u32[]{:S(2)}, u32[]{:S(2)}) %collective-permute-start.10) | collective-permute-done | bytes 102432 | tf_op jit(solution)/shard_map/ppermute | solution.py:497
  31.8 1.7 %collective-permute-start.13 = (bf16[400,128]{1,0:T(8,128)(2,1)}, bf16[400,128]{1,0:T(8,128)(2,1)S(1)}, u32[]{:S(2)}, u32[]{:S(2)}) collective-permute-start(bf16[400,128]{1,0:T(8,128)(2,1)} %get-tuple-element.95), channel_id=1, source_target_pairs={{0,9},{1,8},{2,11},{3,10},{4,13},{5,12},{6,15},{7,14},{8,1},{9,0},... | collective-permute-start | bytes 307208 | tf_op jit(solution)/shard_map/ppermute | solution.py:497
  33.5 0.8 %collective-permute-start.14 = (bf16[400,128]{1,0:T(8,128)(2,1)}, bf16[400,128]{1,0:T(8,128)(2,1)S(1)}, u32[]{:S(2)}, u32[]{:S(2)}) collective-permute-start(bf16[400,128]{1,0:T(8,128)(2,1)} %get-tuple-element.96), channel_id=1, source_target_pairs={{0,1},{1,0},{2,3},{3,2},{4,5},{5,4},{6,7},{7,6},{8,9},{9,8},{10,11... | collective-permute-start | bytes 307208 | tf_op jit(solution)/shard_map/ppermute | solution.py:497
  34.3 2.5 %shard_map.86 = (f32[4,1,128]{2,1,0:T(1,128)S(1)}, bf16[64,256]{1,0:T(8,128)(2,1)S(1)}, s32[1,256]{1,0:T(1,128)S(1)}, bf16[256,768]{1,0:T(8,128)(2,1)}) custom-call(bf16[32,768]{1,0:T(8,128)(2,1)S(1)} %copy-done.1, f32[32,64]{1,0:T(8,128)S(1)} %multiply_reduce_fusion.norm_ref, bf16[2048,768]{1,0:T(8,128)(2,1)S(1)} %bitcast.5, ...), custom_call_target="tpu_custom_call" | custom-call | flops 805306368 | bytes 3932160 | tf_op jit(solution)/shard_map/pallas_call | solution.py:398
  37.4 2.1 %collective-permute-start.2 = (bf16[400,128]{1,0:T(8,128)(2,1)S(1)}, bf16[400,128]{1,0:T(8,128)(2,1)S(1)}, u32[]{:S(2)}, u32[]{:S(2)}) collective-permute-start(bf16[400,128]{1,0:T(8,128)(2,1)S(1)} %copy-done.6), channel_id=1, source_target_pairs={{0,13},{1,12},{2,15},{3,14},{4,9},{5,8},{6,11},{7,10},{8,5},{9,4},... | collective-permute-start | bytes 307208 | tf_op jit(solution)/shard_map/ppermute | solution.py:497
  39.5 1.5 %shard_map.87 = (f32[4,1,128]{2,1,0:T(1,128)S(1)}, bf16[64,256]{1,0:T(8,128)(2,1)S(1)}, s32[1,256]{1,0:T(1,128)S(1)}, bf16[256,768]{1,0:T(8,128)(2,1)}) custom-call(bf16[32,768]{1,0:T(8,128)(2,1)S(1)} %copy-done.1, f32[32,64]{1,0:T(8,128)S(1)} %multiply_reduce_fusion.norm_ref, bf16[2048,768]{1,0:T(8,128)(2,1)S(1)} %bitcast.6, ...), custom_call_target="tpu_custom_call" | custom-call | flops 805306368 | bytes 3932160 | tf_op jit(solution)/shard_map/pallas_call | solution.py:398
  41.1 0.9 %collective-permute-done.13.refs_4_ = bf16[400,128]{1,0:T(8,128)(2,1)S(1)} collective-permute-done((bf16[400,128]{1,0:T(8,128)(2,1)}, bf16[400,128]{1,0:T(8,128)(2,1)S(1)}, u32[]{:S(2)}, u32[]{:S(2)}) %collective-permute-start.13) | collective-permute-done | bytes 102432 | tf_op jit(solution)/shard_map/ppermute | solution.py:497
  42.0 2.6 %shard_map.88 = (f32[6,1,128]{2,1,0:T(1,128)S(1)}, bf16[64,384]{1,0:T(8,128)(2,1)S(1)}, s32[1,384]{1,0:T(1,128)S(1)}, bf16[384,768]{1,0:T(8,128)(2,1)}) custom-call(bf16[32,768]{1,0:T(8,128)(2,1)S(1)} %copy-done.1, f32[32,64]{1,0:T(8,128)S(1)} %multiply_reduce_fusion.norm_ref, bf16[2048,768]{1,0:T(8,128)(2,1)S(1)} %bitcast.7, ...), custom_call_target="tpu_custom_call" | custom-call | flops 1207959552 | bytes 4325376 | tf_op jit(solution)/shard_map/pallas_call | solution.py:398
  44.6 2.0 %shard_map.89 = (f32[16,1,128]{2,1,0:T(1,128)}, bf16[64,128]{1,0:T(8,128)(2,1)S(1)}, s32[1,128]{1,0:T(1,128)S(1)}, bf16[128,768]{1,0:T(8,128)(2,1)}) custom-call(bf16[32,768]{1,0:T(8,128)(2,1)S(1)} %copy-done.1, f32[32,64]{1,0:T(8,128)S(1)} %multiply_reduce_fusion.norm_ref, bf16[2048,768]{1,0:T(8,128)(2,1)S(1)} %bitcast.8, ...), custom_call_target="tpu_custom_call" | custom-call | flops 402653184 | bytes 3538944 | tf_op jit(solution)/shard_map/pallas_call | solution.py:398
  46.7 3.9 %all-to-all-start = ((f32[16,1,128]{2,1,0:T(1,128)}), f32[16,1,128]{2,1,0:T(1,128)S(1)}, u32[]{:S(2)}, u32[]{:S(2)}) async-start(f32[16,1,128]{2,1,0:T(1,128)} %get-tuple-element.98), calls=%async_computation | async-start | bytes 16384 | tf_op jit(solution)/shard_map/all_to_all | solution.py:538
  50.6 9.1 %shard_map.92 = (f32[32,768]{1,0:T(8,128)}, f32[2048,768]{1,0:T(8,128)}) custom-call(bf16[32,768]{1,0:T(8,128)(2,1)S(1)} %copy-done.1, s32[1,256]{1,0:T(1,128)S(1)} %get-tuple-element.99.refs_0_, s32[1,256]{1,0:T(1,128)S(1)} %get-tuple-element.100.refs_1_, s32[1,384]{1,0:T(1,128)S(1)} %get-tuple-element.101.refs_2_, ...), custom_call_target="tpu_custom_call" | custom-call | flops 3221225472 | bytes 11010048 | tf_op jit(solution)/shard_map/pallas_call | solution.py:425
  59.7 0.8 %shard_map.90 = f32[1,512]{1,0:T(1,128)} custom-call(s32[8,512]{1,0:T(8,128)S(1)} %get-tuple-element.58.route_ref, f32[16,1,128]{2,1,0:T(1,128)S(1)} %all-to-all-done.error_ref), custom_call_target="tpu_custom_call" | custom-call | bytes 24576 | tf_op jit(solution)/shard_map/pallas_call | solution.py:540
  (32 shorter events, 2.6 us)
Async XLA Ops:
  0.6 33.7 %copy-start = (bf16[32,64,768]{2,1,0:T(8,128)(2,1)S(1)}, bf16[32,64,768]{2,1,0:T(8,128)(2,1)}, u32[]{:S(2)}) copy-start(bf16[32,64,768]{2,1,0:T(8,128)(2,1)} %param.10) | copy-start | bytes 9437188
  0.6 33.7 %copy-start.1 = (bf16[32,768]{1,0:T(8,128)(2,1)S(1)}, bf16[32,768]{1,0:T(8,128)(2,1)}, u32[]{:S(2)}) copy-start(bf16[32,768]{1,0:T(8,128)(2,1)} %coarse_ref.9) | copy-start | bytes 147460
  3.9 13.8 %collective-permute-start = (bf16[400,128]{1,0:T(8,128)(2,1)}, bf16[400,128]{1,0:T(8,128)(2,1)S(1)}, u32[]{:S(2)}, u32[]{:S(2)}) collective-permute-start(bf16[400,128]{1,0:T(8,128)(2,1)} %get-tuple-element.61), channel_id=1, source_target_pairs={{0,14},{1,15},{2,12},{3,13},{4,10},{5,11},{6,8},{7,9},{8,6},{9,7},... | collective-permute-start | bytes 307208 | tf_op jit(solution)/shard_map/ppermute | solution.py:497
  10.0 9.3 %collective-permute-start.3 = (bf16[400,128]{1,0:T(8,128)(2,1)}, bf16[400,128]{1,0:T(8,128)(2,1)S(1)}, u32[]{:S(2)}, u32[]{:S(2)}) collective-permute-start(bf16[400,128]{1,0:T(8,128)(2,1)} %get-tuple-element.66), channel_id=1, source_target_pairs={{0,6},{1,7},{2,4},{3,5},{4,2},{5,3},{6,0},{7,1},{8,14},{9,15},{10,... | collective-permute-start | bytes 307208 | tf_op jit(solution)/shard_map/ppermute | solution.py:497
  10.0 10.0 %collective-permute-start.5 = (bf16[400,128]{1,0:T(8,128)(2,1)}, bf16[400,128]{1,0:T(8,128)(2,1)}, u32[]{:S(2)}, u32[]{:S(2)}) collective-permute-start(bf16[400,128]{1,0:T(8,128)(2,1)} %get-tuple-element.70), channel_id=1, source_target_pairs={{0,10},{1,11},{2,8},{3,9},{4,14},{5,15},{6,12},{7,13},{8,2},{9,3},... | collective-permute-start | bytes 307208 | tf_op jit(solution)/shard_map/ppermute | solution.py:497
  11.6 8.9 %collective-permute-start.6 = (bf16[400,128]{1,0:T(8,128)(2,1)}, bf16[400,128]{1,0:T(8,128)(2,1)}, u32[]{:S(2)}, u32[]{:S(2)}) collective-permute-start(bf16[400,128]{1,0:T(8,128)(2,1)} %get-tuple-element.73), channel_id=1, source_target_pairs={{0,7},{1,6},{2,5},{3,4},{4,3},{5,2},{6,1},{7,0},{8,15},{9,14},{10,... | collective-permute-start | bytes 307208 | tf_op jit(solution)/shard_map/ppermute | solution.py:497
  11.8 12.5 %collective-permute-start.7 = (bf16[400,128]{1,0:T(8,128)(2,1)}, bf16[400,128]{1,0:T(8,128)(2,1)S(1)}, u32[]{:S(2)}, u32[]{:S(2)}) collective-permute-start(bf16[400,128]{1,0:T(8,128)(2,1)} %get-tuple-element.79), channel_id=1, source_target_pairs={{0,8},{1,9},{2,10},{3,11},{4,12},{5,13},{6,14},{7,15},{8,0},{9,1},... | collective-permute-start | bytes 307208 | tf_op jit(solution)/shard_map/ppermute | solution.py:497
  17.8 10.5 %collective-permute-start.8 = (bf16[400,128]{1,0:T(8,128)(2,1)}, bf16[400,128]{1,0:T(8,128)(2,1)S(1)}, u32[]{:S(2)}, u32[]{:S(2)}) collective-permute-start(bf16[400,128]{1,0:T(8,128)(2,1)} %get-tuple-element.82), channel_id=1, source_target_pairs={{0,5},{1,4},{2,7},{3,6},{4,1},{5,0},{6,3},{7,2},{8,13},{9,12},{10,... | collective-permute-start | bytes 307208 | tf_op jit(solution)/shard_map/ppermute | solution.py:497
  19.3 14.2 %collective-permute-start.1 = (bf16[400,128]{1,0:T(8,128)(2,1)}, bf16[400,128]{1,0:T(8,128)(2,1)S(1)}, u32[]{:S(2)}, u32[]{:S(2)}) collective-permute-start(bf16[400,128]{1,0:T(8,128)(2,1)} %get-tuple-element.62), channel_id=1, source_target_pairs={{0,11},{1,10},{2,9},{3,8},{4,15},{5,14},{6,13},{7,12},{8,3},{9,2},... | collective-permute-start | bytes 307208 | tf_op jit(solution)/shard_map/ppermute | solution.py:497
  20.0 17.5 %collective-permute-start.4 = (bf16[400,128]{1,0:T(8,128)(2,1)}, bf16[400,128]{1,0:T(8,128)(2,1)S(1)}, u32[]{:S(2)}, u32[]{:S(2)}) collective-permute-start(bf16[400,128]{1,0:T(8,128)(2,1)} %get-tuple-element.67), channel_id=1, source_target_pairs={{0,3},{1,2},{2,1},{3,0},{4,7},{5,6},{6,5},{7,4},{8,11},{9,10},{10,... | collective-permute-start | bytes 307208 | tf_op jit(solution)/shard_map/ppermute | solution.py:497
  20.5 9.0 %collective-permute-start.9 = (bf16[400,128]{1,0:T(8,128)(2,1)}, bf16[400,128]{1,0:T(8,128)(2,1)S(1)}, u32[]{:S(2)}, u32[]{:S(2)}) collective-permute-start(bf16[400,128]{1,0:T(8,128)(2,1)} %get-tuple-element.85), channel_id=1, source_target_pairs={{0,12},{1,13},{2,14},{3,15},{4,8},{5,9},{6,10},{7,11},{8,4},{9,5},... | collective-permute-start | bytes 307208 | tf_op jit(solution)/shard_map/ppermute | solution.py:497
  24.2 7.5 %collective-permute-start.10 = (bf16[400,128]{1,0:T(8,128)(2,1)}, bf16[400,128]{1,0:T(8,128)(2,1)S(1)}, u32[]{:S(2)}, u32[]{:S(2)}) collective-permute-start(bf16[400,128]{1,0:T(8,128)(2,1)} %get-tuple-element.88), channel_id=1, source_target_pairs={{0,4},{1,5},{2,6},{3,7},{4,0},{5,1},{6,2},{7,3},{8,12},{9,13},{10,... | collective-permute-start | bytes 307208 | tf_op jit(solution)/shard_map/ppermute | solution.py:497
  24.2 1.1 %copy-start.3 = (bf16[512,768]{1,0:T(8,128)(2,1)S(1)}, bf16[512,768]{1,0:T(8,128)(2,1)}, u32[]{:S(2)}) copy-start(bf16[512,768]{1,0:T(8,128)(2,1)} %rows_ref.1) | copy-start | bytes 2359300
  25.4 12.1 %copy-start.6 = (bf16[400,128]{1,0:T(8,128)(2,1)S(1)}, bf16[400,128]{1,0:T(8,128)(2,1)}, u32[]{:S(2)}) copy-start(bf16[400,128]{1,0:T(8,128)(2,1)} %get-tuple-element.63) | copy-start | bytes 307204
  28.2 16.4 %copy-start.2 = (bf16[400,128]{1,0:T(8,128)(2,1)S(1)}, bf16[400,128]{1,0:T(8,128)(2,1)}, u32[]{:S(2)}) copy-start(bf16[400,128]{1,0:T(8,128)(2,1)} %get-tuple-element.68.refs_1_) | copy-start | bytes 307204
  28.2 12.8 %collective-permute-start.11 = (bf16[400,128]{1,0:T(8,128)(2,1)}, bf16[400,128]{1,0:T(8,128)(2,1)S(1)}, u32[]{:S(2)}, u32[]{:S(2)}) collective-permute-start(bf16[400,128]{1,0:T(8,128)(2,1)} %get-tuple-element.93), channel_id=1, source_target_pairs={{0,15},{1,14},{2,13},{3,12},{4,11},{5,10},{6,9},{7,8},{8,7},{9,6},... | collective-permute-start | bytes 307208 | tf_op jit(solution)/shard_map/ppermute | solution.py:497
  29.6 11.5 %collective-permute-start.12 = (bf16[400,128]{1,0:T(8,128)(2,1)}, bf16[400,128]{1,0:T(8,128)(2,1)S(1)}, u32[]{:S(2)}, u32[]{:S(2)}) collective-permute-start(bf16[400,128]{1,0:T(8,128)(2,1)} %get-tuple-element.94), channel_id=1, source_target_pairs={{0,2},{1,3},{2,0},{3,1},{4,6},{5,7},{6,4},{7,5},{8,10},{9,11},{10,... | collective-permute-start | bytes 307208 | tf_op jit(solution)/shard_map/ppermute | solution.py:497
  31.8 10.3 %collective-permute-start.13 = (bf16[400,128]{1,0:T(8,128)(2,1)}, bf16[400,128]{1,0:T(8,128)(2,1)S(1)}, u32[]{:S(2)}, u32[]{:S(2)}) collective-permute-start(bf16[400,128]{1,0:T(8,128)(2,1)} %get-tuple-element.95), channel_id=1, source_target_pairs={{0,9},{1,8},{2,11},{3,10},{4,13},{5,12},{6,15},{7,14},{8,1},{9,0},... | collective-permute-start | bytes 307208 | tf_op jit(solution)/shard_map/ppermute | solution.py:497
  33.5 8.5 %collective-permute-start.14 = (bf16[400,128]{1,0:T(8,128)(2,1)}, bf16[400,128]{1,0:T(8,128)(2,1)S(1)}, u32[]{:S(2)}, u32[]{:S(2)}) collective-permute-start(bf16[400,128]{1,0:T(8,128)(2,1)} %get-tuple-element.96), channel_id=1, source_target_pairs={{0,1},{1,0},{2,3},{3,2},{4,5},{5,4},{6,7},{7,6},{8,9},{9,8},{10,11... | collective-permute-start | bytes 307208 | tf_op jit(solution)/shard_map/ppermute | solution.py:497
  36.8 0.6 %copy-start.4 = (bf16[64,256]{1,0:T(8,128)(2,1)}, bf16[64,256]{1,0:T(8,128)(2,1)S(1)}, u32[]{:S(2)}) copy-start(bf16[64,256]{1,0:T(8,128)(2,1)S(1)} %get-tuple-element.103.refs_4_) | copy-start | bytes 98308
  37.4 13.2 %copy-start.5 = (bf16[64,256]{1,0:T(8,128)(2,1)S(1)}, bf16[64,256]{1,0:T(8,128)(2,1)}, u32[]{:S(2)}) copy-start(bf16[64,256]{1,0:T(8,128)(2,1)} %copy-done.4) | copy-start | bytes 98308
  37.4 7.2 %collective-permute-start.2 = (bf16[400,128]{1,0:T(8,128)(2,1)S(1)}, bf16[400,128]{1,0:T(8,128)(2,1)S(1)}, u32[]{:S(2)}, u32[]{:S(2)}) collective-permute-start(bf16[400,128]{1,0:T(8,128)(2,1)S(1)} %copy-done.6), channel_id=1, source_target_pairs={{0,13},{1,12},{2,15},{3,14},{4,9},{5,8},{6,11},{7,10},{8,5},{9,4},... | collective-permute-start | bytes 307208 | tf_op jit(solution)/shard_map/ppermute | solution.py:497
  46.7 13.1 %all-to-all-start = ((f32[16,1,128]{2,1,0:T(1,128)}), f32[16,1,128]{2,1,0:T(1,128)S(1)}, u32[]{:S(2)}, u32[]{:S(2)}) async-start(f32[16,1,128]{2,1,0:T(1,128)} %get-tuple-element.98), calls=%async_computation | async-start | bytes 16384 | tf_op jit(solution)/shard_map/all_to_all | solution.py:538

commit v6 on v5

--- a/solution.py
+++ b/solution.py
@@ -10,7 +10,7 @@
 TEMP = 16
 LANES = 128
 META = 16
-DISTANCES = [10, 7, 14, 6, 8, 5, 12, 4, 11, 3, 15, 2, 9, 1, 13, 0]
+DISTANCES = [10, 6, 14, 7, 8, 4, 12, 5, 11, 2, 15, 3, 9, 1, 13, 0]
 WINDOW = 6
 SIZES = (4, 4, 6, 2)
 VMEM_LIMIT = 24 * 1024 * 1024

time: 60.9 us -> 62.8 us (1.031)
  starting transfers between devices: 27.6 us -> 28.8 us
  waiting for transfers between devices: 2.43 us -> 3.15 us
    all_to_all x1, starting transfers between devices: 3.92 us -> 6.67 us  [shards(): lax.all_to_all(scored[-1][0], 'wide', split_axis=0, concat_axis=0, tiled=...]
    ppermute x15, starting transfers between devices: 23.6 us -> 22.2 us  [shards(): lax.ppermute(block_out, 'wide', [(p, p ^ r) for p in range(peers)])]
    ppermute x15, waiting for transfers between devices: 2.43 us -> 3.14 us  [shards(): lax.ppermute(block_out, 'wide', [(p, p ^ r) for p in range(peers)])]
  transfers between devices with their start and end apart: 16 -> 16, of which waited for: 3 -> 3; matrix products, arithmetic and copies ran while one was open for 6% -> 5% of each run, Pallas kernels for 31% -> 30%
where the time goes in v6:
time: 62.8 us; the launch traced here: 62.5 us
  starting transfers between devices  28.8 us (46%)
  Pallas kernels  24.6 us (39%)
  waiting for transfers between devices  3.15 us (5%)
  local copies, waits for them, and re-layouts  2.56 us (4%)
  other arithmetic  2.56 us (4%)
  between operations  0.81 us (1%)
    ppermute x15, starting transfers between devices, shards(): lax.ppermute(block_out, 'wide', [(p, p ^ r) for p in range(peers)])  22.2 us
    pallas_call x1, Pallas kernels, update(): call(functools.partial(update_kernel, sets), (), [VMEM] * (1 + 2 * sets)...  9.14 us
    pallas_call x4, Pallas kernels, score(): call(functools.partial(score_kernel, blocks, capacity, far_of, known), ()...  8.61 us
    all_to_all x1, starting transfers between devices, shards(): lax.all_to_all(scored[-1][0], 'wide', split_axis=0, concat_axis=0, tiled=...  6.67 us
    pallas_call x1, Pallas kernels, shards(): call(functools.partial(pack_split_kernel, peers, capacity, cells_dev, dis...  3.26 us
    ppermute x15, waiting for transfers between devices, shards(): lax.ppermute(block_out, 'wide', [(p, p ^ r) for p in range(peers)])  3.14 us
    pallas_call x1, Pallas kernels, shards(): call(seed_kernel, (), [VMEM, VMEM], HBM, pltpu.HBM((fine_all, width), BF)...  2.82 us
    reduce_sum x1, other arithmetic, shards(): norm = jnp.sum(fine_wide * fine_wide, axis=-1)  2.56 us
  transfers between devices with their start and end apart: 16, of which 3 were waited for; matrix products, arithmetic and copies ran while one was open for 5% of the time, Pallas kernels for 30%

profile of v6, /device:TPU:0, one launch (start us, length us, event | category | flops | bytes accessed | tf_op | source)
XLA Modules:
  0.0 62.5 jit_solution(15165324676921085046)
XLA Ops:
  0.7 3.3 %shard_map.85 = (bf16[400,128]{1,0:T(8,128)(2,1)}, bf16[400,128]{1,0:T(8,128)(2,1)}, bf16[400,128]{1,0:T(8,128)(2,1)}, bf16[400,128]{1,0:T(8,128)(2,1)}, bf16[40...) custom-call(s32[1,512]{1,0:T(1,128)} %bitcast.10, ...), custom_call_target="tpu_custom_call" | custom-call | flops 805306368 | bytes 3145728 | tf_op jit(solution)/shard_map/pallas_call | solution.py:474
  3.9 6.0 %collective-permute-start = (bf16[400,128]{1,0:T(8,128)(2,1)}, bf16[400,128]{1,0:T(8,128)(2,1)S(1)}, u32[]{:S(2)}, u32[]{:S(2)}) collective-permute-start(bf16[400,128]{1,0:T(8,128)(2,1)} %get-tuple-element.61), channel_id=1, source_target_pairs={{0,14},{1,15},{2,12},{3,13},{4,10},{5,11},{6,8},{7,9},{8,6},{9,7},... | collective-permute-start | bytes 307208 | tf_op jit(solution)/shard_map/ppermute | solution.py:497
  10.0 0.8 %collective-permute-start.5 = (bf16[400,128]{1,0:T(8,128)(2,1)}, bf16[400,128]{1,0:T(8,128)(2,1)}, u32[]{:S(2)}, u32[]{:S(2)}) collective-permute-start(bf16[400,128]{1,0:T(8,128)(2,1)} %get-tuple-element.70), channel_id=1, source_target_pairs={{0,10},{1,11},{2,8},{3,9},{4,14},{5,15},{6,12},{7,13},{8,2},{9,3},... | collective-permute-start | bytes 307208 | tf_op jit(solution)/shard_map/ppermute | solution.py:497
  10.8 1.2 %collective-permute-start.6 = (bf16[400,128]{1,0:T(8,128)(2,1)}, bf16[400,128]{1,0:T(8,128)(2,1)}, u32[]{:S(2)}, u32[]{:S(2)}) collective-permute-start(bf16[400,128]{1,0:T(8,128)(2,1)} %get-tuple-element.73), channel_id=1, source_target_pairs={{0,6},{1,7},{2,4},{3,5},{4,2},{5,3},{6,0},{7,1},{8,14},{9,15},{10,... | collective-permute-start | bytes 307208 | tf_op jit(solution)/shard_map/ppermute | solution.py:497
  12.0 2.9 %collective-permute-start.7 = (bf16[400,128]{1,0:T(8,128)(2,1)}, bf16[400,128]{1,0:T(8,128)(2,1)S(1)}, u32[]{:S(2)}, u32[]{:S(2)}) collective-permute-start(bf16[400,128]{1,0:T(8,128)(2,1)} %get-tuple-element.79), channel_id=1, source_target_pairs={{0,8},{1,9},{2,10},{3,11},{4,12},{5,13},{6,14},{7,15},{8,0},{9,1},... | collective-permute-start | bytes 307208 | tf_op jit(solution)/shard_map/ppermute | solution.py:497
  14.9 2.6 %multiply_reduce_fusion.norm_ref = f32[32,64]{1,0:T(8,128)S(1)} fusion(bf16[32,64,768]{2,1,0:T(8,128)(2,1)} %param.10), kind=kLoop, calls=%fused_computation | loop fusion | flops 4716544 | bytes 3153920 | tf_op jit(solution)/shard_map/reduce_sum | solution.py:458
  17.5 0.8 %reshape.28.reseed_ref = s32[1,2048]{1,0:T(1,128)S(1)} reshape(s32[32,64]{1,0:T(8,128)} %param.11) | data formatting | bytes 16384 | tf_op jit(solution)/shard_map/reshape | solution.py:469
  18.3 0.9 %collective-permute-start.8 = (bf16[400,128]{1,0:T(8,128)(2,1)}, bf16[400,128]{1,0:T(8,128)(2,1)S(1)}, u32[]{:S(2)}, u32[]{:S(2)}) collective-permute-start(bf16[400,128]{1,0:T(8,128)(2,1)} %get-tuple-element.82), channel_id=1, source_target_pairs={{0,4},{1,5},{2,6},{3,7},{4,0},{5,1},{6,2},{7,3},{8,12},{9,13},{10,... | collective-permute-start | bytes 307208 | tf_op jit(solution)/shard_map/ppermute | solution.py:497
  19.6 1.0 %collective-permute-start.4 = (bf16[400,128]{1,0:T(8,128)(2,1)}, bf16[400,128]{1,0:T(8,128)(2,1)S(1)}, u32[]{:S(2)}, u32[]{:S(2)}) collective-permute-start(bf16[400,128]{1,0:T(8,128)(2,1)} %get-tuple-element.67), channel_id=1, source_target_pairs={{0,2},{1,3},{2,0},{3,1},{4,6},{5,7},{6,4},{7,5},{8,10},{9,11},{10,... | collective-permute-start | bytes 307208 | tf_op jit(solution)/shard_map/ppermute | solution.py:497
  20.6 1.8 %collective-permute-done.6.refs_1_ = bf16[400,128]{1,0:T(8,128)(2,1)} collective-permute-done((bf16[400,128]{1,0:T(8,128)(2,1)}, bf16[400,128]{1,0:T(8,128)(2,1)}, u32[]{:S(2)}, u32[]{:S(2)}) %collective-permute-start.6) | collective-permute-done | bytes 102432 | tf_op jit(solution)/shard_map/ppermute | solution.py:497
  22.4 2.1 %collective-permute-start.9 = (bf16[400,128]{1,0:T(8,128)(2,1)}, bf16[400,128]{1,0:T(8,128)(2,1)S(1)}, u32[]{:S(2)}, u32[]{:S(2)}) collective-permute-start(bf16[400,128]{1,0:T(8,128)(2,1)} %get-tuple-element.85), channel_id=1, source_target_pairs={{0,12},{1,13},{2,14},{3,15},{4,8},{5,9},{6,10},{7,11},{8,4},{9,5},... | collective-permute-start | bytes 307208 | tf_op jit(solution)/shard_map/ppermute | solution.py:497
  24.5 1.1 %copy-done.3 = bf16[512,768]{1,0:T(8,128)(2,1)S(1)} copy-done((bf16[512,768]{1,0:T(8,128)(2,1)S(1)}, bf16[512,768]{1,0:T(8,128)(2,1)}, u32[]{:S(2)}) %copy-start.3) | copy-done | bytes 786456
  25.6 2.8 %shard_map.91.refs_12_ = bf16[2048,768]{1,0:T(8,128)(2,1)} custom-call(s32[1,2048]{1,0:T(1,128)S(1)} %reshape.28.reseed_ref, bf16[512,768]{1,0:T(8,128)(2,1)S(1)} %copy-done.3), custom_call_target="tpu_custom_call" | custom-call | flops 1610612736 | bytes 3932160 | tf_op jit(solution)/shard_map/pallas_call | solution.py:460
  28.5 2.2 %collective-permute-start.11 = (bf16[400,128]{1,0:T(8,128)(2,1)}, bf16[400,128]{1,0:T(8,128)(2,1)S(1)}, u32[]{:S(2)}, u32[]{:S(2)}) collective-permute-start(bf16[400,128]{1,0:T(8,128)(2,1)} %get-tuple-element.93), channel_id=1, source_target_pairs={{0,15},{1,14},{2,13},{3,12},{4,11},{5,10},{6,9},{7,8},{8,7},{9,6},... | collective-permute-start | bytes 307208 | tf_op jit(solution)/shard_map/ppermute | solution.py:497
  32.0 1.8 %collective-permute-start.13 = (bf16[400,128]{1,0:T(8,128)(2,1)}, bf16[400,128]{1,0:T(8,128)(2,1)S(1)}, u32[]{:S(2)}, u32[]{:S(2)}) collective-permute-start(bf16[400,128]{1,0:T(8,128)(2,1)} %get-tuple-element.95), channel_id=1, source_target_pairs={{0,9},{1,8},{2,11},{3,10},{4,13},{5,12},{6,15},{7,14},{8,1},{9,0},... | collective-permute-start | bytes 307208 | tf_op jit(solution)/shard_map/ppermute | solution.py:497
  34.0 2.5 %shard_map.86 = (f32[4,1,128]{2,1,0:T(1,128)S(1)}, bf16[64,256]{1,0:T(8,128)(2,1)S(1)}, s32[1,256]{1,0:T(1,128)S(1)}, bf16[256,768]{1,0:T(8,128)(2,1)}) custom-call(bf16[32,768]{1,0:T(8,128)(2,1)S(1)} %copy-done.1, f32[32,64]{1,0:T(8,128)S(1)} %multiply_reduce_fusion.norm_ref, bf16[2048,768]{1,0:T(8,128)(2,1)S(1)} %bitcast.5, ...), custom_call_target="tpu_custom_call" | custom-call | flops 805306368 | bytes 3932160 | tf_op jit(solution)/shard_map/pallas_call | solution.py:398
  37.1 1.8 %collective-permute-start.2 = (bf16[400,128]{1,0:T(8,128)(2,1)S(1)}, bf16[400,128]{1,0:T(8,128)(2,1)S(1)}, u32[]{:S(2)}, u32[]{:S(2)}) collective-permute-start(bf16[400,128]{1,0:T(8,128)(2,1)S(1)} %copy-done.6), channel_id=1, source_target_pairs={{0,13},{1,12},{2,15},{3,14},{4,9},{5,8},{6,11},{7,10},{8,5},{9,4},... | collective-permute-start | bytes 307208 | tf_op jit(solution)/shard_map/ppermute | solution.py:497
  38.9 1.5 %shard_map.87 = (f32[4,1,128]{2,1,0:T(1,128)S(1)}, bf16[64,256]{1,0:T(8,128)(2,1)S(1)}, s32[1,256]{1,0:T(1,128)S(1)}, bf16[256,768]{1,0:T(8,128)(2,1)}) custom-call(bf16[32,768]{1,0:T(8,128)(2,1)S(1)} %copy-done.1, f32[32,64]{1,0:T(8,128)S(1)} %multiply_reduce_fusion.norm_ref, bf16[2048,768]{1,0:T(8,128)(2,1)S(1)} %bitcast.6, ...), custom_call_target="tpu_custom_call" | custom-call | flops 805306368 | bytes 3932160 | tf_op jit(solution)/shard_map/pallas_call | solution.py:398
  40.4 0.8 %collective-permute-done.13.refs_4_ = bf16[400,128]{1,0:T(8,128)(2,1)S(1)} collective-permute-done((bf16[400,128]{1,0:T(8,128)(2,1)}, bf16[400,128]{1,0:T(8,128)(2,1)S(1)}, u32[]{:S(2)}, u32[]{:S(2)}) %collective-permute-start.13) | collective-permute-done | bytes 102432 | tf_op jit(solution)/shard_map/ppermute | solution.py:497
  41.2 2.6 %shard_map.88 = (f32[6,1,128]{2,1,0:T(1,128)S(1)}, bf16[64,384]{1,0:T(8,128)(2,1)S(1)}, s32[1,384]{1,0:T(1,128)S(1)}, bf16[384,768]{1,0:T(8,128)(2,1)}) custom-call(bf16[32,768]{1,0:T(8,128)(2,1)S(1)} %copy-done.1, f32[32,64]{1,0:T(8,128)S(1)} %multiply_reduce_fusion.norm_ref, bf16[2048,768]{1,0:T(8,128)(2,1)S(1)} %bitcast.7, ...), custom_call_target="tpu_custom_call" | custom-call | flops 1207959552 | bytes 4325376 | tf_op jit(solution)/shard_map/pallas_call | solution.py:398
  43.9 2.0 %shard_map.89 = (f32[16,1,128]{2,1,0:T(1,128)}, bf16[64,128]{1,0:T(8,128)(2,1)S(1)}, s32[1,128]{1,0:T(1,128)S(1)}, bf16[128,768]{1,0:T(8,128)(2,1)}) custom-call(bf16[32,768]{1,0:T(8,128)(2,1)S(1)} %copy-done.1, f32[32,64]{1,0:T(8,128)S(1)} %multiply_reduce_fusion.norm_ref, bf16[2048,768]{1,0:T(8,128)(2,1)S(1)} %bitcast.8, ...), custom_call_target="tpu_custom_call" | custom-call | flops 402653184 | bytes 3538944 | tf_op jit(solution)/shard_map/pallas_call | solution.py:398
  45.9 6.7 %all-to-all-start = ((f32[16,1,128]{2,1,0:T(1,128)}), f32[16,1,128]{2,1,0:T(1,128)S(1)}, u32[]{:S(2)}, u32[]{:S(2)}) async-start(f32[16,1,128]{2,1,0:T(1,128)} %get-tuple-element.98), calls=%async_computation | async-start | bytes 16384 | tf_op jit(solution)/shard_map/all_to_all | solution.py:538
  52.6 9.1 %shard_map.92 = (f32[32,768]{1,0:T(8,128)}, f32[2048,768]{1,0:T(8,128)}) custom-call(bf16[32,768]{1,0:T(8,128)(2,1)S(1)} %copy-done.1, s32[1,256]{1,0:T(1,128)S(1)} %get-tuple-element.99.refs_0_, s32[1,256]{1,0:T(1,128)S(1)} %get-tuple-element.100.refs_1_, s32[1,384]{1,0:T(1,128)S(1)} %get-tuple-element.101.refs_2_, ...), custom_call_target="tpu_custom_call" | custom-call | flops 3221225472 | bytes 11010048 | tf_op jit(solution)/shard_map/pallas_call | solution.py:425
  61.7 0.8 %shard_map.90 = f32[1,512]{1,0:T(1,128)} custom-call(s32[8,512]{1,0:T(8,128)S(1)} %get-tuple-element.58.route_ref, f32[16,1,128]{2,1,0:T(1,128)S(1)} %all-to-all-done.error_ref), custom_call_target="tpu_custom_call" | custom-call | bytes 24576 | tf_op jit(solution)/shard_map/pallas_call | solution.py:540
  (32 shorter events, 2.4 us)
Async XLA Ops:
  0.6 33.3 %copy-start = (bf16[32,64,768]{2,1,0:T(8,128)(2,1)S(1)}, bf16[32,64,768]{2,1,0:T(8,128)(2,1)}, u32[]{:S(2)}) copy-start(bf16[32,64,768]{2,1,0:T(8,128)(2,1)} %param.10) | copy-start | bytes 9437188
  0.6 33.3 %copy-start.1 = (bf16[32,768]{1,0:T(8,128)(2,1)S(1)}, bf16[32,768]{1,0:T(8,128)(2,1)}, u32[]{:S(2)}) copy-start(bf16[32,768]{1,0:T(8,128)(2,1)} %coarse_ref.9) | copy-start | bytes 147460
  3.9 14.4 %collective-permute-start = (bf16[400,128]{1,0:T(8,128)(2,1)}, bf16[400,128]{1,0:T(8,128)(2,1)S(1)}, u32[]{:S(2)}, u32[]{:S(2)}) collective-permute-start(bf16[400,128]{1,0:T(8,128)(2,1)} %get-tuple-element.61), channel_id=1, source_target_pairs={{0,14},{1,15},{2,12},{3,13},{4,10},{5,11},{6,8},{7,9},{8,6},{9,7},... | collective-permute-start | bytes 307208 | tf_op jit(solution)/shard_map/ppermute | solution.py:497
  10.0 9.3 %collective-permute-start.3 = (bf16[400,128]{1,0:T(8,128)(2,1)}, bf16[400,128]{1,0:T(8,128)(2,1)S(1)}, u32[]{:S(2)}, u32[]{:S(2)}) collective-permute-start(bf16[400,128]{1,0:T(8,128)(2,1)} %get-tuple-element.66), channel_id=1, source_target_pairs={{0,7},{1,6},{2,5},{3,4},{4,3},{5,2},{6,1},{7,0},{8,15},{9,14},{10,... | collective-permute-start | bytes 307208 | tf_op jit(solution)/shard_map/ppermute | solution.py:497
  10.0 9.6 %collective-permute-start.5 = (bf16[400,128]{1,0:T(8,128)(2,1)}, bf16[400,128]{1,0:T(8,128)(2,1)}, u32[]{:S(2)}, u32[]{:S(2)}) collective-permute-start(bf16[400,128]{1,0:T(8,128)(2,1)} %get-tuple-element.70), channel_id=1, source_target_pairs={{0,10},{1,11},{2,8},{3,9},{4,14},{5,15},{6,12},{7,13},{8,2},{9,3},... | collective-permute-start | bytes 307208 | tf_op jit(solution)/shard_map/ppermute | solution.py:497
  10.8 11.6 %collective-permute-start.6 = (bf16[400,128]{1,0:T(8,128)(2,1)}, bf16[400,128]{1,0:T(8,128)(2,1)}, u32[]{:S(2)}, u32[]{:S(2)}) collective-permute-start(bf16[400,128]{1,0:T(8,128)(2,1)} %get-tuple-element.73), channel_id=1, source_target_pairs={{0,6},{1,7},{2,4},{3,5},{4,2},{5,3},{6,0},{7,1},{8,14},{9,15},{10,... | collective-permute-start | bytes 307208 | tf_op jit(solution)/shard_map/ppermute | solution.py:497
  12.0 12.5 %collective-permute-start.7 = (bf16[400,128]{1,0:T(8,128)(2,1)}, bf16[400,128]{1,0:T(8,128)(2,1)S(1)}, u32[]{:S(2)}, u32[]{:S(2)}) collective-permute-start(bf16[400,128]{1,0:T(8,128)(2,1)} %get-tuple-element.79), channel_id=1, source_target_pairs={{0,8},{1,9},{2,10},{3,11},{4,12},{5,13},{6,14},{7,15},{8,0},{9,1},... | collective-permute-start | bytes 307208 | tf_op jit(solution)/shard_map/ppermute | solution.py:497
  18.3 10.2 %collective-permute-start.8 = (bf16[400,128]{1,0:T(8,128)(2,1)}, bf16[400,128]{1,0:T(8,128)(2,1)S(1)}, u32[]{:S(2)}, u32[]{:S(2)}) collective-permute-start(bf16[400,128]{1,0:T(8,128)(2,1)} %get-tuple-element.82), channel_id=1, source_target_pairs={{0,4},{1,5},{2,6},{3,7},{4,0},{5,1},{6,2},{7,3},{8,12},{9,13},{10,... | collective-permute-start | bytes 307208 | tf_op jit(solution)/shard_map/ppermute | solution.py:497
  19.3 14.6 %collective-permute-start.1 = (bf16[400,128]{1,0:T(8,128)(2,1)}, bf16[400,128]{1,0:T(8,128)(2,1)S(1)}, u32[]{:S(2)}, u32[]{:S(2)}) collective-permute-start(bf16[400,128]{1,0:T(8,128)(2,1)} %get-tuple-element.62), channel_id=1, source_target_pairs={{0,11},{1,10},{2,9},{3,8},{4,15},{5,14},{6,13},{7,12},{8,3},{9,2},... | collective-permute-start | bytes 307208 | tf_op jit(solution)/shard_map/ppermute | solution.py:497
  19.6 17.5 %collective-permute-start.4 = (bf16[400,128]{1,0:T(8,128)(2,1)}, bf16[400,128]{1,0:T(8,128)(2,1)S(1)}, u32[]{:S(2)}, u32[]{:S(2)}) collective-permute-start(bf16[400,128]{1,0:T(8,128)(2,1)} %get-tuple-element.67), channel_id=1, source_target_pairs={{0,2},{1,3},{2,0},{3,1},{4,6},{5,7},{6,4},{7,5},{8,10},{9,11},{10,... | collective-permute-start | bytes 307208 | tf_op jit(solution)/shard_map/ppermute | solution.py:497
  22.4 8.3 %collective-permute-start.9 = (bf16[400,128]{1,0:T(8,128)(2,1)}, bf16[400,128]{1,0:T(8,128)(2,1)S(1)}, u32[]{:S(2)}, u32[]{:S(2)}) collective-permute-start(bf16[400,128]{1,0:T(8,128)(2,1)} %get-tuple-element.85), channel_id=1, source_target_pairs={{0,12},{1,13},{2,14},{3,15},{4,8},{5,9},{6,10},{7,11},{8,4},{9,5},... | collective-permute-start | bytes 307208 | tf_op jit(solution)/shard_map/ppermute | solution.py:497
  24.5 7.5 %collective-permute-start.10 = (bf16[400,128]{1,0:T(8,128)(2,1)}, bf16[400,128]{1,0:T(8,128)(2,1)S(1)}, u32[]{:S(2)}, u32[]{:S(2)}) collective-permute-start(bf16[400,128]{1,0:T(8,128)(2,1)} %get-tuple-element.88), channel_id=1, source_target_pairs={{0,5},{1,4},{2,7},{3,6},{4,1},{5,0},{6,3},{7,2},{8,13},{9,12},{10,... | collective-permute-start | bytes 307208 | tf_op jit(solution)/shard_map/ppermute | solution.py:497
  24.5 1.1 %copy-start.3 = (bf16[512,768]{1,0:T(8,128)(2,1)S(1)}, bf16[512,768]{1,0:T(8,128)(2,1)}, u32[]{:S(2)}) copy-start(bf16[512,768]{1,0:T(8,128)(2,1)} %rows_ref.1) | copy-start | bytes 2359300
  25.6 11.5 %copy-start.6 = (bf16[400,128]{1,0:T(8,128)(2,1)S(1)}, bf16[400,128]{1,0:T(8,128)(2,1)}, u32[]{:S(2)}) copy-start(bf16[400,128]{1,0:T(8,128)(2,1)} %get-tuple-element.63) | copy-start | bytes 307204
  28.5 15.4 %copy-start.2 = (bf16[400,128]{1,0:T(8,128)(2,1)S(1)}, bf16[400,128]{1,0:T(8,128)(2,1)}, u32[]{:S(2)}) copy-start(bf16[400,128]{1,0:T(8,128)(2,1)} %get-tuple-element.68.refs_1_) | copy-start | bytes 307204
  28.5 11.9 %collective-permute-start.11 = (bf16[400,128]{1,0:T(8,128)(2,1)}, bf16[400,128]{1,0:T(8,128)(2,1)S(1)}, u32[]{:S(2)}, u32[]{:S(2)}) collective-permute-start(bf16[400,128]{1,0:T(8,128)(2,1)} %get-tuple-element.93), channel_id=1, source_target_pairs={{0,15},{1,14},{2,13},{3,12},{4,11},{5,10},{6,9},{7,8},{8,7},{9,6},... | collective-permute-start | bytes 307208 | tf_op jit(solution)/shard_map/ppermute | solution.py:497
  30.7 9.7 %collective-permute-start.12 = (bf16[400,128]{1,0:T(8,128)(2,1)}, bf16[400,128]{1,0:T(8,128)(2,1)S(1)}, u32[]{:S(2)}, u32[]{:S(2)}) collective-permute-start(bf16[400,128]{1,0:T(8,128)(2,1)} %get-tuple-element.94), channel_id=1, source_target_pairs={{0,3},{1,2},{2,1},{3,0},{4,7},{5,6},{6,5},{7,4},{8,11},{9,10},{10,... | collective-permute-start | bytes 307208 | tf_op jit(solution)/shard_map/ppermute | solution.py:497
  32.0 9.3 %collective-permute-start.13 = (bf16[400,128]{1,0:T(8,128)(2,1)}, bf16[400,128]{1,0:T(8,128)(2,1)S(1)}, u32[]{:S(2)}, u32[]{:S(2)}) collective-permute-start(bf16[400,128]{1,0:T(8,128)(2,1)} %get-tuple-element.95), channel_id=1, source_target_pairs={{0,9},{1,8},{2,11},{3,10},{4,13},{5,12},{6,15},{7,14},{8,1},{9,0},... | collective-permute-start | bytes 307208 | tf_op jit(solution)/shard_map/ppermute | solution.py:497
  33.8 7.4 %collective-permute-start.14 = (bf16[400,128]{1,0:T(8,128)(2,1)}, bf16[400,128]{1,0:T(8,128)(2,1)S(1)}, u32[]{:S(2)}, u32[]{:S(2)}) collective-permute-start(bf16[400,128]{1,0:T(8,128)(2,1)} %get-tuple-element.96), channel_id=1, source_target_pairs={{0,1},{1,0},{2,3},{3,2},{4,5},{5,4},{6,7},{7,6},{8,9},{9,8},{10,11... | collective-permute-start | bytes 307208 | tf_op jit(solution)/shard_map/ppermute | solution.py:497
  36.5 0.6 copy-start.4
  37.1 15.5 %copy-start.5 = (bf16[64,256]{1,0:T(8,128)(2,1)S(1)}, bf16[64,256]{1,0:T(8,128)(2,1)}, u32[]{:S(2)}) copy-start(bf16[64,256]{1,0:T(8,128)(2,1)} %copy-done.4) | copy-start | bytes 98308
  37.1 6.8 %collective-permute-start.2 = (bf16[400,128]{1,0:T(8,128)(2,1)S(1)}, bf16[400,128]{1,0:T(8,128)(2,1)S(1)}, u32[]{:S(2)}, u32[]{:S(2)}) collective-permute-start(bf16[400,128]{1,0:T(8,128)(2,1)S(1)} %copy-done.6), channel_id=1, source_target_pairs={{0,13},{1,12},{2,15},{3,14},{4,9},{5,8},{6,11},{7,10},{8,5},{9,4},... | collective-permute-start | bytes 307208 | tf_op jit(solution)/shard_map/ppermute | solution.py:497
  45.9 15.8 %all-to-all-start = ((f32[16,1,128]{2,1,0:T(1,128)}), f32[16,1,128]{2,1,0:T(1,128)S(1)}, u32[]{:S(2)}, u32[]{:S(2)}) async-start(f32[16,1,128]{2,1,0:T(1,128)} %get-tuple-element.98), calls=%async_computation | async-start | bytes 16384 | tf_op jit(solution)/shard_map/all_to_all | solution.py:538
